TPU v7x, 256 devices: a whole 4x4x8 slice. The times are simulated.
256 devices in a mesh: dp: 32 (over y, x, z_lo), col: 8 (over z_hi, core).
Axes of the slice: x: 4, y: 4, z: 8 (z_hi: 4, z_lo: 2; z = z_hi * 2 + z_lo), core: 2. Of those that a mesh axis runs over, the one named last changes fastest.
Arguments:
- features: bfloat16 [512, 512, 256], P('dp', 'col'), may hold values from -6 to 6
- cotangent: bfloat16 [512, 512, 256], P('dp'), may hold values from -6 to 6
- lengths: int32 [512], P('dp'), may hold values from 1 to 256, as said below
- route: int32 [512, 2], P('dp'), may hold values from 0 to 31, as said below
- w_in: bfloat16 [4, 512, 512], P(None, None, 'col'), may hold values from -0.25 to 0.25
- w_out: bfloat16 [512, 512], P('col'), may hold values from -0.25 to 0.25
Outputs:
- mixed: bfloat16 [512, 512, 256], P('dp', 'col')
- grad_features: bfloat16 [512, 512, 256], P('dp', 'col')
- grad_in: float32 [4, 512, 512], P(None, None, 'col')
- grad_out: float32 [512, 512], P('col')
Inputs may be any that keep to these rules, and one draw needn't show every extreme that they name: `lengths`: positions at or past a history's length are padding; some history has length 256. route[h, 0] is the data group that receives history h and route[h, 1] its slot there; every group receives exactly 16 histories, one in each slot, and the histories of one group go to 16 different groups.
All inputs are finite; a program needn't handle non-finite values.
Results may differ from a plain program's by a relative error of at most 0.039.
Values may be sent and summed in bfloat16 or wider, within the bound.
No kernel may reach another device: no remote copies, remote signals or barrier semaphores. Data moves between devices by JAX's collectives and lax.ppermute only.
A program may use at most 128 MiB of HBM per device.

v0:
```python
import jax
import jax.numpy as jnp
from jax import lax
from jax.sharding import PartitionSpec as P

D = 512
H = 8
DH = 64
TILE = 128


norm_eps = 1e-05


def silu_slope(values):
    sigma = jax.nn.sigmoid(values)
    return sigma * (1.0 + values * (1.0 - sigma))


def pair_live(rows, length):
    position = jnp.arange(rows, dtype=jnp.int32)
    return (
        (position[None, :] <= position[:, None])
        & (position[:, None] < length)
        & (position[None, :] < length)
    )


def pair_weights(queries, keys, length):
    factor = queries.shape[1] ** (-0.5)
    scores = jnp.einsum("hdi,hdj->hij", queries, keys, preferred_element_type=jnp.float32) * factor
    live = pair_live(queries.shape[2], length)[None]
    weights = jnp.where(live, jax.nn.silu(scores), 0.0).astype(jnp.bfloat16)
    return (scores, live, weights, factor)


def attend_forward(queries, keys, values, length):
    scores, live, weights, factor = pair_weights(queries, keys, length)
    return (jnp.einsum("hij,hdj->hdi", weights, values, preferred_element_type=jnp.float32),)


def attend_backward(queries, keys, values, grad_att, length):
    scores, live, weights, factor = pair_weights(queries, keys, length)
    grad_weights = jnp.einsum("hdi,hdj->hij", grad_att, values, preferred_element_type=jnp.float32)
    grad_values = jnp.einsum("hij,hdi->hdj", weights, grad_att, preferred_element_type=jnp.float32)
    grad_scores = jnp.where(live, grad_weights * silu_slope(scores), 0.0).astype(jnp.bfloat16)
    grad_queries = (
        jnp.einsum("hij,hdj->hdi", grad_scores, keys, preferred_element_type=jnp.float32) * factor
    )
    grad_keys = (
        jnp.einsum("hij,hdi->hdj", grad_scores, queries, preferred_element_type=jnp.float32)
        * factor
    )
    return (grad_queries, grad_keys, grad_values)


def by_tiles(kernel, arrays, length):
    slot_len = arrays[0].shape[-1]
    tile_len = TILE
    tile_count = slot_len // tile_len

    def make_branch(used):
        kept = used * tile_len

        def branch(pieces):

            def one_head(head_pieces):
                outputs = kernel(*[piece[None, :, :kept] for piece in head_pieces], length)
                return tuple((output[0] for output in outputs))

            outputs = lax.map(one_head, tuple(pieces))
            return tuple(
                (jnp.pad(output, ((0, 0), (0, 0), (0, slot_len - kept))) for output in outputs)
            )

        return branch

    branches = [make_branch(used) for used in range(1, tile_count + 1)]
    which = jnp.clip((length + tile_len - 1) // tile_len - 1, 0, tile_count - 1)
    return lax.switch(which, branches, tuple(arrays))


def pick_rows(data, index, live):
    taken = jnp.take(data, index, axis=0)
    live_shape = (live.shape[0],) + (1,) * (data.ndim - 1)
    return jnp.where(live.reshape(live_shape), taken, jnp.zeros_like(taken))


def on_device(features, cotangent, lengths, route, w_in, w_out):
    histories = features.shape[0]
    col_rows = features.shape[1]
    slot_len = features.shape[2]
    local_cols = w_in.shape[2]
    heads_here = local_cols // DH
    all_cols = H * DH
    groups = lax.axis_size("dp")
    col_start = lax.axis_index("col") * col_rows
    dest_group = route[:, 0]
    group_ids = jnp.arange(groups, dtype=jnp.int32)
    local_ids = jnp.arange(histories, dtype=jnp.int32)
    matched = (dest_group[None, :] == group_ids[:, None]).astype(jnp.int32)
    is_sent = jnp.sum(matched, axis=1) > 0
    sent_from = jnp.sum(matched * local_ids[None, :], axis=1)
    sent_slot = jnp.where(is_sent, jnp.sum(matched * route[None, :, 1], axis=1), -1)
    sent_meta = jnp.stack([sent_slot, jnp.sum(matched * lengths[None, :], axis=1)], axis=1)
    full_x = lax.all_gather(features, "col", axis=1, tiled=True)
    full_float = full_x.astype(jnp.float32)
    centred = full_float - jnp.mean(full_float, axis=1, keepdims=True)
    inv_in = lax.rsqrt(jnp.mean(centred * centred, axis=1, keepdims=True) + norm_eps)
    normed_full = centred * inv_in
    xn_full = normed_full.astype(jnp.bfloat16)
    pre_act = jnp.einsum("hds,cdf->chfs", xn_full, w_in, preferred_element_type=jnp.float32)
    proj = jax.nn.silu(pre_act).astype(jnp.bfloat16)
    head_shape = (histories, heads_here, DH, slot_len)
    flat_shape = (histories, local_cols, slot_len)
    up_proj = proj[0]
    values = proj[1].reshape(head_shape)
    queries = proj[2].reshape(head_shape)
    keys = proj[3].reshape(head_shape)

    def forward_one(entries):
        return by_tiles(attend_forward, entries[:3], entries[3])

    attended = lax.map(forward_one, (queries, keys, values, lengths))[0].reshape(flat_shape)
    totals, squares = (
        lax.psum(jnp.sum(attended, axis=1).astype(jnp.bfloat16), "col").astype(jnp.float32),
        lax.psum(jnp.sum(attended * attended, axis=1).astype(jnp.bfloat16), "col").astype(
            jnp.float32
        ),
    )
    row_mean = (totals / all_cols)[:, None, :]
    inv_out = lax.rsqrt(squares[:, None, :] / all_cols - row_mean * row_mean + norm_eps)
    out_norm = (attended - row_mean) * inv_out
    up_float = up_proj.astype(jnp.float32)
    gated = (out_norm * up_float).astype(jnp.bfloat16)
    partial_term = jnp.einsum("hfs,fd->hds", gated, w_out, preferred_element_type=jnp.float32)
    summed = lax.psum_scatter(
        partial_term.astype(jnp.bfloat16), "col", scatter_dimension=1, tiled=True
    ).astype(jnp.float32)
    mixed_here = (features.astype(jnp.float32) + summed).astype(jnp.bfloat16)
    moved_out = (
        lax.all_to_all(
            pick_rows(mixed_here, sent_from, is_sent), "dp", split_axis=0, concat_axis=0, tiled=True
        ),
        lax.all_to_all(sent_meta, "dp", split_axis=0, concat_axis=0, tiled=True),
    )
    arrived_meta = moved_out[1]
    hit_mask = (arrived_meta[None, :, 0] == local_ids[:, None]).astype(jnp.int32)
    source = jnp.sum(hit_mask * group_ids[None, :], axis=1)
    mixed = jnp.take(moved_out[0], source, axis=0)
    returned = lax.all_to_all(
        pick_rows(cotangent, jnp.maximum(arrived_meta[:, 0], 0), arrived_meta[:, 0] >= 0),
        "dp",
        split_axis=0,
        concat_axis=0,
        tiled=True,
    )
    grad_y = jnp.take(returned, dest_group, axis=0)
    grad_gated = jnp.einsum("hds,fd->hfs", grad_y, w_out, preferred_element_type=jnp.float32)
    grad_wout = jnp.einsum("hfs,hds->fd", gated, grad_y, preferred_element_type=jnp.float32)
    grad_normo = grad_gated * up_float
    grad_up = grad_gated * out_norm
    first_sum, second_sum = (
        lax.psum(jnp.sum(grad_normo, axis=1).astype(jnp.bfloat16), "col").astype(jnp.float32),
        lax.psum(jnp.sum(grad_normo * out_norm, axis=1).astype(jnp.bfloat16), "col").astype(
            jnp.float32
        ),
    )
    grad_att = (
        inv_out
        * (
            grad_normo
            - (first_sum / all_cols)[:, None, :]
            - out_norm * (second_sum / all_cols)[:, None, :]
        )
    ).astype(jnp.bfloat16)

    def backward_one(entries):
        return by_tiles(attend_backward, entries[:4], entries[4])

    grad_q, grad_k, grad_v = lax.map(
        backward_one, (queries, keys, values, grad_att.reshape(head_shape), lengths)
    )
    grad_proj = jnp.stack(
        [
            grad_up,
            grad_v.reshape(flat_shape),
            grad_q.reshape(flat_shape),
            grad_k.reshape(flat_shape),
        ]
    )
    grad_pre = (grad_proj * silu_slope(pre_act)).astype(jnp.bfloat16)
    grad_win = jnp.einsum("hds,chfs->cdf", xn_full, grad_pre, preferred_element_type=jnp.float32)
    input_term = jnp.einsum("chfs,cdf->hds", grad_pre, w_in, preferred_element_type=jnp.float32)
    grad_xn = lax.psum_scatter(
        input_term.astype(jnp.bfloat16), "col", scatter_dimension=1, tiled=True
    ).astype(jnp.float32)
    normed_here = lax.dynamic_slice_in_dim(normed_full, col_start, col_rows, 1)
    lead_sum, cross_sum = (
        lax.psum(jnp.sum(grad_xn, axis=1).astype(jnp.bfloat16), "col").astype(jnp.float32),
        lax.psum(jnp.sum(grad_xn * normed_here, axis=1).astype(jnp.bfloat16), "col").astype(
            jnp.float32
        ),
    )
    correction = inv_in * (
        grad_xn - lead_sum[:, None, :] / D - normed_here * cross_sum[:, None, :] / D
    )
    own_grad = lax.dynamic_slice_in_dim(grad_y, col_start, col_rows, 1).astype(jnp.float32)
    grad_here = (own_grad + correction).astype(jnp.bfloat16)
    win_sum, wout_sum = (
        lax.psum(grad_win.astype(jnp.bfloat16), "dp").astype(jnp.float32),
        lax.psum(grad_wout.astype(jnp.bfloat16), "dp").astype(jnp.float32),
    )
    factor = float(histories * groups * slot_len) ** (-0.5)
    return (mixed, grad_here, win_sum * factor, wout_sum * factor)


def solution(mesh):
    in_specs = (
        P("dp", "col", None),
        P("dp", None, None),
        P("dp"),
        P("dp", None),
        P(None, None, "col"),
        P("col", None),
    )
    out_specs = (P("dp", "col", None), P("dp", "col", None), P(None, None, "col"), P("col", None))
    return jax.shard_map(
        on_device, mesh=mesh, in_specs=in_specs, out_specs=out_specs, check_vma=False
    )
```

profile of v0, /device:TPU:34, one launch (start us, length us, event | category | flops | bytes accessed | tf_op | source)
XLA Modules:
  0.0 810.8 jit_solution(7050485232227841854)
XLA Ops:
  9.8 14.5 %all_to_all.22 = s32[32,1,2]{2,1,0:T(1,128)S(1)} all-to-all(s32[32,1,2]{2,1,0:T(1,128)S(1)} %copy.94), channel_id=1, replica_groups=mesh['dp'=32,'col'=8] {'dp'}, dimensions={0} | all-to-all | bytes 512 | tf_op jit(solution)/shard_map/all_to_all | solution.py:145
  24.9 7.1 gather_fusion.2
  32.1 7.6 select_select_fusion
  39.6 7.0 all-to-all-start.2
  48.9 71.6 %all-gather.2.cloned.1.call-done = bf16[16,512,256]{2,0,1:T(8,128)(2,1)} async-done(((bf16[16,64,256]{2,0,1:T(8,128)(2,1)}), bf16[16,512,256]{2,0,1:T(8,128)(2,1)}) %all-gather.2.cloned.1.call-update) | async-done | bytes 4194320 | tf_op jit(solution)/shard_map/all_gather | solution.py:106
  127.5 4.9 broadcast_subtract_fusion
  133.7 87.9 %while.44 = (s32[]{:T(128)}, f32[16,1,64,256]{3,2,1,0:T(8,128)S(1)}, s32[16]{0:T(128)}, bf16[16,1,64,256]{3,2,1,0:T(8,128)(2,1)}, bf16[16,1,64,256]{3,2,1,0:T(8,...) while((s32[]{:T(128)}, ...), condition=%wide.region_10.11_spmd, body=%wide.region_7.10_spmd.sunk | while | flops 17432852 | bytes 509455 | solution.py:124
  135.5 3.7 conditional.4
  141.0 3.7 conditional.4
  146.5 3.7 conditional.4
  152.0 3.7 conditional.4
  157.5 3.7 conditional.4
  163.0 3.7 conditional.4
  168.5 3.7 conditional.4
  174.0 3.7 conditional.4
  185.0 3.7 conditional.4
  201.5 3.7 conditional.4
  212.4 3.7 conditional.4
  221.8 28.4 %all-reduce.7 = (bf16[16,256]{1,0:T(8,128)(2,1)S(1)}, bf16[16,256]{1,0:T(8,128)(2,1)S(1)}) all-reduce(bf16[16,256]{1,0:T(8,128)(2,1)S(1)} %fusion.118, bf16[16,256]{1,0:T(8,128)(2,1)S(1)} %reduce_sum.131), channel_id=1, replica_groups=mesh['dp'=32,'col'=8] {'col'}, use_global_device_ids=true, to_apply=%region_14.15 | all-reduce | flops 8192 | bytes 32768 | tf_op jit(solution)/shard_map/psum | solution.py:127
  250.3 6.3 gather_fusion.3
  263.1 27.8 %all-reduce.6 = (bf16[16,256]{1,0:T(8,128)(2,1)}, bf16[16,256]{1,0:T(8,128)(2,1)}) all-reduce(bf16[16,256]{1,0:T(8,128)(2,1)S(1)} %get-tuple-element.804, bf16[16,256]{1,0:T(8,128)(2,1)S(1)} %get-tuple-element.803), channel_id=1, replica_groups=mesh['dp'=32,'col'=8] {'col'}, use_global_device_ids=true, to_apply=%region_19.20 | all-reduce | flops 8192 | bytes 32768 | tf_op jit(solution)/shard_map/psum | solution.py:165
  298.5 7.9 copy.103
  307.4 4.2 fusion.110
  312.9 92.3 %while.45 = (s32[]{:T(128)}, f32[16,1,64,256]{3,2,1,0:T(8,128)S(1)}, f32[16,1,64,256]{3,2,1,0:T(8,128)S(1)}, f32[16,1,64,256]{3,2,1,0:T(8,128)}, s32[16]{0:T(128...) while((s32[]{:T(128)}, ...), condition=%wide.region_23.24_spmd, body=%wide.region_20.23_spmd.sunk | while | flops 43483412 | bytes 2005687 | solution.py:181
  405.3 6.4 fusion.88
  416.4 4.8 fusion.87
  421.2 7.9 copy.112
  433.3 14.9 %all-to-all-start.1 = ((bf16[32,64,256]{2,1,0:T(8,128)(2,1)}), bf16[32,64,256]{2,1,0:T(8,128)(2,1)S(1)}, u32[]{:S(2)}, u32[]{:S(2)}) async-start(bf16[32,64,256]{2,1,0:T(8,128)(2,1)} %select_select_fusion.1), calls=%async_computation.2 | async-start | bytes 2097152 | tf_op jit(solution)/shard_map/all_to_all | solution.py:142
  448.2 7.0 fusion.84
  455.1 256.7 %all-reduce.10.cloned.1.call-done = (bf16[4,512,64]{1,2,0:T(8,128)(2,1)}, bf16[64,512]{1,0:T(8,128)(2,1)}) async-done(((bf16[4,512,64]{1,2,0:T(8,128)(2,1)}, bf16[64,512]{1,0:T(8,128)(2,1)}), (bf16[4,512,64]{1,2,0:T(8,128)(2,1)}, bf16[64,512]{1,0:T(8,128)(2,1)})) %all-reduce.10.cloned.1.call-update) | async-done | bytes 327696 | tf_op jit(solution)/shard_map/psum | solution.py:211
  715.2 54.9 %reduce-scatter.5.cloned.1.call-done = bf16[16,64,256]{2,0,1:T(8,128)(2,1)} async-done(((bf16[16,512,256]{2,0,1:T(8,128)(2,1)}), bf16[16,64,256]{2,0,1:T(8,128)(2,1)}) %reduce-scatter.5.cloned.1.call-update) | async-done | bytes 524304 | tf_op jit(solution)/shard_map/reduce_scatter | solution.py:195
  772.8 27.2 %all-reduce.5 = (bf16[16,256]{1,0:T(8,128)(2,1)S(1)}, bf16[16,256]{1,0:T(8,128)(2,1)S(1)}) all-reduce(bf16[16,256]{1,0:T(8,128)(2,1)S(1)} %fusion.115, bf16[16,256]{1,0:T(8,128)(2,1)S(1)} %reduce_sum.137), channel_id=1, replica_groups=mesh['dp'=32,'col'=8] {'col'}, use_global_device_ids=true, to_apply=%region_28.29 | all-reduce | flops 8192 | bytes 32768 | tf_op jit(solution)/shard_map/psum | solution.py:201
  (457 shorter events, 276.3 us)
Async XLA Ops:
  7.2 118.4 %copy-start = (bf16[4,512,64]{1,2,0:T(8,128)(2,1)S(1)}, bf16[4,512,64]{1,2,0:T(8,128)(2,1)}, u32[]{:S(2)}) copy-start(bf16[4,512,64]{1,2,0:T(8,128)(2,1)} %param.18) | copy-start | bytes 786436
  9.2 0.5 copy-start.14
  39.6 7.0 copy-start.8
  39.6 8.8 %copy-start.16 = (s32[16,2]{0,1:T(2,128)S(1)}, s32[16,2]{0,1:T(2,128)}, u32[]{:S(2)}) copy-start(s32[16,2]{0,1:T(2,128)} %param.17) | copy-start | bytes 388
  39.6 210.6 %all-to-all-start.2 = ((bf16[32,512,256]{2,1,0:T(8,128)(2,1)}), bf16[32,512,256]{2,1,0:T(8,128)(2,1)}, u32[]{:S(2)}, u32[]{:S(2)}) async-start(bf16[32,512,256]{2,1,0:T(8,128)(2,1)} %select_select_fusion), calls=%async_computation.3 | async-start | bytes 16777216 | tf_op jit(solution)/shard_map/all_to_all | solution.py:151
  46.6 73.9 %all-gather.2.cloned.1.call-start = ((), (), s32[]{:S(2)}) async-start(), calls=%async_computation.5 | async-start | bytes 4718592 | tf_op jit(solution)/shard_map/all_gather | solution.py:106
  47.8 382.1 %reduce-scatter.3.cloned.1.call-start = ((), (), s32[]{:S(2)}) async-start(), calls=%async_computation.6 | async-start | bytes 4718592 | tf_op jit(solution)/shard_map/reduce_scatter | solution.py:137
  120.5 3.5 copy-start.2
  124.0 1.6 copy-start.11
  127.5 4.9 copy-start.4
  250.3 6.3 copy-start.17
  256.6 4.6 copy-start.10
  259.3 1.9 copy-start.1
  294.5 0.8 copy-start.5
  306.4 1.0 copy-start.6
  306.4 405.5 %all-reduce.10.cloned.1.call-start = ((), (), s32[]{:S(2)}) async-start(), calls=%async_computation.8 | async-start | bytes 655360 | tf_op jit(solution)/shard_map/psum | solution.py:211
  405.3 7.7 copy-start.3
  405.3 7.7 copy-start.12
  411.6 1.3 copy-start.7
  416.3 353.8 %reduce-scatter.5.cloned.1.call-start = ((), (), s32[]{:S(2)}) async-start(), calls=%async_computation.7 | async-start | bytes 4718592 | tf_op jit(solution)/shard_map/reduce_scatter | solution.py:195
  429.1 0.6 copy-start.13
  429.1 0.6 copy-start.15
  429.1 0.7 copy-start.18
  429.1 1.0 copy-start.9
  433.3 369.5 %all-to-all-start.1 = ((bf16[32,64,256]{2,1,0:T(8,128)(2,1)}), bf16[32,64,256]{2,1,0:T(8,128)(2,1)S(1)}, u32[]{:S(2)}, u32[]{:S(2)}) async-start(bf16[32,64,256]{2,1,0:T(8,128)(2,1)} %select_select_fusion.1), calls=%async_computation.2 | async-start | bytes 2097152 | tf_op jit(solution)/shard_map/all_to_all | solution.py:142
Sparse Core Ops, SparseCore 0:
  49.9 70.5 all-gather.1
  306.5 62.3 reduce-scatter.2
  416.4 295.3 all-reduce.9
  714.4 55.6 reduce-scatter.4
where the time goes:
time: 823 us; the launch traced here: 811 us
  waiting for transfers between devices  383 us (47%)
  local copies, waits for them, and re-layouts  142 us (17%)
  blocking collectives  97.9 us (12%)
  other arithmetic  80.6 us (10%)
  matrix products  48.8 us (6%)
  starting transfers between devices  22 us (3%)
  loops' own time  21.8 us (3%)
  between operations  14.1 us (2%)
    psum x1, waiting for transfers between devices, on_device(): lax.psum(grad_win.astype(jnp.bfloat16), 'dp').astype(jnp.float32)  257 us
    all_gather x1, waiting for transfers between devices, on_device(): full_x = lax.all_gather(features, 'col', axis=1, tiled=True)  71.6 us
    reduce_scatter x1, waiting for transfers between devices, on_device(): lax.psum_scatter(input_term.astype(jnp.bfloat16), 'col', scatter_dimensio...  54.9 us
    squeeze x64, local copies, waits for them, and re-layouts, branch(): outputs = lax.map(one_head, tuple(pieces))  49.8 us
    dynamic_slice x32, local copies, waits for them, and re-layouts, on_device(): lax.map(forward_one, (queries, keys, values, lengths))[0]  40.4 us
    psum x1, blocking collectives, on_device(): lax.psum(jnp.sum(attended * attended, axis=1).astype(jnp.bfloat16), 'col')  28.4 us
    psum x1, blocking collectives, on_device(): lax.psum(jnp.sum(grad_normo * out_norm, axis=1).astype(jnp.bfloat16), 'col')  27.8 us
    lt x32, other arithmetic, pair_live(): position[:, None] < length  27.3 us
  transfers between devices with their start and end apart: 6, of which 3 were waited for; matrix products, arithmetic and copies ran while one was open for 27% of the time, Pallas kernels for 0%

commit v1 on v0

v1 whole, which is shorter than its diff:
```python
import jax
import jax.numpy as jnp
from jax import lax
from jax.experimental import pallas as pl
from jax.experimental.pallas import tpu as pltpu
from jax.sharding import Mesh
from jax.sharding import PartitionSpec as P

D = 512
H = 8
DH = 64
SLOT = 256
HIST = 16
EPS = 1e-05
META = 16
ROWS = 5 * DH
PIECE = ROWS // 4
F32 = jnp.float32
BF16 = jnp.bfloat16
DP = ("y", "x", "zlo")
COL = ("zhi", "core")
VMEM = pl.BlockSpec(memory_space=pltpu.VMEM)
SMEM = pl.BlockSpec(memory_space=pltpu.SMEM)


def params(mib):
    return pltpu.CompilerParams(vmem_limit_bytes=mib * 1024 * 1024)


def spread_kernel(route, lengths, rows, sent):
    sent[...] = jnp.zeros_like(sent)
    for h in range(HIST):
        group = route[h, 0]
        sent[group, :DH, :] = rows[h]
        slot = (route[h, 1] + 1).astype(F32)
        count = lengths[h].astype(F32)
        sent[group, DH:, : SLOT // 2] = jnp.full((META, SLOT // 2), slot, F32).astype(BF16)
        sent[group, DH:, SLOT // 2 :] = jnp.full((META, SLOT // 2), count, F32).astype(BF16)


def settle_kernel(arrived, rows, meta):
    groups = arrived.shape[0]
    for group in range(groups):
        note = arrived[group, DH:, :].astype(F32)
        slot = jnp.max(note[:, : SLOT // 2]).astype(jnp.int32)
        count = jnp.max(note[:, SLOT // 2 :]).astype(jnp.int32)

        @pl.when(slot > 0)
        def _():
            rows[slot - 1] = arrived[group, :DH, :]
            meta[0, slot - 1] = group
            meta[1, slot - 1] = count


def return_kernel(meta, rows, sent):
    sent[...] = jnp.zeros_like(sent)
    for k in range(HIST):
        sent[meta[0, k]] = rows[k]


def collect_kernel(route, arrived, rows):
    for h in range(HIST):
        rows[h] = arrived[route[h, 0]]


def tn(a, b):
    return lax.dot_general(a, b, (((0,), (0,)), ((), ())), preferred_element_type=F32)


def nt(a, b):
    return lax.dot_general(a, b, (((1,), (1,)), ((), ())), preferred_element_type=F32)


def nn(a, b):
    return lax.dot_general(a, b, (((1,), (0,)), ((), ())), preferred_element_type=F32)


def silu_parts(z):
    sigma = 0.5 * jnp.tanh(0.5 * z) + 0.5
    silu = z * sigma
    return silu, sigma + silu * (1.0 - sigma)


def layer_kernel(
    place,
    meta,
    xa,
    gy_ref,
    wg,
    mixed,
    gfeat,
    mine,
    other,
    x_s,
    norm_s,
    xn_s,
    slope_s,
    proj_s,
    att_s,
    w_s,
    sl_s,
    gated_s,
    gy_s,
    gatt_s,
    gpre_s,
    sum_s,
    wo_s,
    gwo_s,
):
    tokens = 2 * SLOT
    col = place[0]
    core = place[1]
    factor = BF16(DH**-0.5)
    for i in range(2):
        lanes = slice(i * SLOT, (i + 1) * SLOT)
        x_s[:, lanes] = xa[:, i].reshape(D, SLOT).astype(F32)
        gy_s[:, lanes] = gy_ref[i]
    wo_s[...] = wg[:, 4 * DH :, :].reshape(D, D)

    inv_in = []
    for i in range(tokens // 128):
        lanes = slice(i * 128, (i + 1) * 128)
        x = x_s[:, lanes]
        centred = x - jnp.mean(x, axis=0, keepdims=True)
        inv = lax.rsqrt(jnp.mean(centred * centred, axis=0, keepdims=True) + EPS)
        normed = centred * inv
        inv_in.append(inv)
        norm_s[:, lanes] = normed
        xn_s[:, lanes] = normed.astype(BF16)

    key_at = lax.broadcasted_iota(jnp.int32, (SLOT, SLOT), 0)
    query_at = lax.broadcasted_iota(jnp.int32, (SLOT, SLOT), 1)

    def forward_head(h, sums):
        silu, slope = silu_parts(nn(wg[h, : 4 * DH, :], xn_s[...]))
        slope_s[h] = slope
        proj_s[h] = silu.astype(BF16)
        parts = []
        for i in range(2):
            lanes = slice(i * SLOT, (i + 1) * SLOT)
            value = proj_s[h, DH : 2 * DH, lanes]
            query = proj_s[h, 2 * DH : 3 * DH, lanes]
            key = proj_s[h, 3 * DH :, lanes] * factor
            live = (key_at <= query_at) & (query_at < meta[1, 2 * col + i])
            silu_w, slope_w = silu_parts(tn(key, query))
            weights = jnp.where(live, silu_w, 0.0).astype(BF16)
            w_s[h, i] = weights
            sl_s[h, i] = jnp.where(live, slope_w, 0.0).astype(BF16)
            parts.append(nn(value, weights))
        att = jnp.concatenate(parts, axis=1)
        att_s[pl.ds(h * DH, DH), :] = att
        return (
            sums[0] + jnp.sum(att, axis=0, keepdims=True),
            sums[1] + jnp.sum(att * att, axis=0, keepdims=True),
        )

    zero = jnp.zeros((1, tokens), F32)
    totals, squares = lax.fori_loop(0, H, forward_head, (zero, zero))
    mean = totals / D
    inv_out = lax.rsqrt(squares / D - mean * mean + EPS)

    def gate_head(h, carry):
        rows = pl.ds(h * DH, DH)
        normed = (att_s[rows, :] - mean) * inv_out
        att_s[rows, :] = normed
        gated_s[rows, :] = (normed * proj_s[h, :DH, :].astype(F32)).astype(BF16)
        return carry

    lax.fori_loop(0, H, gate_head, 0)
    out = (x_s[...] + tn(wo_s[...], gated_s[...])).astype(BF16)
    for i in range(2):
        mixed[:, i] = out[:, i * SLOT : (i + 1) * SLOT].reshape(H, DH, SLOT)

    x_s[...] = nn(wo_s[...], gy_s[...])
    gwo_s[...] = nt(gated_s[...], gy_s[...]).astype(BF16)

    def sum_head(h, sums):
        rows = pl.ds(h * DH, DH)
        grad = x_s[rows, :] * proj_s[h, :DH, :].astype(F32)
        return (
            sums[0] + jnp.sum(grad, axis=0, keepdims=True),
            sums[1] + jnp.sum(grad * att_s[rows, :], axis=0, keepdims=True),
        )

    first, second = lax.fori_loop(0, H, sum_head, (zero, zero))
    first = first / D
    second = second / D

    def store_grad(ref, at, grad_win, grad_wout):
        last = 4 * DH - 3 * PIECE
        for part in range(4):
            lanes = slice(part * 128, (part + 1) * 128)
            for cut in range(3):
                ref[4 * part + cut, at] = grad_win[cut * PIECE : (cut + 1) * PIECE, lanes]
            ref[4 * part + 3, at, :last, :] = grad_win[3 * PIECE :, lanes]
            ref[4 * part + 3, at, last:, :] = grad_wout[:, lanes]

    sum_s[...] = jnp.zeros_like(sum_s)

    def backward_head(h, carry):
        rows = pl.ds(h * DH, DH)
        grad_gated = x_s[rows, :]
        normed = att_s[rows, :]
        grad_normo = grad_gated * proj_s[h, :DH, :].astype(F32)
        gatt_s[...] = (inv_out * (grad_normo - first - normed * second)).astype(BF16)
        gpre_s[:DH, :] = (grad_gated * normed * slope_s[h, :DH, :]).astype(BF16)
        for i in range(2):
            lanes = slice(i * SLOT, (i + 1) * SLOT)
            value = proj_s[h, DH : 2 * DH, lanes]
            query = proj_s[h, 2 * DH : 3 * DH, lanes] * factor
            key = proj_s[h, 3 * DH :, lanes] * factor
            grad = gatt_s[:, lanes]
            grad_scores = (tn(value, grad) * sl_s[h, i].astype(F32)).astype(BF16)
            grad_value = nt(grad, w_s[h, i])
            grad_query = nn(key, grad_scores)
            grad_key = nt(query, grad_scores)
            for c, part in ((1, grad_value), (2, grad_query), (3, grad_key)):
                at = slice(c * DH, (c + 1) * DH)
                gpre_s[at, lanes] = (part * slope_s[h, at, lanes]).astype(BF16)
        grad_win = nt(gpre_s[...], xn_s[...]).astype(BF16)
        grad_wout = gwo_s[rows, :]

        @pl.when(h % 2 == core)
        def _():
            store_grad(mine, h // 2, grad_win, grad_wout)

        @pl.when(h % 2 != core)
        def _():
            store_grad(other, h // 2, grad_win, grad_wout)

        sum_s[...] += tn(wg[h, : 4 * DH, :], gpre_s[...])
        return carry

    lax.fori_loop(0, H, backward_head, 0)
    for i in range(tokens // 128):
        lanes = slice(i * 128, (i + 1) * 128)
        grad = sum_s[:, lanes]
        normed = norm_s[:, lanes]
        lead = jnp.mean(grad, axis=0, keepdims=True)
        cross = jnp.mean(grad * normed, axis=0, keepdims=True)
        total = gy_s[:, lanes].astype(F32) + inv_in[i] * (grad - lead - normed * cross)
        here = slice(i % 2 * 128, (i % 2 + 1) * 128)
        gfeat[:, i // 2, :, here] = total.astype(BF16).reshape(H, DH, 128)


def run_layer(place, meta, xa, grad_y, wg):
    tokens = 2 * SLOT
    piece = jax.ShapeDtypeStruct((16, 4, PIECE, 128), BF16)
    block = jax.ShapeDtypeStruct((H, 2, DH, SLOT), BF16)
    return pl.pallas_call(
        layer_kernel,
        out_shape=(block, block, piece, piece),
        in_specs=[SMEM, SMEM, VMEM, VMEM, VMEM],
        out_specs=(VMEM, VMEM, VMEM, VMEM),
        scratch_shapes=[
            pltpu.VMEM((D, tokens), F32),
            pltpu.VMEM((D, tokens), F32),
            pltpu.VMEM((D, tokens), BF16),
            pltpu.VMEM((H, 4 * DH, tokens), F32),
            pltpu.VMEM((H, 4 * DH, tokens), BF16),
            pltpu.VMEM((D, tokens), F32),
            pltpu.VMEM((H, 2, SLOT, SLOT), BF16),
            pltpu.VMEM((H, 2, SLOT, SLOT), BF16),
            pltpu.VMEM((D, tokens), BF16),
            pltpu.VMEM((D, tokens), BF16),
            pltpu.VMEM((DH, tokens), BF16),
            pltpu.VMEM((4 * DH, tokens), BF16),
            pltpu.VMEM((D, tokens), F32),
            pltpu.VMEM((D, D), BF16),
            pltpu.VMEM((D, D), BF16),
        ],
        compiler_params=params(48),
    )(place, meta, xa, grad_y, wg)


def swap(x, axes):
    return lax.all_to_all(x, axes, split_axis=0, concat_axis=0, tiled=True)


def on_device(features, cotangent, lengths, route, w_in, w_out):
    groups = lax.axis_size(DP)
    col = lax.axis_index(COL)
    place = jnp.stack([col, lax.axis_index("core")]).astype(jnp.int32)

    packed = jnp.concatenate([w_in.transpose(0, 2, 1).reshape(4 * DH, D), w_out], axis=0)
    wg = lax.all_gather(packed, COL)
    sent = pl.pallas_call(
        spread_kernel,
        out_shape=jax.ShapeDtypeStruct((groups, DH + META, SLOT), BF16),
        in_specs=[SMEM, SMEM, VMEM],
        out_specs=VMEM,
        compiler_params=params(16),
    )(route, lengths, features)
    rows, meta = pl.pallas_call(
        settle_kernel,
        out_shape=(
            jax.ShapeDtypeStruct((HIST, DH, SLOT), BF16),
            jax.ShapeDtypeStruct((2, HIST), jnp.int32),
        ),
        in_specs=[VMEM],
        out_specs=(VMEM, SMEM),
        compiler_params=params(16),
    )(swap(sent, DP))
    xa = swap(rows, COL).reshape(H, 2, DH, SLOT)
    grad_y = lax.dynamic_slice_in_dim(cotangent, 2 * col, 2, 0)
    mixed, gfeat, mine, other = run_layer(place, meta, xa, grad_y, wg)

    came = lax.ppermute(other, "core", [(0, 1), (1, 0)])
    half = (mine.astype(F32) + came.astype(F32)).astype(BF16)
    part = jnp.sum(swap(half, ("y", "x")).reshape(16, 4, PIECE, 128).astype(F32), axis=0)
    part = part.astype(BF16).reshape(8, PIECE // 2, 128)
    part = jnp.sum(swap(part, ("zhi", "zlo")).astype(F32), axis=0).astype(BF16)
    whole = swap(jnp.broadcast_to(part[None], (groups, PIECE // 2, 128)), DP)
    whole = whole.reshape(4, 4, 2, PIECE // 2, 128).transpose(1, 2, 3, 0, 4).reshape(ROWS, D)
    whole = whole.astype(F32) * (float(HIST * groups * SLOT) ** -0.5)
    grad_in = whole[: 4 * DH].reshape(4, DH, D).transpose(0, 2, 1)
    grad_out = whole[4 * DH :]

    home = swap(gfeat.reshape(HIST, DH, SLOT), COL)
    back = pl.pallas_call(
        return_kernel,
        out_shape=jax.ShapeDtypeStruct((groups, DH, SLOT), BF16),
        in_specs=[SMEM, VMEM],
        out_specs=VMEM,
        compiler_params=params(16),
    )(meta, home)
    grad_features = pl.pallas_call(
        collect_kernel,
        out_shape=jax.ShapeDtypeStruct((HIST, DH, SLOT), BF16),
        in_specs=[SMEM, VMEM],
        out_specs=VMEM,
        compiler_params=params(16),
    )(route, swap(back, DP))
    return (swap(mixed.reshape(HIST, DH, SLOT), COL), grad_features, grad_in, grad_out)


def solution(mesh):
    split = Mesh(mesh.devices.reshape(4, 4, 2, 4, 2), ("y", "x", "zlo", "zhi", "core"))
    in_specs = (P(DP, COL, None), P(DP, None, None), P(DP), P(DP, None), P(None, None, COL), P(COL, None))
    out_specs = (P(DP, COL, None), P(DP, COL, None), P(None, None, COL), P(COL, None))
    return jax.shard_map(
        on_device, mesh=split, in_specs=in_specs, out_specs=out_specs, check_vma=False
    )
```

time: 823 us -> 233 us (0.28); the launches traced: 811 us -> 231 us
  waiting for transfers between devices: 383 us -> 73.7 us
  local copies, waits for them, and re-layouts: 142 us -> 6.01 us
  other arithmetic: 80.6 us -> 4.43 us
  matrix products: 48.8 us -> 0 us
  blocking collectives: 97.9 us -> 65.9 us
  Pallas kernels: 0 us -> 31.3 us
  loops' own time: 21.8 us -> 0 us
  starting transfers between devices: 22 us -> 35.1 us
    psum x1 -> x0, waiting for transfers between devices: 257 us -> none  [on_device(): lax.psum(grad_win.astype(jnp.bfloat16), 'dp').astype(jnp.float32)]
    psum x3 -> x0, blocking collectives: 83.4 us -> none  [the longest x1 28.4 us: on_device(): lax.psum(jnp.sum(attended * attended, axis=1).astype(jnp.bfloat16), 'col')]
    all_to_all x2 -> x6, waiting for transfers between devices: 0.01 us -> 73.7 us  [swap(): return lax.all_to_all(x, axes, split_axis=0, concat_axis=0, tiled=True)]
    all_gather x1, waiting for transfers between devices: 71.6 us -> 0.01 us  [on_device(): wg = lax.all_gather(packed, COL)]
    reduce_scatter x2 -> x0, waiting for transfers between devices: 54.9 us -> none  [the longest x1 54.9 us: on_device(): lax.psum_scatter(input_term.astype(jnp.bfloat16), 'col', scatter_dimensio...]
    all_to_all x1 -> x2, blocking collectives: 14.5 us -> 65.9 us  [swap(): return lax.all_to_all(x, axes, split_axis=0, concat_axis=0, tiled=True)]
    squeeze x64 -> x0, local copies, waits for them, and re-layouts: 49.8 us -> none  [branch(): outputs = lax.map(one_head, tuple(pieces))]
    dot_general x102 -> x0, matrix products: 48.8 us -> none  [the longest x16 16 us: attend_forward(): jnp.einsum('hij,hdj->hdi', weights, values, preferred_element_type=jnp.fl...]
  transfers between devices with their start and end apart: 6 -> 8, of which waited for: 3 -> 6; matrix products, arithmetic and copies ran while one was open for 27% -> 2% of each run, Pallas kernels for 0% -> 4%
where the time goes in v1:
time: 233 us; the launch traced here: 231 us
  waiting for transfers between devices  73.7 us (32%)
  blocking collectives  65.9 us (28%)
  starting transfers between devices  35.1 us (15%)
  Pallas kernels  31.3 us (13%)
  between operations  14.1 us (6%)
  local copies, waits for them, and re-layouts  6.01 us (3%)
  other arithmetic  4.43 us (2%)
    all_to_all x6, waiting for transfers between devices, swap(): return lax.all_to_all(x, axes, split_axis=0, concat_axis=0, tiled=True)  73.7 us
    all_to_all x2, blocking collectives, swap(): return lax.all_to_all(x, axes, split_axis=0, concat_axis=0, tiled=True)  65.9 us
    all_to_all x6, starting transfers between devices, swap(): return lax.all_to_all(x, axes, split_axis=0, concat_axis=0, tiled=True)  35 us
    pallas_call x1, Pallas kernels, run_layer(): pl.pallas_call(layer_kernel, out_shape=(block, block, piece, piece), in_s...  22.6 us
    pallas_call x1, Pallas kernels, on_device(): pl.pallas_call(settle_kernel, out_shape=(jax.ShapeDtypeStruct((HIST, DH,...  4.82 us
  transfers between devices with their start and end apart: 8, of which 6 were waited for; matrix products, arithmetic and copies ran while one was open for 2% of the time, Pallas kernels for 4%

profile of v1, /device:TPU:34, one launch (start us, length us, event | category | flops | bytes accessed | tf_op | source)
XLA Modules:
  0.0 230.5 jit_solution(4825094485866104459)
XLA Ops:
  7.2 1.8 pad_maximum_fusion
  9.0 0.8 copy.17.route
  9.8 0.7 copy-done.1
  10.4 0.8 shard_map.93
  11.2 43.1 %all_to_all.40.arrived = bf16[32,80,256]{2,1,0:T(8,128)(2,1)S(1)} all-to-all(bf16[32,80,256]{2,1,0:T(8,128)(2,1)S(1)} %shard_map.93), channel_id=1, replica_groups=mesh['y'=4,'x'=4,'zlo'=2,'zhi'=4,'core'=2] {'y','x','zlo'}, dimensions={0} | all-to-all | bytes 2621440 | tf_op jit(solution)/shard_map/all_to_all | solution.py:277
  54.3 4.8 %shard_map.94 = (bf16[16,64,256]{2,1,0:T(8,128)(2,1)}, s32[2,16]{1,0:T(2,128)S(1)}) custom-call(bf16[32,80,256]{2,1,0:T(8,128)(2,1)S(1)} %all_to_all.40.arrived), custom_call_target="tpu_custom_call" | custom-call | tf_op jit(solution)/shard_map/pallas_call | solution.py:294
  59.2 11.1 %all-to-all-start.1 = ((bf16[16,64,256]{2,1,0:T(8,128)(2,1)}), bf16[16,64,256]{2,1,0:T(8,128)(2,1)S(1)}, u32[]{:S(2)}, u32[]{:S(2)}) async-start(bf16[16,64,256]{2,1,0:T(8,128)(2,1)} %get-tuple-element.11), calls=%async_computation.1 | async-start | bytes 1048576 | tf_op jit(solution)/shard_map/all_to_all | solution.py:277
  70.2 0.1 pad_add_fusion.place
  70.3 1.1 constant_dynamic-slice_fusion.gy_ref
  71.4 17.2 %all-to-all-done.1 = bf16[16,64,256]{2,1,0:T(8,128)(2,1)S(1)} async-done(((bf16[16,64,256]{2,1,0:T(8,128)(2,1)}), bf16[16,64,256]{2,1,0:T(8,128)(2,1)S(1)}, u32[]{:S(2)}, u32[]{:S(2)}) %all-to-all-start.1) | async-done | bytes 524320 | tf_op jit(solution)/shard_map/all_to_all | solution.py:277
  88.6 22.6 %shard_map.95 = (bf16[8,2,64,256]{3,2,1,0:T(8,128)(2,1)}, bf16[8,2,64,256]{3,2,1,0:T(8,128)(2,1)}, bf16[16,4,80,128]{3,2,1,0:T(8,128)(2,1)S(1)}, bf16[16,4,80,128]{3,2,1,0:T(8,128)(2,1)}) custom-call(s32[2]{0:T(128)S(1)} %pad_add_fusion.place, s32[2,16]{1,0:T(2,128)S(1)} %get-tuple-element.10.meta, bf16[8,2,64,256]{3,2,1,0:T(8,128)(2,1)S(1)} %bitcast.21, ...), custom_call_target="tpu_custom_call" | custom-call | tf_op jit(solution)/shard_map/pallas_call | solution.py:250
  111.2 3.5 %all-to-all-start.3 = ((bf16[16,64,256]{2,1,0:T(8,128)(2,1)}), bf16[16,64,256]{2,1,0:T(8,128)(2,1)S(1)}, u32[]{:S(2)}, u32[]{:S(2)}) async-start(bf16[16,64,256]{2,1,0:T(8,128)(2,1)} %bitcast.7), calls=%async_computation.3 | async-start | bytes 1048576 | tf_op jit(solution)/shard_map/all_to_all | solution.py:277
  114.7 1.7 add_convert_fusion
  116.3 16.1 %all-to-all-done.3.rows = bf16[16,64,256]{2,1,0:T(8,128)(2,1)S(1)} async-done(((bf16[16,64,256]{2,1,0:T(8,128)(2,1)}), bf16[16,64,256]{2,1,0:T(8,128)(2,1)S(1)}, u32[]{:S(2)}, u32[]{:S(2)}) %all-to-all-start.3) | async-done | bytes 524320 | tf_op jit(solution)/shard_map/all_to_all | solution.py:277
  132.4 22.8 %all_to_all.41 = bf16[16,4,80,128]{3,2,1,0:T(8,128)(2,1)S(1)} all-to-all(bf16[16,4,80,128]{3,2,1,0:T(8,128)(2,1)S(1)} %add_convert_fusion), channel_id=1, replica_groups=mesh['y'=4,'x'=4,'zlo'=2,'zhi'=4,'core'=2] {'y','x'}, dimensions={0} | all-to-all | bytes 2621440 | tf_op jit(solution)/shard_map/all_to_all | solution.py:277
  155.2 3.5 %all-to-all-start.2 = ((bf16[16,64,256]{2,1,0:T(8,128)(2,1)}), bf16[16,64,256]{2,1,0:T(8,128)(2,1)S(1)}, u32[]{:S(2)}, u32[]{:S(2)}) async-start(bf16[16,64,256]{2,1,0:T(8,128)(2,1)} %bitcast.6), calls=%async_computation.2 | async-start | bytes 1048576 | tf_op jit(solution)/shard_map/all_to_all | solution.py:277
  158.7 0.8 reduce_sum.24
  159.6 15.4 %all-to-all-done.2 = bf16[16,64,256]{2,1,0:T(8,128)(2,1)S(1)} async-done(((bf16[16,64,256]{2,1,0:T(8,128)(2,1)}), bf16[16,64,256]{2,1,0:T(8,128)(2,1)S(1)}, u32[]{:S(2)}, u32[]{:S(2)}) %all-to-all-start.2) | async-done | bytes 524320 | tf_op jit(solution)/shard_map/all_to_all | solution.py:277
  175.0 4.7 %all-to-all-start.6 = ((bf16[8,40,128]{2,1,0:T(8,128)(2,1)}), bf16[8,40,128]{2,1,0:T(8,128)(2,1)S(1)}, u32[]{:S(2)}, u32[]{:S(2)}) async-start(bf16[8,40,128]{2,1,0:T(8,128)(2,1)} %bitcast.8), calls=%async_computation.6 | async-start | bytes 163840 | tf_op jit(solution)/shard_map/all_to_all | solution.py:277
  179.7 1.6 shard_map.96
  181.4 5.5 %all-to-all-done.6 = bf16[8,40,128]{2,1,0:T(8,128)(2,1)S(1)} async-done(((bf16[8,40,128]{2,1,0:T(8,128)(2,1)}), bf16[8,40,128]{2,1,0:T(8,128)(2,1)S(1)}, u32[]{:S(2)}, u32[]{:S(2)}) %all-to-all-start.6) | async-done | bytes 81952 | tf_op jit(solution)/shard_map/all_to_all | solution.py:277
  186.9 5.9 %all-to-all-start.4 = ((bf16[32,64,256]{2,1,0:T(8,128)(2,1)}), bf16[32,64,256]{2,1,0:T(8,128)(2,1)S(1)}, u32[]{:S(2)}, u32[]{:S(2)}) async-start(bf16[32,64,256]{2,1,0:T(8,128)(2,1)} %shard_map.96), calls=%async_computation.4 | async-start | bytes 2097152 | tf_op jit(solution)/shard_map/all_to_all | solution.py:277
  192.8 13.0 %all-to-all-done.4.arrived = bf16[32,64,256]{2,1,0:T(8,128)(2,1)S(1)} async-done(((bf16[32,64,256]{2,1,0:T(8,128)(2,1)}), bf16[32,64,256]{2,1,0:T(8,128)(2,1)S(1)}, u32[]{:S(2)}, u32[]{:S(2)}) %all-to-all-start.4) | async-done | bytes 1048608 | tf_op jit(solution)/shard_map/all_to_all | solution.py:277
  205.9 0.8 broadcast_in_dim.2
  206.7 6.3 %all-to-all-start.7 = ((bf16[32,40,128]{2,1,0:T(8,128)(2,1)}), bf16[32,40,128]{2,1,0:T(8,128)(2,1)S(1)}, u32[]{:S(2)}, u32[]{:S(2)}) async-start(bf16[32,40,128]{2,1,0:T(8,128)(2,1)} %broadcast_in_dim.2), calls=%async_computation.7 | async-start | bytes 655360 | tf_op jit(solution)/shard_map/all_to_all | solution.py:277
  213.0 1.5 shard_map.97
  214.5 6.4 %all-to-all-done.7 = bf16[32,40,128]{2,1,0:T(8,128)(2,1)S(1)} async-done(((bf16[32,40,128]{2,1,0:T(8,128)(2,1)}), bf16[32,40,128]{2,1,0:T(8,128)(2,1)S(1)}, u32[]{:S(2)}, u32[]{:S(2)}) %all-to-all-start.7) | async-done | bytes 327712 | tf_op jit(solution)/shard_map/all_to_all | solution.py:277
  220.8 0.1 convert_multiply_fusion
  220.9 0.4 copy.19
  221.4 0.7 slice.9
  222.1 0.8 slice.8
  222.9 0.8 copy.24
  (10 shorter events, 0.1 us)
Async XLA Ops:
  7.2 2.6 %copy-start = (bf16[16,64,256]{2,1,0:T(8,128)(2,1)S(1)}, bf16[16,64,256]{2,1,0:T(8,128)(2,1)}, u32[]{:S(2)}) copy-start(bf16[16,64,256]{2,1,0:T(8,128)(2,1)} %rows.1) | copy-start | bytes 1572868
  7.2 81.4 %all-gather.3.cloned.1.call-start = ((), (), s32[]{:S(2)}) async-start(), calls=%async_computation.8 | async-start | bytes 2949120 | tf_op jit(solution)/shard_map/all_gather | solution.py:286
  9.8 0.7 copy-start.1
  59.2 29.4 %all-to-all-start.1 = ((bf16[16,64,256]{2,1,0:T(8,128)(2,1)}), bf16[16,64,256]{2,1,0:T(8,128)(2,1)S(1)}, u32[]{:S(2)}, u32[]{:S(2)}) async-start(bf16[16,64,256]{2,1,0:T(8,128)(2,1)} %get-tuple-element.11), calls=%async_computation.1 | async-start | bytes 1048576 | tf_op jit(solution)/shard_map/all_to_all | solution.py:277
  111.2 3.5 %collective-permute-start = (bf16[16,4,80,128]{3,2,1,0:T(8,128)(2,1)}, bf16[16,4,80,128]{3,2,1,0:T(8,128)(2,1)}, u32[]{:S(2)}, u32[]{:S(2)}) collective-permute-start(bf16[16,4,80,128]{3,2,1,0:T(8,128)(2,1)} %get-tuple-element.15), channel_id=1, source_target_pairs={{0,1},{1,0},{2,3},{3,2},{4,5},{5,4},{6,7},{7,6},{8,9},{9,8},{10,11... | collective-permute-start | bytes 3932168 | tf_op jit(solution)/shard_map/ppermute | solution.py:308
  111.2 21.3 %all-to-all-start.3 = ((bf16[16,64,256]{2,1,0:T(8,128)(2,1)}), bf16[16,64,256]{2,1,0:T(8,128)(2,1)S(1)}, u32[]{:S(2)}, u32[]{:S(2)}) async-start(bf16[16,64,256]{2,1,0:T(8,128)(2,1)} %bitcast.7), calls=%async_computation.3 | async-start | bytes 1048576 | tf_op jit(solution)/shard_map/all_to_all | solution.py:277
  155.2 19.8 %all-to-all-start.2 = ((bf16[16,64,256]{2,1,0:T(8,128)(2,1)}), bf16[16,64,256]{2,1,0:T(8,128)(2,1)S(1)}, u32[]{:S(2)}, u32[]{:S(2)}) async-start(bf16[16,64,256]{2,1,0:T(8,128)(2,1)} %bitcast.6), calls=%async_computation.2 | async-start | bytes 1048576 | tf_op jit(solution)/shard_map/all_to_all | solution.py:277
  175.0 11.8 %all-to-all-start.6 = ((bf16[8,40,128]{2,1,0:T(8,128)(2,1)}), bf16[8,40,128]{2,1,0:T(8,128)(2,1)S(1)}, u32[]{:S(2)}, u32[]{:S(2)}) async-start(bf16[8,40,128]{2,1,0:T(8,128)(2,1)} %bitcast.8), calls=%async_computation.6 | async-start | bytes 163840 | tf_op jit(solution)/shard_map/all_to_all | solution.py:277
  186.9 19.0 %all-to-all-start.4 = ((bf16[32,64,256]{2,1,0:T(8,128)(2,1)}), bf16[32,64,256]{2,1,0:T(8,128)(2,1)S(1)}, u32[]{:S(2)}, u32[]{:S(2)}) async-start(bf16[32,64,256]{2,1,0:T(8,128)(2,1)} %shard_map.96), calls=%async_computation.4 | async-start | bytes 2097152 | tf_op jit(solution)/shard_map/all_to_all | solution.py:277
  206.7 14.2 %all-to-all-start.7 = ((bf16[32,40,128]{2,1,0:T(8,128)(2,1)}), bf16[32,40,128]{2,1,0:T(8,128)(2,1)S(1)}, u32[]{:S(2)}, u32[]{:S(2)}) async-start(bf16[32,40,128]{2,1,0:T(8,128)(2,1)} %broadcast_in_dim.2), calls=%async_computation.7 | async-start | bytes 655360 | tf_op jit(solution)/shard_map/all_to_all | solution.py:277
Sparse Core Ops, SparseCore 0:
  10.4 49.2 all-gather.2

commit v2 on v1

v2 whole, which is shorter than its diff:
```python
import jax
import jax.numpy as jnp
from jax import lax
from jax.experimental import pallas as pl
from jax.experimental.pallas import tpu as pltpu
from jax.sharding import Mesh
from jax.sharding import PartitionSpec as P

D = 512
H = 8
DH = 64
SLOT = 256
HIST = 16
EPS = 1e-05
META = 16
ROWS = 5 * DH
PIECE = ROWS // 4
F32 = jnp.float32
BF16 = jnp.bfloat16
DP = ("y", "x", "zlo")
COL = ("zhi", "core")
VMEM = pl.BlockSpec(memory_space=pltpu.VMEM)
SMEM = pl.BlockSpec(memory_space=pltpu.SMEM)


def params(mib):
    return pltpu.CompilerParams(vmem_limit_bytes=mib * 1024 * 1024)


def spread_kernel(route, lengths, rows, sent):
    sent[...] = jnp.zeros_like(sent)
    for h in range(HIST):
        group = route[h, 0]
        sent[group, :DH, :] = rows[h]
        slot = (route[h, 1] + 1).astype(F32)
        count = lengths[h].astype(F32)
        sent[group, DH:, : SLOT // 2] = jnp.full((META, SLOT // 2), slot, F32).astype(BF16)
        sent[group, DH:, SLOT // 2 :] = jnp.full((META, SLOT // 2), count, F32).astype(BF16)


def settle_kernel(arrived, rows, meta):
    codes = []
    for group in range(arrived.shape[0]):
        note = arrived[group, DH:, :].astype(F32)[:8]
        code = jnp.max(note[:, : SLOT // 2] * 512.0 + note[:, SLOT // 2 :])
        codes.append(code.astype(jnp.int32))
    for group, code in enumerate(codes):

        @pl.when(code >= 512)
        def _():
            slot = lax.shift_right_logical(code, 9) - 1
            rows[slot] = arrived[group, :DH, :]
            meta[0, slot] = group
            meta[1, slot] = code & 511


def return_kernel(meta, rows, sent):
    sent[...] = jnp.zeros_like(sent)
    for k in range(HIST):
        sent[meta[0, k]] = rows[k]


def collect_kernel(route, arrived, rows):
    for h in range(HIST):
        rows[h] = arrived[route[h, 0]]


def tn(a, b):
    return lax.dot_general(a, b, (((0,), (0,)), ((), ())), preferred_element_type=F32)


def nt(a, b):
    return lax.dot_general(a, b, (((1,), (1,)), ((), ())), preferred_element_type=F32)


def nn(a, b):
    return lax.dot_general(a, b, (((1,), (0,)), ((), ())), preferred_element_type=F32)


def silu_parts(z):
    sigma = 0.5 * jnp.tanh(0.5 * z) + 0.5
    silu = z * sigma
    return silu, sigma + silu * (1.0 - sigma)


def wrap(position, back):
    return lax.rem(position - back + 4, 4)


def forward_kernel(
    place,
    meta,
    xa,
    own0,
    own1,
    own2,
    own3,
    far0,
    far1,
    far2,
    far3,
    mixed,
    win,
    wout,
    xn,
    inv_in,
    slopes,
    proj,
    weights,
    score_slopes,
    out_norm,
    inv_out,
    gated,
    x_s,
):
    tokens = 2 * SLOT
    col = place[0]
    core = place[1]
    factor = BF16(DH**-0.5)
    for i in range(2):
        x_s[:, i * SLOT : (i + 1) * SLOT] = xa[:, i].reshape(D, SLOT).astype(F32)
    for side, refs, along in ((core, (own0, own1, own2, own3), place[3]), (1 - core, (far0, far1, far2, far3), place[4])):
        for k in range(4):
            piece = wrap(along, k)
            for z in range(4):
                head = 2 * wrap(place[2], z) + side
                at = pl.multiple_of(piece * DH, DH)
                win[head, pl.ds(at, DH), :] = refs[k][z, :DH, :]
                at = pl.multiple_of(head * DH + piece * (DH // 4), DH // 4)
                wout[pl.ds(at, DH // 4), :] = refs[k][z, DH:, :]

    for i in range(tokens // 128):
        lanes = slice(i * 128, (i + 1) * 128)
        x = x_s[:, lanes]
        centred = x - jnp.mean(x, axis=0, keepdims=True)
        inv = lax.rsqrt(jnp.mean(centred * centred, axis=0, keepdims=True) + EPS)
        inv_in[:, lanes] = inv
        xn[:, lanes] = (centred * inv).astype(BF16)

    key_at = lax.broadcasted_iota(jnp.int32, (SLOT, SLOT), 0)
    query_at = lax.broadcasted_iota(jnp.int32, (SLOT, SLOT), 1)

    def head_step(h, sums):
        silu, slope = silu_parts(nn(win[h], xn[...]))
        slopes[h] = slope.astype(BF16)
        proj[h] = silu.astype(BF16)
        parts = []
        for i in range(2):
            lanes = slice(i * SLOT, (i + 1) * SLOT)
            value = proj[h, DH : 2 * DH, lanes]
            query = proj[h, 2 * DH : 3 * DH, lanes]
            key = proj[h, 3 * DH :, lanes] * factor
            live = (key_at <= query_at) & (query_at < meta[1, 2 * col + i])
            silu_w, slope_w = silu_parts(tn(key, query))
            weight = jnp.where(live, silu_w, 0.0).astype(BF16)
            weights[h, i] = weight
            score_slopes[h, i] = jnp.where(live, slope_w, 0.0).astype(BF16)
            parts.append(nn(value, weight))
        att = jnp.concatenate(parts, axis=1)
        out_norm[pl.ds(h * DH, DH), :] = att
        return (
            sums[0] + jnp.sum(att, axis=0, keepdims=True),
            sums[1] + jnp.sum(att * att, axis=0, keepdims=True),
        )

    zero = jnp.zeros((1, tokens), F32)
    totals, squares = lax.fori_loop(0, H, head_step, (zero, zero))
    mean = totals / D
    inv = lax.rsqrt(squares / D - mean * mean + EPS)
    inv_out[...] = inv

    def gate_step(h, carry):
        rows = pl.ds(h * DH, DH)
        normed = (out_norm[rows, :] - mean) * inv
        out_norm[rows, :] = normed
        gated[rows, :] = (normed * proj[h, :DH, :].astype(F32)).astype(BF16)
        return carry

    lax.fori_loop(0, H, gate_step, 0)
    out = (x_s[...] + tn(wout[...], gated[...])).astype(BF16)
    for i in range(2):
        mixed[:, i] = out[:, i * SLOT : (i + 1) * SLOT].reshape(H, DH, SLOT)


def backward_kernel(
    place,
    gy_ref,
    win,
    wout,
    xn,
    inv_in,
    slopes,
    proj,
    weights,
    score_slopes,
    out_norm,
    inv_out,
    gated,
    gfeat,
    mine,
    other,
    grad_s,
    gy_s,
    gatt_s,
    gpre_s,
    sum_s,
    gwo_s,
):
    tokens = 2 * SLOT
    core = place[1]
    factor = BF16(DH**-0.5)
    for i in range(2):
        gy_s[:, i * SLOT : (i + 1) * SLOT] = gy_ref[i]
    grad_s[...] = nn(wout[...], gy_s[...])
    gwo_s[...] = nt(gated[...], gy_s[...]).astype(BF16)

    def sum_step(h, sums):
        rows = pl.ds(h * DH, DH)
        grad = grad_s[rows, :] * proj[h, :DH, :].astype(F32)
        return (
            sums[0] + jnp.sum(grad, axis=0, keepdims=True),
            sums[1] + jnp.sum(grad * out_norm[rows, :], axis=0, keepdims=True),
        )

    zero = jnp.zeros((1, tokens), F32)
    first, second = lax.fori_loop(0, H, sum_step, (zero, zero))
    first = first / D
    second = second / D
    inv = inv_out[...]

    def store_grad(ref, at, grad_win, grad_wout):
        for part in range(4):
            lanes = slice(part * 128, (part + 1) * 128)
            for c in range(4):
                ref[4 * part + c, at, :DH, :] = grad_win[c * DH : (c + 1) * DH, lanes]
                ref[4 * part + c, at, DH:, :] = grad_wout[c * DH // 4 : (c + 1) * DH // 4, lanes]

    sum_s[...] = jnp.zeros_like(sum_s)

    def head_step(h, carry):
        rows = pl.ds(h * DH, DH)
        grad_gated = grad_s[rows, :]
        normed = out_norm[rows, :]
        grad_normo = grad_gated * proj[h, :DH, :].astype(F32)
        gatt_s[...] = (inv * (grad_normo - first - normed * second)).astype(BF16)
        gpre_s[:DH, :] = (grad_gated * normed * slopes[h, :DH, :].astype(F32)).astype(BF16)
        for i in range(2):
            lanes = slice(i * SLOT, (i + 1) * SLOT)
            value = proj[h, DH : 2 * DH, lanes]
            query = proj[h, 2 * DH : 3 * DH, lanes] * factor
            key = proj[h, 3 * DH :, lanes] * factor
            grad = gatt_s[:, lanes]
            grad_scores = (tn(value, grad) * score_slopes[h, i].astype(F32)).astype(BF16)
            grad_value = nt(grad, weights[h, i])
            grad_query = nn(key, grad_scores)
            grad_key = nt(query, grad_scores)
            for c, part in ((1, grad_value), (2, grad_query), (3, grad_key)):
                at = slice(c * DH, (c + 1) * DH)
                gpre_s[at, lanes] = (part * slopes[h, at, lanes].astype(F32)).astype(BF16)
        grad_win = nt(gpre_s[...], xn[...]).astype(BF16)
        grad_wout = gwo_s[rows, :]

        @pl.when(h % 2 == core)
        def _():
            store_grad(mine, h // 2, grad_win, grad_wout)

        @pl.when(h % 2 != core)
        def _():
            store_grad(other, h // 2, grad_win, grad_wout)

        sum_s[...] += tn(win[h], gpre_s[...])
        return carry

    lax.fori_loop(0, H, head_step, 0)
    for i in range(tokens // 128):
        lanes = slice(i * 128, (i + 1) * 128)
        grad = sum_s[:, lanes]
        normed = xn[:, lanes].astype(F32)
        lead = jnp.mean(grad, axis=0, keepdims=True)
        cross = jnp.mean(grad * normed, axis=0, keepdims=True)
        total = gy_s[:, lanes].astype(F32) + inv_in[:, lanes] * (grad - lead - normed * cross)
        here = slice(i % 2 * 128, (i % 2 + 1) * 128)
        gfeat[:, i // 2, :, here] = total.astype(BF16).reshape(H, DH, 128)


def run_forward(place, meta, xa, pieces):
    tokens = 2 * SLOT
    shape = jax.ShapeDtypeStruct
    return pl.pallas_call(
        forward_kernel,
        out_shape=(
            shape((H, 2, DH, SLOT), BF16),
            shape((H, 4 * DH, D), BF16),
            shape((D, D), BF16),
            shape((D, tokens), BF16),
            shape((1, tokens), F32),
            shape((H, 4 * DH, tokens), BF16),
            shape((H, 4 * DH, tokens), BF16),
            shape((H, 2, SLOT, SLOT), BF16),
            shape((H, 2, SLOT, SLOT), BF16),
            shape((D, tokens), F32),
            shape((1, tokens), F32),
            shape((D, tokens), BF16),
        ),
        in_specs=[SMEM, SMEM] + [VMEM] * 9,
        out_specs=(VMEM,) * 12,
        scratch_shapes=[pltpu.VMEM((D, tokens), F32)],
        compiler_params=params(28),
    )(place, meta, xa, *pieces)


def run_backward(place, grad_y, saved):
    tokens = 2 * SLOT
    piece = jax.ShapeDtypeStruct((16, 4, PIECE, 128), BF16)
    return pl.pallas_call(
        backward_kernel,
        out_shape=(jax.ShapeDtypeStruct((H, 2, DH, SLOT), BF16), piece, piece),
        in_specs=[SMEM] + [VMEM] * 12,
        out_specs=(VMEM,) * 3,
        scratch_shapes=[
            pltpu.VMEM((D, tokens), F32),
            pltpu.VMEM((D, tokens), BF16),
            pltpu.VMEM((DH, tokens), BF16),
            pltpu.VMEM((4 * DH, tokens), BF16),
            pltpu.VMEM((D, tokens), F32),
            pltpu.VMEM((D, D), BF16),
        ],
        compiler_params=params(32),
    )(place, grad_y, *saved)


def finish_kernel(arrived, grad_in, grad_out):
    factor = float(HIST * 32 * SLOT) ** -0.5
    for part in range(4):
        lanes = slice(part * 128, (part + 1) * 128)
        for c in range(4):
            block = arrived[4 * part + c].astype(F32) * factor
            grad_in[c, :, lanes] = block[:DH]
            grad_out[c * DH // 4 : (c + 1) * DH // 4, lanes] = block[DH:]


def gather_weights(w_in, w_out, place):
    along = place[3]
    proj = lax.dynamic_index_in_dim(w_in.transpose(0, 2, 1), along, 0, keepdims=False)
    rows = lax.dynamic_slice_in_dim(w_out, along * (DH // 4), DH // 4, 0)
    piece = jnp.concatenate([proj, rows], axis=0)
    shards = [piece]
    for k in range(1, 4):
        shards.append(lax.ppermute(piece, "zhi", [(i, (i + k) % 4) for i in range(4)]))
    own = [jnp.stack(shards)]
    for k in range(1, 4):
        pairs = []
        for y in range(4):
            for x in range(4):
                pairs.append(((4 * y + x) * 2, (4 * y + (x + k) % 4) * 2))
                pairs.append(((4 * y + x) * 2 + 1, (4 * ((y + k) % 4) + x) * 2 + 1))
        own.append(lax.ppermute(own[0], ("y", "x", "core"), pairs))
    return own + [lax.ppermute(part, "core", [(0, 1), (1, 0)]) for part in own]


def swap(x, axes):
    return lax.all_to_all(x, axes, split_axis=0, concat_axis=0, tiled=True)


def on_device(features, cotangent, lengths, route, w_in, w_out):
    groups = lax.axis_size(DP)
    col = lax.axis_index(COL)
    core = lax.axis_index("core")
    zhi = lax.axis_index("zhi")
    x = lax.axis_index("x")
    y = lax.axis_index("y")
    along = jnp.where(core == 0, x, y)
    place = jnp.stack([col, core, zhi, along, x + y - along]).astype(jnp.int32)

    sent = pl.pallas_call(
        spread_kernel,
        out_shape=jax.ShapeDtypeStruct((groups, DH + META, SLOT), BF16),
        in_specs=[SMEM, SMEM, VMEM],
        out_specs=VMEM,
        compiler_params=params(16),
    )(route, lengths, features)
    arrived = swap(sent, DP)
    pieces = gather_weights(w_in, w_out, place)
    rows, meta = pl.pallas_call(
        settle_kernel,
        out_shape=(
            jax.ShapeDtypeStruct((HIST, DH, SLOT), BF16),
            jax.ShapeDtypeStruct((2, HIST), jnp.int32),
        ),
        in_specs=[VMEM],
        out_specs=(VMEM, SMEM),
        compiler_params=params(16),
    )(arrived)
    xa = swap(rows, COL).reshape(H, 2, DH, SLOT)
    grad_y = lax.dynamic_slice_in_dim(cotangent, 2 * col, 2, 0)
    mixed, *saved = run_forward(place, meta, xa, pieces)
    mixed = swap(mixed.reshape(HIST, DH, SLOT), COL)
    gfeat, mine, other = run_backward(place, grad_y, saved)

    came = lax.ppermute(other, "core", [(0, 1), (1, 0)])
    home = swap(gfeat.reshape(HIST, DH, SLOT), COL)
    half = (mine.astype(F32) + came.astype(F32)).astype(BF16)
    part = jnp.sum(swap(half, ("y", "x")).reshape(16, 4, PIECE, 128).astype(F32), axis=0)
    part = part.astype(BF16)
    total = lax.dynamic_index_in_dim(part, zhi, 0, keepdims=False).astype(F32)
    for k in range(1, 4):
        chunk = lax.dynamic_index_in_dim(part, (zhi + k) % 4, 0, keepdims=False)
        total = total + lax.ppermute(chunk, "zhi", [(i, (i + k) % 4) for i in range(4)]).astype(F32)
    pair = lax.ppermute(total.astype(BF16), "zlo", [(0, 1), (1, 0)])
    part = (total + pair.astype(F32)).astype(BF16)
    whole = swap(jnp.broadcast_to(part[None], (16, PIECE, 128)), ("y", "x"))
    grad_in, grad_out = pl.pallas_call(
        finish_kernel,
        out_shape=(jax.ShapeDtypeStruct((4, DH, D), F32), jax.ShapeDtypeStruct((DH, D), F32)),
        in_specs=[VMEM],
        out_specs=(VMEM, VMEM),
        compiler_params=params(16),
    )(whole)

    back = pl.pallas_call(
        return_kernel,
        out_shape=jax.ShapeDtypeStruct((groups, DH, SLOT), BF16),
        in_specs=[SMEM, VMEM],
        out_specs=VMEM,
        compiler_params=params(16),
    )(meta, home)
    grad_features = pl.pallas_call(
        collect_kernel,
        out_shape=jax.ShapeDtypeStruct((HIST, DH, SLOT), BF16),
        in_specs=[SMEM, VMEM],
        out_specs=VMEM,
        compiler_params=params(16),
    )(route, swap(back, DP))
    return (mixed, grad_features, grad_in.transpose(0, 2, 1), grad_out)


def solution(mesh):
    split = Mesh(mesh.devices.reshape(4, 4, 2, 4, 2), ("y", "x", "zlo", "zhi", "core"))
    in_specs = (P(DP, COL, None), P(DP, None, None), P(DP), P(DP, None), P(None, None, COL), P(COL, None))
    out_specs = (P(DP, COL, None), P(DP, COL, None), P(None, None, COL), P(COL, None))
    return jax.shard_map(
        on_device, mesh=split, in_specs=in_specs, out_specs=out_specs, check_vma=False
    )
```

time: 233 us -> 212 us (0.910)
  blocking collectives: 65.9 us -> 24.1 us
  starting transfers between devices: 35.1 us -> 57.9 us
  between operations: 14.1 us -> 0.84 us
  waiting for transfers between devices: 73.7 us -> 85.9 us
  other arithmetic: 4.43 us -> 2.06 us
    all_to_all x2 -> x1, blocking collectives: 65.9 us -> 24.1 us  [swap(): return lax.all_to_all(x, axes, split_axis=0, concat_axis=0, tiled=True)]
    ppermute x0 -> x14, waiting for transfers between devices: none -> 36.6 us  [the longest x3 16.4 us: gather_weights(): lax.ppermute(piece, 'zhi', [(i, (i + k) % 4) for i in range(4)])]
    all_to_all x6, waiting for transfers between devices: 73.7 us -> 49.3 us  [swap(): return lax.all_to_all(x, axes, split_axis=0, concat_axis=0, tiled=True)]
    ppermute x0 -> x14, starting transfers between devices: none -> 23.3 us  [the longest x3 8.93 us: gather_weights(): lax.ppermute(piece, 'zhi', [(i, (i + k) % 4) for i in range(4)])]
    pallas_call x1, Pallas kernels: 4.82 us -> 1.24 us  [on_device(): pl.pallas_call(settle_kernel, out_shape=(jax.ShapeDtypeStruct((HIST, DH,...]
    unnamed x7 -> x10, local copies, waits for them, and re-layouts: 2.25 us -> 5.45 us
    pallas_call x1 -> x3, Pallas kernels: 22.6 us -> 24.3 us  [the longest x1 12.6 us: run_backward(): pl.pallas_call(backward_kernel, out_shape=(jax.ShapeDtypeStruct((H, 2, DH...]
  transfers between devices with their start and end apart: 8 -> 21, of which waited for: 6 -> 13; matrix products, arithmetic and copies ran while one was open for 2% -> 2% of each run, Pallas kernels for 4% -> 1%
where the time goes in v2:
time: 212 us; the launch traced here: 210 us
  waiting for transfers between devices  85.9 us (41%)
  starting transfers between devices  57.9 us (27%)
  Pallas kernels  30.6 us (14%)
  blocking collectives  24.1 us (11%)
  local copies, waits for them, and re-layouts  8.13 us (4%)
    all_to_all x6, waiting for transfers between devices, swap(): return lax.all_to_all(x, axes, split_axis=0, concat_axis=0, tiled=True)  49.3 us
    all_to_all x6, starting transfers between devices, swap(): return lax.all_to_all(x, axes, split_axis=0, concat_axis=0, tiled=True)  34.5 us
    all_to_all x1, blocking collectives, swap(): return lax.all_to_all(x, axes, split_axis=0, concat_axis=0, tiled=True)  24.1 us
    ppermute x3, waiting for transfers between devices, gather_weights(): lax.ppermute(piece, 'zhi', [(i, (i + k) % 4) for i in range(4)])  16.4 us
    pallas_call x1, Pallas kernels, run_backward(): pl.pallas_call(backward_kernel, out_shape=(jax.ShapeDtypeStruct((H, 2, DH...  12.6 us
    pallas_call x1, Pallas kernels, run_forward(): pl.pallas_call(forward_kernel, out_shape=(shape((H, 2, DH, SLOT), BF16),...  10.9 us
    ppermute x3, starting transfers between devices, gather_weights(): lax.ppermute(piece, 'zhi', [(i, (i + k) % 4) for i in range(4)])  8.93 us
    ppermute x3, starting transfers between devices, on_device(): lax.ppermute(chunk, 'zhi', [(i, (i + k) % 4) for i in range(4)]).astype(F32)  8.81 us
  transfers between devices with their start and end apart: 21, of which 13 were waited for; matrix products, arithmetic and copies ran while one was open for 2% of the time, Pallas kernels for 1%

profile of v2, /device:TPU:34, one launch (start us, length us, event | category | flops | bytes accessed | tf_op | source)
XLA Modules:
  0.0 209.5 jit_solution(5917738694256165475)
XLA Ops:
  3.1 1.9 shard_map.93
  5.0 8.5 %all-to-all-start = ((bf16[32,80,256]{2,1,0:T(8,128)(2,1)}), bf16[32,80,256]{2,1,0:T(8,128)(2,1)S(1)}, u32[]{:S(2)}, u32[]{:S(2)}) async-start(bf16[32,80,256]{2,1,0:T(8,128)(2,1)} %shard_map.93), calls=%async_computation | async-start | bytes 2621440 | tf_op jit(solution)/shard_map/all_to_all | solution.py:362
  14.3 17.2 %all-to-all-done.arrived = bf16[32,80,256]{2,1,0:T(8,128)(2,1)S(1)} async-done(((bf16[32,80,256]{2,1,0:T(8,128)(2,1)}), bf16[32,80,256]{2,1,0:T(8,128)(2,1)S(1)}, u32[]{:S(2)}, u32[]{:S(2)}) %all-to-all-start) | async-done | bytes 1310752 | tf_op jit(solution)/shard_map/all_to_all | solution.py:362
  32.7 7.6 %all-to-all-start.1 = ((bf16[16,64,256]{2,1,0:T(8,128)(2,1)}), bf16[16,64,256]{2,1,0:T(8,128)(2,1)S(1)}, u32[]{:S(2)}, u32[]{:S(2)}) async-start(bf16[16,64,256]{2,1,0:T(8,128)(2,1)} %get-tuple-element.24), calls=%async_computation.1 | async-start | bytes 1048576 | tf_op jit(solution)/shard_map/all_to_all | solution.py:362
  40.3 4.2 %collective-permute-start.2 = (bf16[80,512]{1,0:T(8,128)(2,1)S(1)}, bf16[80,512]{1,0:T(8,128)(2,1)S(1)}, u32[]{:S(2)}, u32[]{:S(2)}) collective-permute-start(bf16[80,512]{1,0:T(8,128)(2,1)S(1)} %get-tuple-element.46), channel_id=1, source_target_pairs={{0,6},{2,0},{4,2},{6,4},{1,7},{3,1},{5,3},{7,5},{8,14},{10,8},{12,... | collective-permute-start | bytes 245768 | tf_op jit(solution)/shard_map/ppermute | solution.py:349
  44.5 2.4 %collective-permute-start.1 = (bf16[80,512]{1,0:T(8,128)(2,1)S(1)}, bf16[80,512]{1,0:T(8,128)(2,1)S(1)}, u32[]{:S(2)}, u32[]{:S(2)}) collective-permute-start(bf16[80,512]{1,0:T(8,128)(2,1)S(1)} %get-tuple-element.46), channel_id=1, source_target_pairs={{0,4},{2,6},{4,0},{6,2},{1,5},{3,7},{5,1},{7,3},{8,12},{10,14},{12... | collective-permute-start | bytes 245768 | tf_op jit(solution)/shard_map/ppermute | solution.py:349
  46.9 2.4 %collective-permute-start = (bf16[80,512]{1,0:T(8,128)(2,1)S(1)}, bf16[80,512]{1,0:T(8,128)(2,1)S(1)}, u32[]{:S(2)}, u32[]{:S(2)}) collective-permute-start(bf16[80,512]{1,0:T(8,128)(2,1)S(1)} %get-tuple-element.46), channel_id=1, source_target_pairs={{0,2},{2,4},{4,6},{6,0},{1,3},{3,5},{5,7},{7,1},{8,10},{10,12},{12... | collective-permute-start | bytes 245768 | tf_op jit(solution)/shard_map/ppermute | solution.py:349
  49.2 5.7 %collective-permute-done.2 = bf16[80,512]{1,0:T(8,128)(2,1)S(1)} collective-permute-done((bf16[80,512]{1,0:T(8,128)(2,1)S(1)}, bf16[80,512]{1,0:T(8,128)(2,1)S(1)}, u32[]{:S(2)}, u32[]{:S(2)}) %collective-permute-start.2) | collective-permute-done | bytes 81952 | tf_op jit(solution)/shard_map/ppermute | solution.py:349
  55.0 10.7 %collective-permute-done.1 = bf16[80,512]{1,0:T(8,128)(2,1)S(1)} collective-permute-done((bf16[80,512]{1,0:T(8,128)(2,1)S(1)}, bf16[80,512]{1,0:T(8,128)(2,1)S(1)}, u32[]{:S(2)}, u32[]{:S(2)}) %collective-permute-start.1) | collective-permute-done | bytes 81952 | tf_op jit(solution)/shard_map/ppermute | solution.py:349
  66.5 3.5 %collective-permute-start.4 = (bf16[4,80,512]{2,1,0:T(8,128)(2,1)S(1)}, bf16[4,80,512]{2,1,0:T(8,128)(2,1)S(1)}, u32[]{:S(2)}, u32[]{:S(2)}) collective-permute-start(bf16[4,80,512]{2,1,0:T(8,128)(2,1)S(1)} %pad_maximum_fusion.own0), channel_id=1, source_target_pairs={{0,32},{1,129},{16,48},{17,145},{32,0},{33,161},{48,16},{49,177},{... | collective-permute-start | bytes 983048 | tf_op jit(solution)/shard_map/ppermute | solution.py:357
  70.0 3.0 %collective-permute-done.3.own1 = bf16[4,80,512]{2,1,0:T(8,128)(2,1)S(1)} collective-permute-done((bf16[4,80,512]{2,1,0:T(8,128)(2,1)S(1)}, bf16[4,80,512]{2,1,0:T(8,128)(2,1)S(1)}, u32[]{:S(2)}, u32[]{:S(2)}) %collective-permute-start.3) | collective-permute-done | bytes 327712 | tf_op jit(solution)/shard_map/ppermute | solution.py:357
  73.0 2.2 %collective-permute-done.4.own2 = bf16[4,80,512]{2,1,0:T(8,128)(2,1)S(1)} collective-permute-done((bf16[4,80,512]{2,1,0:T(8,128)(2,1)S(1)}, bf16[4,80,512]{2,1,0:T(8,128)(2,1)S(1)}, u32[]{:S(2)}, u32[]{:S(2)}) %collective-permute-start.4) | collective-permute-done | bytes 327712 | tf_op jit(solution)/shard_map/ppermute | solution.py:357
  75.2 3.4 %collective-permute-done.5.own3 = bf16[4,80,512]{2,1,0:T(8,128)(2,1)S(1)} collective-permute-done((bf16[4,80,512]{2,1,0:T(8,128)(2,1)S(1)}, bf16[4,80,512]{2,1,0:T(8,128)(2,1)S(1)}, u32[]{:S(2)}, u32[]{:S(2)}) %collective-permute-start.5) | collective-permute-done | bytes 327712 | tf_op jit(solution)/shard_map/ppermute | solution.py:357
  80.4 10.9 %shard_map.95 = (bf16[8,2,64,256]{3,2,1,0:T(8,128)(2,1)}, bf16[8,256,512]{2,1,0:T(8,128)(2,1)S(1)}, bf16[512,512]{1,0:T(8,128)(2,1)S(1)}, bf16[512,512]{1,0:T(8,...) custom-call(s32[5]{0:T(128)S(1)} %stack.38.place, ...), custom_call_target="tpu_custom_call" | custom-call | tf_op jit(solution)/shard_map/pallas_call | solution.py:289
  91.2 12.6 %shard_map.96 = (bf16[8,2,64,256]{3,2,1,0:T(8,128)(2,1)}, bf16[16,4,80,128]{3,2,1,0:T(8,128)(2,1)S(1)}, bf16[16,4,80,128]{3,2,1,0:T(8,128)(2,1)}) custom-call(s32[5]{0:T(128)S(1)} %stack.38.place, bf16[2,512,256]{2,1,0:T(8,128)(2,1)S(1)} %constant_dynamic-slice_fusion.gy_ref, bf16[8,256,512]{2,1,0:T(8,128)(2,1)S(1)} %get-tuple-element.26.win, ...), custom_call_target="tpu_custom_call" | custom-call | tf_op jit(solution)/shard_map/pallas_call | solution.py:315
  103.9 4.3 %all-to-all-start.2 = ((bf16[16,64,256]{2,1,0:T(8,128)(2,1)}), bf16[16,64,256]{2,1,0:T(8,128)(2,1)}, u32[]{:S(2)}, u32[]{:S(2)}) async-start(bf16[16,64,256]{2,1,0:T(8,128)(2,1)} %bitcast.12), calls=%async_computation.2 | async-start | bytes 1048576 | tf_op jit(solution)/shard_map/all_to_all | solution.py:362
  109.4 1.8 add_convert_fusion
  111.1 13.7 %all-to-all-done.2 = bf16[16,64,256]{2,1,0:T(8,128)(2,1)} async-done(((bf16[16,64,256]{2,1,0:T(8,128)(2,1)}), bf16[16,64,256]{2,1,0:T(8,128)(2,1)}, u32[]{:S(2)}, u32[]{:S(2)}) %all-to-all-start.2) | async-done | bytes 524320 | tf_op jit(solution)/shard_map/all_to_all | solution.py:362
  124.8 24.1 %all_to_all.35 = bf16[16,4,80,128]{3,2,1,0:T(8,128)(2,1)S(1)} all-to-all(bf16[16,4,80,128]{3,2,1,0:T(8,128)(2,1)S(1)} %add_convert_fusion), channel_id=1, replica_groups=mesh['y'=4,'x'=4,'zlo'=2,'zhi'=4,'core'=2] {'y','x'}, dimensions={0} | all-to-all | bytes 2621440 | tf_op jit(solution)/shard_map/all_to_all | solution.py:362
  148.9 3.5 %all-to-all-start.3 = ((bf16[16,64,256]{2,1,0:T(8,128)(2,1)}), bf16[16,64,256]{2,1,0:T(8,128)(2,1)S(1)}, u32[]{:S(2)}, u32[]{:S(2)}) async-start(bf16[16,64,256]{2,1,0:T(8,128)(2,1)} %bitcast.13), calls=%async_computation.3 | async-start | bytes 1048576 | tf_op jit(solution)/shard_map/all_to_all | solution.py:362
  152.6 4.1 %collective-permute-start.13 = (bf16[80,128]{1,0:T(8,128)(2,1)S(1)}, bf16[80,128]{1,0:T(8,128)(2,1)S(1)}, u32[]{:S(2)}, u32[]{:S(2)}) collective-permute-start(bf16[80,128]{1,0:T(8,128)(2,1)S(1)} %get-tuple-element.43), channel_id=1, source_target_pairs={{0,6},{2,0},{4,2},{6,4},{1,7},{3,1},{5,3},{7,5},{8,14},{10,8},{12,... | collective-permute-start | bytes 61448 | tf_op jit(solution)/shard_map/ppermute | solution.py:408
  156.7 2.3 %collective-permute-start.12 = (bf16[80,128]{1,0:T(8,128)(2,1)S(1)}, bf16[80,128]{1,0:T(8,128)(2,1)S(1)}, u32[]{:S(2)}, u32[]{:S(2)}) collective-permute-start(bf16[80,128]{1,0:T(8,128)(2,1)S(1)} %get-tuple-element.44), channel_id=1, source_target_pairs={{0,4},{2,6},{4,0},{6,2},{1,5},{3,7},{5,1},{7,3},{8,12},{10,14},{12... | collective-permute-start | bytes 61448 | tf_op jit(solution)/shard_map/ppermute | solution.py:408
  159.1 2.4 %collective-permute-start.11 = (bf16[80,128]{1,0:T(8,128)(2,1)S(1)}, bf16[80,128]{1,0:T(8,128)(2,1)S(1)}, u32[]{:S(2)}, u32[]{:S(2)}) collective-permute-start(bf16[80,128]{1,0:T(8,128)(2,1)S(1)} %get-tuple-element.42), channel_id=1, source_target_pairs={{0,2},{2,4},{4,6},{6,0},{1,3},{3,5},{5,7},{7,1},{8,10},{10,12},{12... | collective-permute-start | bytes 61448 | tf_op jit(solution)/shard_map/ppermute | solution.py:408
  161.4 7.1 %collective-permute-done.13 = bf16[80,128]{1,0:T(8,128)(2,1)S(1)} collective-permute-done((bf16[80,128]{1,0:T(8,128)(2,1)S(1)}, bf16[80,128]{1,0:T(8,128)(2,1)S(1)}, u32[]{:S(2)}, u32[]{:S(2)}) %collective-permute-start.13) | collective-permute-done | bytes 20512 | tf_op jit(solution)/shard_map/ppermute | solution.py:408
  171.3 2.5 %collective-permute-done.14 = bf16[80,128]{1,0:T(8,128)(2,1)S(1)} collective-permute-done((bf16[80,128]{1,0:T(8,128)(2,1)S(1)}, bf16[80,128]{1,0:T(8,128)(2,1)S(1)}, u32[]{:S(2)}, u32[]{:S(2)}) %collective-permute-start.14) | collective-permute-done | bytes 20512 | tf_op jit(solution)/shard_map/ppermute | solution.py:409
  174.6 4.8 %all-to-all-start.6 = ((bf16[16,80,128]{2,1,0:T(8,128)(2,1)}), bf16[16,80,128]{2,1,0:T(8,128)(2,1)S(1)}, u32[]{:S(2)}, u32[]{:S(2)}) async-start(bf16[16,80,128]{2,1,0:T(8,128)(2,1)} %broadcast_in_dim.2), calls=%async_computation.6 | async-start | bytes 655360 | tf_op jit(solution)/shard_map/all_to_all | solution.py:362
  179.4 1.6 shard_map.97
  181.0 6.1 %all-to-all-done.6.arrived = bf16[16,80,128]{2,1,0:T(8,128)(2,1)S(1)} async-done(((bf16[16,80,128]{2,1,0:T(8,128)(2,1)}), bf16[16,80,128]{2,1,0:T(8,128)(2,1)S(1)}, u32[]{:S(2)}, u32[]{:S(2)}) %all-to-all-start.6) | async-done | bytes 327712 | tf_op jit(solution)/shard_map/all_to_all | solution.py:362
  187.1 5.8 %all-to-all-start.4 = ((bf16[32,64,256]{2,1,0:T(8,128)(2,1)}), bf16[32,64,256]{2,1,0:T(8,128)(2,1)S(1)}, u32[]{:S(2)}, u32[]{:S(2)}) async-start(bf16[32,64,256]{2,1,0:T(8,128)(2,1)} %shard_map.97), calls=%async_computation.4 | async-start | bytes 2097152 | tf_op jit(solution)/shard_map/all_to_all | solution.py:362
  193.8 12.3 %all-to-all-done.4.arrived = bf16[32,64,256]{2,1,0:T(8,128)(2,1)S(1)} async-done(((bf16[32,64,256]{2,1,0:T(8,128)(2,1)}), bf16[32,64,256]{2,1,0:T(8,128)(2,1)S(1)}, u32[]{:S(2)}, u32[]{:S(2)}) %all-to-all-start.4) | async-done | bytes 1048608 | tf_op jit(solution)/shard_map/all_to_all | solution.py:362
  206.1 1.5 shard_map.98
  207.6 1.9 copy.13
  (40 shorter events, 12.9 us)
Async XLA Ops:
  0.6 13.7 %copy-start = (bf16[4,512,64]{1,2,0:T(8,128)(2,1)S(1)}, bf16[4,512,64]{1,2,0:T(8,128)(2,1)}, u32[]{:S(2)}) copy-start(bf16[4,512,64]{1,2,0:T(8,128)(2,1)} %param.10) | copy-start | bytes 786436
  1.4 1.0 copy-start.1
  2.5 0.7 copy-start.2
  5.0 26.5 %all-to-all-start = ((bf16[32,80,256]{2,1,0:T(8,128)(2,1)}), bf16[32,80,256]{2,1,0:T(8,128)(2,1)S(1)}, u32[]{:S(2)}, u32[]{:S(2)}) async-start(bf16[32,80,256]{2,1,0:T(8,128)(2,1)} %shard_map.93), calls=%async_computation | async-start | bytes 2621440 | tf_op jit(solution)/shard_map/all_to_all | solution.py:362
  32.7 47.6 %all-to-all-start.1 = ((bf16[16,64,256]{2,1,0:T(8,128)(2,1)}), bf16[16,64,256]{2,1,0:T(8,128)(2,1)S(1)}, u32[]{:S(2)}, u32[]{:S(2)}) async-start(bf16[16,64,256]{2,1,0:T(8,128)(2,1)} %get-tuple-element.24), calls=%async_computation.1 | async-start | bytes 1048576 | tf_op jit(solution)/shard_map/all_to_all | solution.py:362
  40.3 14.6 %collective-permute-start.2 = (bf16[80,512]{1,0:T(8,128)(2,1)S(1)}, bf16[80,512]{1,0:T(8,128)(2,1)S(1)}, u32[]{:S(2)}, u32[]{:S(2)}) collective-permute-start(bf16[80,512]{1,0:T(8,128)(2,1)S(1)} %get-tuple-element.46), channel_id=1, source_target_pairs={{0,6},{2,0},{4,2},{6,4},{1,7},{3,1},{5,3},{7,5},{8,14},{10,8},{12,... | collective-permute-start | bytes 245768 | tf_op jit(solution)/shard_map/ppermute | solution.py:349
  44.5 21.2 %collective-permute-start.1 = (bf16[80,512]{1,0:T(8,128)(2,1)S(1)}, bf16[80,512]{1,0:T(8,128)(2,1)S(1)}, u32[]{:S(2)}, u32[]{:S(2)}) collective-permute-start(bf16[80,512]{1,0:T(8,128)(2,1)S(1)} %get-tuple-element.46), channel_id=1, source_target_pairs={{0,4},{2,6},{4,0},{6,2},{1,5},{3,7},{5,1},{7,3},{8,12},{10,14},{12... | collective-permute-start | bytes 245768 | tf_op jit(solution)/shard_map/ppermute | solution.py:349
  46.9 18.8 %collective-permute-start = (bf16[80,512]{1,0:T(8,128)(2,1)S(1)}, bf16[80,512]{1,0:T(8,128)(2,1)S(1)}, u32[]{:S(2)}, u32[]{:S(2)}) collective-permute-start(bf16[80,512]{1,0:T(8,128)(2,1)S(1)} %get-tuple-element.46), channel_id=1, source_target_pairs={{0,2},{2,4},{4,6},{6,0},{1,3},{3,5},{5,7},{7,1},{8,10},{10,12},{12... | collective-permute-start | bytes 245768 | tf_op jit(solution)/shard_map/ppermute | solution.py:349
  65.7 7.2 %collective-permute-start.3 = (bf16[4,80,512]{2,1,0:T(8,128)(2,1)S(1)}, bf16[4,80,512]{2,1,0:T(8,128)(2,1)S(1)}, u32[]{:S(2)}, u32[]{:S(2)}) collective-permute-start(bf16[4,80,512]{2,1,0:T(8,128)(2,1)S(1)} %pad_maximum_fusion.own0), channel_id=1, source_target_pairs={{0,16},{1,65},{16,32},{17,81},{32,48},{33,97},{48,0},{49,113},{64,... | collective-permute-start | bytes 983048 | tf_op jit(solution)/shard_map/ppermute | solution.py:357
  66.5 8.7 %collective-permute-start.4 = (bf16[4,80,512]{2,1,0:T(8,128)(2,1)S(1)}, bf16[4,80,512]{2,1,0:T(8,128)(2,1)S(1)}, u32[]{:S(2)}, u32[]{:S(2)}) collective-permute-start(bf16[4,80,512]{2,1,0:T(8,128)(2,1)S(1)} %pad_maximum_fusion.own0), channel_id=1, source_target_pairs={{0,32},{1,129},{16,48},{17,145},{32,0},{33,161},{48,16},{49,177},{... | collective-permute-start | bytes 983048 | tf_op jit(solution)/shard_map/ppermute | solution.py:357
  70.0 8.6 %collective-permute-start.5 = (bf16[4,80,512]{2,1,0:T(8,128)(2,1)S(1)}, bf16[4,80,512]{2,1,0:T(8,128)(2,1)S(1)}, u32[]{:S(2)}, u32[]{:S(2)}) collective-permute-start(bf16[4,80,512]{2,1,0:T(8,128)(2,1)S(1)} %pad_maximum_fusion.own0), channel_id=1, source_target_pairs={{0,48},{1,193},{16,0},{17,209},{32,16},{33,225},{48,32},{49,241},{... | collective-permute-start | bytes 983048 | tf_op jit(solution)/shard_map/ppermute | solution.py:357
  70.0 9.8 %collective-permute-start.6 = (bf16[4,80,512]{2,1,0:T(8,128)(2,1)S(1)}, bf16[4,80,512]{2,1,0:T(8,128)(2,1)S(1)}, u32[]{:S(2)}, u32[]{:S(2)}) collective-permute-start(bf16[4,80,512]{2,1,0:T(8,128)(2,1)S(1)} %pad_maximum_fusion.own0), channel_id=1, source_target_pairs={{0,1},{1,0},{2,3},{3,2},{4,5},{5,4},{6,7},{7,6},{8,9},{9,8},{10,11... | collective-permute-start | bytes 983048 | tf_op jit(solution)/shard_map/ppermute | solution.py:358
  72.9 6.8 %collective-permute-start.7 = (bf16[4,80,512]{2,1,0:T(8,128)(2,1)S(1)}, bf16[4,80,512]{2,1,0:T(8,128)(2,1)S(1)}, u32[]{:S(2)}, u32[]{:S(2)}) collective-permute-start(bf16[4,80,512]{2,1,0:T(8,128)(2,1)S(1)} %collective-permute-done.3.own1), channel_id=1, source_target_pairs={{0,1},{1,0},{2,3},{3,2},{4,5},{5,4},{6,7},{7,6},{8,9},{9,8},{10,11... | collective-permute-start | bytes 983048 | tf_op jit(solution)/shard_map/ppermute | solution.py:358
  75.2 4.6 %collective-permute-start.8 = (bf16[4,80,512]{2,1,0:T(8,128)(2,1)S(1)}, bf16[4,80,512]{2,1,0:T(8,128)(2,1)}, u32[]{:S(2)}, u32[]{:S(2)}) collective-permute-start(bf16[4,80,512]{2,1,0:T(8,128)(2,1)S(1)} %collective-permute-done.4.own2), channel_id=1, source_target_pairs={{0,1},{1,0},{2,3},{3,2},{4,5},{5,4},{6,7},{7,6},{8,9},{9,8},{10,11... | collective-permute-start | bytes 983048 | tf_op jit(solution)/shard_map/ppermute | solution.py:358
  78.6 1.8 collective-permute-start.9
  103.8 4.5 %collective-permute-start.10 = (bf16[16,4,80,128]{3,2,1,0:T(8,128)(2,1)}, bf16[16,4,80,128]{3,2,1,0:T(8,128)(2,1)S(1)}, u32[]{:S(2)}, u32[]{:S(2)}) collective-permute-start(bf16[16,4,80,128]{3,2,1,0:T(8,128)(2,1)} %get-tuple-element.39), channel_id=1, source_target_pairs={{0,1},{1,0},{2,3},{3,2},{4,5},{5,4},{6,7},{7,6},{8,9},{9,8},{10,11... | collective-permute-start | bytes 3932168 | tf_op jit(solution)/shard_map/ppermute | solution.py:400
  103.9 20.9 %all-to-all-start.2 = ((bf16[16,64,256]{2,1,0:T(8,128)(2,1)}), bf16[16,64,256]{2,1,0:T(8,128)(2,1)}, u32[]{:S(2)}, u32[]{:S(2)}) async-start(bf16[16,64,256]{2,1,0:T(8,128)(2,1)} %bitcast.12), calls=%async_computation.2 | async-start | bytes 1048576 | tf_op jit(solution)/shard_map/all_to_all | solution.py:362
  108.3 1.1 copy-start.3
  148.9 25.0 %all-to-all-start.3 = ((bf16[16,64,256]{2,1,0:T(8,128)(2,1)}), bf16[16,64,256]{2,1,0:T(8,128)(2,1)S(1)}, u32[]{:S(2)}, u32[]{:S(2)}) async-start(bf16[16,64,256]{2,1,0:T(8,128)(2,1)} %bitcast.13), calls=%async_computation.3 | async-start | bytes 1048576 | tf_op jit(solution)/shard_map/all_to_all | solution.py:362
  152.6 15.9 %collective-permute-start.13 = (bf16[80,128]{1,0:T(8,128)(2,1)S(1)}, bf16[80,128]{1,0:T(8,128)(2,1)S(1)}, u32[]{:S(2)}, u32[]{:S(2)}) collective-permute-start(bf16[80,128]{1,0:T(8,128)(2,1)S(1)} %get-tuple-element.43), channel_id=1, source_target_pairs={{0,6},{2,0},{4,2},{6,4},{1,7},{3,1},{5,3},{7,5},{8,14},{10,8},{12,... | collective-permute-start | bytes 61448 | tf_op jit(solution)/shard_map/ppermute | solution.py:408
  156.7 13.2 %collective-permute-start.12 = (bf16[80,128]{1,0:T(8,128)(2,1)S(1)}, bf16[80,128]{1,0:T(8,128)(2,1)S(1)}, u32[]{:S(2)}, u32[]{:S(2)}) collective-permute-start(bf16[80,128]{1,0:T(8,128)(2,1)S(1)} %get-tuple-element.44), channel_id=1, source_target_pairs={{0,4},{2,6},{4,0},{6,2},{1,5},{3,7},{5,1},{7,3},{8,12},{10,14},{12... | collective-permute-start | bytes 61448 | tf_op jit(solution)/shard_map/ppermute | solution.py:408
  159.1 10.8 %collective-permute-start.11 = (bf16[80,128]{1,0:T(8,128)(2,1)S(1)}, bf16[80,128]{1,0:T(8,128)(2,1)S(1)}, u32[]{:S(2)}, u32[]{:S(2)}) collective-permute-start(bf16[80,128]{1,0:T(8,128)(2,1)S(1)} %get-tuple-element.42), channel_id=1, source_target_pairs={{0,2},{2,4},{4,6},{6,0},{1,3},{3,5},{5,7},{7,1},{8,10},{10,12},{12... | collective-permute-start | bytes 61448 | tf_op jit(solution)/shard_map/ppermute | solution.py:408
  169.9 3.9 %collective-permute-start.14 = (bf16[80,128]{1,0:T(8,128)(2,1)S(1)}, bf16[80,128]{1,0:T(8,128)(2,1)S(1)}, u32[]{:S(2)}, u32[]{:S(2)}) collective-permute-start(bf16[80,128]{1,0:T(8,128)(2,1)S(1)} %fusion.2), channel_id=1, source_target_pairs={{0,8},{8,0},{1,9},{9,1},{2,10},{10,2},{3,11},{11,3},{4,12},{12,4},... | collective-permute-start | bytes 61448 | tf_op jit(solution)/shard_map/ppermute | solution.py:409
  174.6 12.6 %all-to-all-start.6 = ((bf16[16,80,128]{2,1,0:T(8,128)(2,1)}), bf16[16,80,128]{2,1,0:T(8,128)(2,1)S(1)}, u32[]{:S(2)}, u32[]{:S(2)}) async-start(bf16[16,80,128]{2,1,0:T(8,128)(2,1)} %broadcast_in_dim.2), calls=%async_computation.6 | async-start | bytes 655360 | tf_op jit(solution)/shard_map/all_to_all | solution.py:362
  187.1 19.0 %all-to-all-start.4 = ((bf16[32,64,256]{2,1,0:T(8,128)(2,1)}), bf16[32,64,256]{2,1,0:T(8,128)(2,1)S(1)}, u32[]{:S(2)}, u32[]{:S(2)}) async-start(bf16[32,64,256]{2,1,0:T(8,128)(2,1)} %shard_map.97), calls=%async_computation.4 | async-start | bytes 2097152 | tf_op jit(solution)/shard_map/all_to_all | solution.py:362

commit v3 on v2

v3 whole, which is shorter than its diff:
```python
import jax
import jax.numpy as jnp
from jax import lax
from jax.experimental import pallas as pl
from jax.experimental.pallas import tpu as pltpu
from jax.sharding import Mesh
from jax.sharding import PartitionSpec as P

D = 512
H = 8
DH = 64
SLOT = 256
HIST = 16
EPS = 1e-05
META = 16
TILE = 128
ROWS = 5 * DH
PIECE = ROWS // 4
F32 = jnp.float32
BF16 = jnp.bfloat16
DP = ("y", "x", "zlo")
COL = ("zhi", "core")
VMEM = pl.BlockSpec(memory_space=pltpu.VMEM)
SMEM = pl.BlockSpec(memory_space=pltpu.SMEM)
ANY = pl.BlockSpec(memory_space=pl.ANY)


def params(mib):
    return pltpu.CompilerParams(vmem_limit_bytes=mib * 1024 * 1024)


def cost(flops, moved):
    return pl.CostEstimate(flops=flops, bytes_accessed=moved, transcendentals=0)


def spread_kernel(place, route, lengths, rows, proj, wout, sent, piece):
    along = place[3]
    piece[:DH, :] = proj[along]
    piece[DH:, :] = wout[pl.ds(pl.multiple_of(along * (DH // 4), DH // 4), DH // 4), :]
    sent[...] = jnp.zeros_like(sent)
    for h in range(HIST):
        group = route[0, h]
        sent[group, :DH, :] = rows[h]
        slot = (route[1, h] + 1).astype(F32)
        count = lengths[h].astype(F32)
        sent[group, DH:, : SLOT // 2] = jnp.full((META, SLOT // 2), slot, F32).astype(BF16)
        sent[group, DH:, SLOT // 2 :] = jnp.full((META, SLOT // 2), count, F32).astype(BF16)


def settle_kernel(arrived, shard1, shard2, shard3, rows, meta):
    codes = []
    for group in range(arrived.shape[0]):
        note = arrived[group, DH:, :].astype(F32)[:8]
        code = jnp.max(note[:, : SLOT // 2] * 512.0 + note[:, SLOT // 2 :])
        codes.append(code.astype(jnp.int32))
    for group, code in enumerate(codes):

        @pl.when(code >= 512)
        def _():
            slot = lax.shift_right_logical(code, 9) - 1
            rows[slot] = arrived[group, :DH, :]
            meta[0, slot] = group
            meta[1, slot] = code & 511


def add_kernel(place, mine, came, sum0, sum1, sum2, sum3):
    core = place[1]
    for k, total in enumerate((sum0, sum1, sum2, sum3)):
        ahead = lax.rem(place[3] + k, 4)
        for j in range(4):
            piece = jnp.where(core == 0, 4 * j + ahead, 4 * ahead + j)
            total[j] = (mine[piece].astype(F32) + came[piece].astype(F32)).astype(BF16)


def cross_kernel(place, kept, came1, came2, came3, sum0, sum1, sum2, sum3):
    for k, total in enumerate((sum0, sum1, sum2, sum3)):
        j = lax.rem(place[4] + k, 4)
        part = kept[j].astype(F32)
        for came in (came1, came2, came3):
            part = part + came[j].astype(F32)
        total[...] = part.astype(BF16)


def depth_kernel(place, kept, came1, came2, came3, sum0, sum1, sum2, sum3):
    for k, total in enumerate((sum0, sum1, sum2, sum3)):
        z = lax.rem(place[2] + k, 4)
        part = kept[z].astype(F32)
        for came in (came1, came2, came3):
            part = part + came[z].astype(F32)
        total[...] = part.astype(BF16) if k else part


def last_kernel(kept, came1, came2, came3, total, rounded):
    part = kept[...]
    for came in (came1, came2, came3):
        part = part + came[...].astype(F32)
    total[...] = part
    rounded[...] = part.astype(BF16)


def repeat_kernel(total, came, after, whole):
    summed = (total[...] + came[...].astype(F32)).astype(BF16)
    for group in range(whole.shape[0]):
        whole[group] = summed


def pair_kernel(same, came, after, pair0, pair1, pair2, pair3):
    for k, pair in enumerate((pair0, pair1, pair2, pair3)):
        pair[0] = same[k]
        pair[1] = came[k]


def return_kernel(meta, rows, after, sent):
    sent[...] = jnp.zeros_like(sent)
    for k in range(HIST):
        sent[meta[0, k]] = rows[k]


def collect_kernel(place, route, arrived, pair0, pair1, pair2, pair3, rows, mixed):
    for h in range(HIST):
        rows[h] = arrived[route[0, h]]
    core = place[1]
    for k, pair in enumerate((pair0, pair1, pair2, pair3)):
        for side in range(2):
            owner = 2 * wrap(place[2], k) + (core if side == 0 else 1 - core)
            for i in range(2):
                mixed[2 * owner + i] = pair[side, i]


def tn(a, b):
    return lax.dot_general(a, b, (((0,), (0,)), ((), ())), preferred_element_type=F32)


def nt(a, b):
    return lax.dot_general(a, b, (((1,), (1,)), ((), ())), preferred_element_type=F32)


def nn(a, b):
    return lax.dot_general(a, b, (((1,), (0,)), ((), ())), preferred_element_type=F32)


def silu_parts(half):
    t = jnp.tanh(half)
    up = 1.0 + t
    silu = half * up
    return silu, up + silu * (1.0 - t)


def live_row(meta, col):
    at = lax.broadcasted_iota(jnp.int32, (1, SLOT), 1)
    rows = [(at < meta[1, 2 * col + i]).astype(F32) for i in range(2)]
    return jnp.concatenate(rows, axis=1)


def wrap(position, back):
    return lax.rem(position - back + 4, 4)


def split_chunks(place, chunks, same, cross):
    for k in range(4):
        goal = 2 * lax.rem(place[2] + k, 4)
        same[k] = chunks[goal + place[1]]
        cross[k] = chunks[goal + 1 - place[1]]


def forward_kernel(
    place,
    meta,
    xa,
    own0,
    own1,
    own2,
    own3,
    far0,
    far1,
    far2,
    far3,
    msame,
    mcross,
    win,
    wout,
    xn,
    inv_in,
    slopes,
    proj,
    weights,
    score_slopes,
    out_norm,
    inv_out,
    gated,
    mixed,
    x_s,
):
    tokens = 2 * SLOT
    col = place[0]
    core = place[1]
    for i in range(2):
        x_s[:, i * SLOT : (i + 1) * SLOT] = xa[:, i].reshape(D, SLOT).astype(F32)
    for side, refs, along in ((core, (own0, own1, own2, own3), place[3]), (1 - core, (far0, far1, far2, far3), place[4])):
        for k in range(4):
            piece = wrap(along, k)
            for z in range(4):
                head = 2 * wrap(place[2], z) + side
                at = pl.multiple_of(piece * DH, DH)
                win[head, pl.ds(at, DH), :] = refs[k][z, :DH, :]
                at = pl.multiple_of(head * DH + piece * (DH // 4), DH // 4)
                wout[pl.ds(at, DH // 4), :] = refs[k][z, DH:, :]

    for i in range(tokens // 128):
        lanes = slice(i * 128, (i + 1) * 128)
        x = x_s[:, lanes]
        centred = x - jnp.mean(x, axis=0, keepdims=True)
        inv = lax.rsqrt(jnp.mean(centred * centred, axis=0, keepdims=True) + EPS)
        inv_in[:, lanes] = inv
        xn[:, lanes] = (0.5 * (centred * inv)).astype(BF16)

    live = live_row(meta, col)
    square = (TILE, TILE)
    causal = lax.broadcasted_iota(jnp.int32, square, 0) <= lax.broadcasted_iota(jnp.int32, square, 1)

    def one_head(h):
        silu, slope = silu_parts(nn(win[h], xn[...]))
        slopes[h] = slope.astype(BF16)
        rounded = silu.astype(BF16)
        proj[h] = rounded
        scores = []
        for i in range(2):
            low = i * SLOT
            key = rounded[3 * DH :, low : low + SLOT] * BF16(0.5 * DH**-0.5)
            query = rounded[2 * DH : 3 * DH, low : low + SLOT]
            both = tn(key[:, :TILE], query)
            scores.append((both[:, :TILE], both[:, TILE:], tn(key[:, TILE:], query[:, TILE:])))
        parts = []
        for i in range(2):
            low = i * SLOT
            value = rounded[DH : 2 * DH, low : low + SLOT]
            held = []
            for at, half in enumerate(scores[i]):
                weight, slope = silu_parts(half)
                if at != 1:
                    weight = jnp.where(causal, weight, 0.0)
                    slope = jnp.where(causal, slope, 0.0)
                lanes = slice(at * TILE, (at + 1) * TILE)
                held.append(weight.astype(BF16))
                weights[h, i, :, lanes] = held[at]
                score_slopes[h, i, :, lanes] = slope.astype(BF16)
            first = nn(value[:, :TILE], jnp.concatenate(held[:2], axis=1))
            parts += [first[:, :TILE], first[:, TILE:] + nn(value[:, TILE:], held[2])]
        att = jnp.concatenate(parts, axis=1) * live
        out_norm[pl.ds(pl.multiple_of(h * DH, DH), DH), :] = att
        return att

    def head_step(z, sums):
        for h in (2 * z, 2 * z + 1):
            att = one_head(h)
            sums = (
                sums[0] + jnp.sum(att, axis=0, keepdims=True),
                sums[1] + jnp.sum(att * att, axis=0, keepdims=True),
            )
        return sums

    zero = jnp.zeros((1, tokens), F32)
    totals, squares = lax.fori_loop(0, H // 2, head_step, (zero, zero), unroll=True)
    mean = totals / D
    inv = lax.rsqrt(squares / D - mean * mean + EPS)
    inv_out[...] = inv

    def gate_step(h, carry):
        rows = pl.ds(h * DH, DH)
        normed = (out_norm[rows, :] - mean) * inv
        out_norm[rows, :] = normed
        gated[rows, :] = (normed * proj[h, :DH, :].astype(F32)).astype(BF16)
        return carry

    lax.fori_loop(0, H, gate_step, 0, unroll=4)
    out = (x_s[...] + tn(wout[...], gated[...])).astype(BF16)
    for i in range(2):
        mixed[:, i] = out[:, i * SLOT : (i + 1) * SLOT].reshape(H, DH, SLOT)
    split_chunks(place, mixed, msame, mcross)


def backward_kernel(
    place,
    meta,
    gy_ref,
    win,
    wout,
    xn,
    inv_in,
    slopes,
    proj,
    weights,
    score_slopes,
    out_norm,
    inv_out,
    gated,
    gfeat,
    mine,
    other,
    grad_s,
    gy_s,
    gpre_s,
    sum_s,
    gwo_s,
):
    tokens = 2 * SLOT
    core = place[1]
    for i in range(2):
        gy_s[:, i * SLOT : (i + 1) * SLOT] = gy_ref[i]
    grad_s[...] = nn(wout[...], gy_s[...])
    gwo_s[...] = nt(gated[...], gy_s[...]).astype(BF16)

    def sum_step(h, sums):
        rows = pl.ds(h * DH, DH)
        grad = grad_s[rows, :] * proj[h, :DH, :].astype(F32)
        return (
            sums[0] + jnp.sum(grad, axis=0, keepdims=True),
            sums[1] + jnp.sum(grad * out_norm[rows, :], axis=0, keepdims=True),
        )

    zero = jnp.zeros((1, tokens), F32)
    first, second = lax.fori_loop(0, H, sum_step, (zero, zero), unroll=4)
    first = first / D
    second = second / D
    inv = inv_out[...] * live_row(meta, place[0])

    def store_grad(ref, at, grad_win, grad_wout):
        for part in range(4):
            lanes = slice(part * 128, (part + 1) * 128)
            for c in range(4):
                ref[4 * part + c, at, :DH, :] = grad_win[c * DH : (c + 1) * DH, lanes]
                ref[4 * part + c, at, DH:, :] = grad_wout[c * DH // 4 : (c + 1) * DH // 4, lanes]

    def one_head(h):
        rows = pl.ds(pl.multiple_of(h * DH, DH), DH)
        grad_gated = grad_s[rows, :]
        normed = out_norm[rows, :]
        grad_normo = grad_gated * proj[h, :DH, :].astype(F32)
        grad_att = (inv * (grad_normo - first - normed * second)).astype(BF16)
        grads = ([], [], [])
        for i in range(2):
            low = i * SLOT
            lanes = slice(low, low + SLOT)
            value = proj[h, DH : 2 * DH, lanes]
            query = proj[h, 2 * DH : 3 * DH, lanes] * BF16(0.5 * DH**-0.5)
            key = proj[h, 3 * DH :, lanes] * BF16(0.5 * DH**-0.5)
            grad = grad_att[:, lanes]
            scores = tn(value[:, :TILE], grad) * score_slopes[h, i, :, :SLOT].astype(F32)
            scores = scores.astype(BF16)
            tail = tn(value[:, TILE:], grad[:, TILE:]) * score_slopes[h, i, :, SLOT:].astype(F32)
            tail = tail.astype(BF16)
            grad_query = nn(key[:, :TILE], scores)
            grads[0].append(nt(grad, weights[h, i, :, :SLOT]))
            grads[0].append(nt(grad[:, TILE:], weights[h, i, :, SLOT:]))
            grads[1].append(grad_query[:, :TILE])
            grads[1].append(grad_query[:, TILE:] + nn(key[:, TILE:], tail))
            grads[2].append(nt(query, scores))
            grads[2].append(nt(query[:, TILE:], tail))
        stacked = [grad_gated * normed] + [jnp.concatenate(blocks, axis=1) for blocks in grads]
        grad_pre = (jnp.concatenate(stacked, axis=0) * slopes[h].astype(F32)).astype(BF16)
        gpre_s[h] = grad_pre
        return nt(grad_pre, xn[...]).astype(BF16), gwo_s[rows, :]

    def head_step(z, carry):
        store_grad(mine, z, *one_head(2 * z + core))
        store_grad(other, z, *one_head(2 * z + 1 - core))
        return carry

    lax.fori_loop(0, H // 2, head_step, 0, unroll=True)
    sum_s[...] = tn(win[...].reshape(4 * D, D), gpre_s[...].reshape(4 * D, tokens))
    for i in range(tokens // 128):
        lanes = slice(i * 128, (i + 1) * 128)
        grad = 0.5 * sum_s[:, lanes]
        normed = 2.0 * xn[:, lanes].astype(F32)
        lead = jnp.mean(grad, axis=0, keepdims=True)
        cross = jnp.mean(grad * normed, axis=0, keepdims=True)
        total = gy_s[:, lanes].astype(F32) + inv_in[:, lanes] * (grad - lead - normed * cross)
        here = slice(i % 2 * 128, (i % 2 + 1) * 128)
        gfeat[:, i // 2, :, here] = total.astype(BF16).reshape(H, DH, 128)


def run_forward(place, meta, xa, pieces):
    tokens = 2 * SLOT
    shape = jax.ShapeDtypeStruct
    return pl.pallas_call(
        forward_kernel,
        out_shape=(
            shape((4, 2, DH, SLOT), BF16),
            shape((4, 2, DH, SLOT), BF16),
            shape((H, 4 * DH, D), BF16),
            shape((D, D), BF16),
            shape((D, tokens), BF16),
            shape((1, tokens), F32),
            shape((H, 4 * DH, tokens), BF16),
            shape((H, 4 * DH, tokens), BF16),
            shape((H, 2, TILE, 3 * TILE), BF16),
            shape((H, 2, TILE, 3 * TILE), BF16),
            shape((D, tokens), F32),
            shape((1, tokens), F32),
            shape((D, tokens), BF16),
        ),
        in_specs=[SMEM, SMEM] + [VMEM] * 9,
        out_specs=(VMEM,) * 13,
        scratch_shapes=[pltpu.VMEM((H, 2, DH, SLOT), BF16), pltpu.VMEM((D, tokens), F32)],
        compiler_params=params(28),
        cost_estimate=cost(10**10, 2**24),
    )(place, meta, xa, *pieces)


def run_backward(place, meta, grad_y, saved):
    tokens = 2 * SLOT
    piece = jax.ShapeDtypeStruct((16, 4, PIECE, 128), BF16)
    return pl.pallas_call(
        backward_kernel,
        out_shape=(jax.ShapeDtypeStruct((H, 2, DH, SLOT), BF16), piece, piece),
        in_specs=[SMEM, SMEM] + [VMEM] * 12,
        out_specs=(VMEM,) * 3,
        cost_estimate=cost(12 * 10**9, 2**24),
        scratch_shapes=[
            pltpu.VMEM((D, tokens), F32),
            pltpu.VMEM((D, tokens), BF16),
            pltpu.VMEM((H, 4 * DH, tokens), BF16),
            pltpu.VMEM((D, tokens), F32),
            pltpu.VMEM((D, D), BF16),
        ],
        compiler_params=params(32),
    )(place, meta, grad_y, *saved)


def finish_kernel(arrived, grad_in, grad_out):
    factor = float(HIST * 32 * SLOT) ** -0.5
    for part in range(4):
        lanes = slice(part * 128, (part + 1) * 128)
        for c in range(4):
            block = arrived[4 * part + c].astype(F32) * factor
            grad_in[c, :, lanes] = block[:DH]
            grad_out[c * DH // 4 : (c + 1) * DH // 4, lanes] = block[DH:]


def shift(x, axis, k):
    return lax.ppermute(x, axis, [(i, (i + k) % 4) for i in range(4)])


def trade(x, axis):
    return lax.ppermute(x, axis, [(0, 1), (1, 0)])


def turn(part, k, flip):
    pairs = []
    for y in range(4):
        for x in range(4):
            for core in range(2):
                goal = 4 * y + (x + k) % 4 if core == flip else 4 * ((y + k) % 4) + x
                pairs.append(((4 * y + x) * 2 + core, goal * 2 + core))
    return lax.ppermute(part, ("y", "x", "core"), pairs)


def gather_weights(shards):
    own = [jnp.stack(shards)]
    own += [turn(own[0], k, 0) for k in range(1, 4)]
    return own + [trade(part, "core") for part in own]


def swap(x, axes):
    return lax.all_to_all(x, axes, split_axis=0, concat_axis=0, tiled=True)


def on_device(features, cotangent, lengths, route, w_in, w_out):
    groups = lax.axis_size(DP)
    col = lax.axis_index(COL)
    core = lax.axis_index("core")
    zhi = lax.axis_index("zhi")
    route = route.T
    x = lax.axis_index("x")
    y = lax.axis_index("y")
    along = jnp.where(core == 0, x, y)
    place = jnp.stack([col, core, zhi, along, x + y - along]).astype(jnp.int32)

    sent, piece = pl.pallas_call(
        spread_kernel,
        out_shape=(
            jax.ShapeDtypeStruct((groups, DH + META, SLOT), BF16),
            jax.ShapeDtypeStruct((PIECE, D), BF16),
        ),
        in_specs=[SMEM, SMEM, SMEM, VMEM, VMEM, VMEM],
        out_specs=(VMEM, VMEM),
        compiler_params=params(16),
    )(place, route, lengths, features, w_in.transpose(0, 2, 1), w_out)
    arrived = swap(sent, DP)
    shards = [piece] + [shift(piece, "zhi", k) for k in range(1, 4)]
    rows, meta = pl.pallas_call(
        settle_kernel,
        out_shape=(
            jax.ShapeDtypeStruct((HIST, DH, SLOT), BF16),
            jax.ShapeDtypeStruct((2, HIST), jnp.int32),
        ),
        in_specs=[VMEM, ANY, ANY, ANY],
        out_specs=(VMEM, SMEM),
        compiler_params=params(16),
    )(arrived, *shards[1:])
    pieces = gather_weights(shards)
    xa = swap(rows, COL).reshape(H, 2, DH, SLOT)
    grad_y = lax.dynamic_slice_in_dim(cotangent, 2 * col, 2, 0)
    msame, mcross, *saved = run_forward(place, meta, xa, pieces)
    gfeat, mine, other = run_backward(place, meta, grad_y, saved)
    home = swap(gfeat.reshape(HIST, DH, SLOT), COL)

    def local(kernel, outs, *args):
        return pl.pallas_call(
            kernel,
            out_shape=outs,
            in_specs=[SMEM] + [VMEM] * (len(args) - 1),
            out_specs=(VMEM,) * len(outs),
            compiler_params=params(16),
        )(*args)

    part = jax.ShapeDtypeStruct((4, 4, PIECE, 128), BF16)
    sums = local(add_kernel, (part,) * 4, place, mine, trade(other, "core"))
    came = [turn(sums[k], k, 0) for k in range(1, 4)]
    part = jax.ShapeDtypeStruct((4, PIECE, 128), BF16)
    sums = local(cross_kernel, (part,) * 4, place, sums[0], *came)
    gate1 = sums[1]
    came = [turn(sums[k], k, 1) for k in range(1, 4)]
    part = jax.ShapeDtypeStruct((PIECE, 128), BF16)
    kept = jax.ShapeDtypeStruct((PIECE, 128), F32)
    sums = local(depth_kernel, (kept,) + (part,) * 3, place, sums[0], *came)
    gate2 = sums[1]
    came = [shift(sums[k], "zhi", k) for k in range(1, 4)]
    total, rounded = pl.pallas_call(
        last_kernel,
        out_shape=(kept, part),
        in_specs=[VMEM] * 4,
        out_specs=(VMEM, VMEM),
        compiler_params=params(16),
    )(sums[0], *came)

    def col_pairs(same, cross, after):
        pair = jax.ShapeDtypeStruct((2, 2, DH, SLOT), BF16)
        pairs = pl.pallas_call(
            pair_kernel,
            out_shape=(pair,) * 4,
            in_specs=[VMEM, VMEM, ANY],
            out_specs=(VMEM,) * 4,
            compiler_params=params(16),
        )(same, trade(cross, "core"), after)
        return [pairs[0]] + [shift(pairs[k], "zhi", k) for k in range(1, 4)]

    back = pl.pallas_call(
        return_kernel,
        out_shape=jax.ShapeDtypeStruct((groups, DH, SLOT), BF16),
        in_specs=[SMEM, VMEM, ANY],
        out_specs=VMEM,
        compiler_params=params(16),
    )(meta, home, gate2)
    arrived = swap(back, DP)
    moved = col_pairs(msame, mcross, rounded)
    block = jax.ShapeDtypeStruct((HIST, DH, SLOT), BF16)
    grad_features, mixed = pl.pallas_call(
        collect_kernel,
        out_shape=(block, block),
        in_specs=[SMEM, SMEM] + [VMEM] * 5,
        out_specs=(VMEM, VMEM),
        compiler_params=params(16),
    )(place, route, arrived, *moved)

    whole = pl.pallas_call(
        repeat_kernel,
        out_shape=jax.ShapeDtypeStruct((16, PIECE, 128), BF16),
        in_specs=[VMEM, VMEM, ANY],
        out_specs=VMEM,
        compiler_params=params(16),
    )(total, trade(rounded, "zlo"), arrived)
    whole = swap(whole, ("y", "x"))
    grad_in, grad_out = pl.pallas_call(
        finish_kernel,
        out_shape=(jax.ShapeDtypeStruct((4, DH, D), F32), jax.ShapeDtypeStruct((DH, D), F32)),
        in_specs=[VMEM],
        out_specs=(VMEM, VMEM),
        compiler_params=params(16),
    )(whole)
    return (mixed, grad_features, grad_in.transpose(0, 2, 1), grad_out)


def solution(mesh):
    split = Mesh(mesh.devices.reshape(4, 4, 2, 4, 2), ("y", "x", "zlo", "zhi", "core"))
    in_specs = (P(DP, COL, None), P(DP, None, None), P(DP), P(DP, None), P(None, None, COL), P(COL, None))
    out_specs = (P(DP, COL, None), P(DP, COL, None), P(None, None, COL), P(COL, None))
    return jax.shard_map(
        on_device, mesh=split, in_specs=in_specs, out_specs=out_specs, check_vma=False
    )
```

time: 212 us -> 168 us (0.79); the launches traced: 210 us -> 168 us
  waiting for transfers between devices: 85.9 us -> 54 us
  blocking collectives: 24.1 us -> 0 us
  starting transfers between devices: 57.9 us -> 77.3 us
  Pallas kernels: 30.6 us -> 26.9 us
    all_to_all x6 -> x5, waiting for transfers between devices: 49.3 us -> 2.04 us  [swap(): return lax.all_to_all(x, axes, split_axis=0, concat_axis=0, tiled=True)]
    all_to_all x1 -> x0, blocking collectives: 24.1 us -> none  [swap(): return lax.all_to_all(x, axes, split_axis=0, concat_axis=0, tiled=True)]
    ppermute x15 -> x25, starting transfers between devices: 23.5 us -> 44.1 us  [the longest x9 23.7 us: shift(): return lax.ppermute(x, axis, [(i, (i + k) % 4) for i in range(4)])]
    ppermute x15 -> x25, waiting for transfers between devices: 36.6 us -> 51.9 us  [the longest x9 32.1 us: shift(): return lax.ppermute(x, axis, [(i, (i + k) % 4) for i in range(4)])]
    pallas_call x1, Pallas kernels: 12.6 us -> 8.71 us  [run_backward(): pl.pallas_call(backward_kernel, out_shape=(jax.ShapeDtypeStruct((H, 2, DH...]
    unnamed x10 -> x22, local copies, waits for them, and re-layouts: 5.45 us -> 7.36 us
    all_to_all x6 -> x5, starting transfers between devices: 34.5 us -> 33.2 us  [swap(): return lax.all_to_all(x, axes, split_axis=0, concat_axis=0, tiled=True)]
    pallas_call x3 -> x9, Pallas kernels: 14.2 us -> 14.4 us  [the longest x1 8.07 us: run_forward(): pl.pallas_call(forward_kernel, out_shape=(shape((4, 2, DH, SLOT), BF16),...]
  transfers between devices with their start and end apart: 21 -> 30, of which waited for: 13 -> 16; matrix products, arithmetic and copies ran while one was open for 2% -> 1% of each run, Pallas kernels for 1% -> 3%
where the time goes in v3:
time: 168 us
  starting transfers between devices  77.3 us (46%)
  waiting for transfers between devices  54 us (32%)
  Pallas kernels  26.9 us (16%)
  local copies, waits for them, and re-layouts  8.52 us (5%)
    all_to_all x5, starting transfers between devices, swap(): return lax.all_to_all(x, axes, split_axis=0, concat_axis=0, tiled=True)  33.2 us
    ppermute x9, waiting for transfers between devices, shift(): return lax.ppermute(x, axis, [(i, (i + k) % 4) for i in range(4)])  32.1 us
    ppermute x9, starting transfers between devices, shift(): return lax.ppermute(x, axis, [(i, (i + k) % 4) for i in range(4)])  23.7 us
    ppermute x9, waiting for transfers between devices, turn(): return lax.ppermute(part, ('y', 'x', 'core'), pairs)  16.5 us
    ppermute x9, starting transfers between devices, turn(): return lax.ppermute(part, ('y', 'x', 'core'), pairs)  14.9 us
    pallas_call x1, Pallas kernels, run_backward(): pl.pallas_call(backward_kernel, out_shape=(jax.ShapeDtypeStruct((H, 2, DH...  8.71 us
    pallas_call x1, Pallas kernels, run_forward(): pl.pallas_call(forward_kernel, out_shape=(shape((4, 2, DH, SLOT), BF16),...  8.07 us
    unnamed x22, local copies, waits for them, and re-layouts  7.36 us
  transfers between devices with their start and end apart: 30, of which 16 were waited for; matrix products, arithmetic and copies ran while one was open for 1% of the time, Pallas kernels for 3%

profile of v3, /device:TPU:34, one launch (start us, length us, event | category | flops | bytes accessed | tf_op | source)
XLA Modules:
  0.0 167.6 jit_solution(4461656973006685468)
XLA Ops:
  4.9 1.8 %shard_map.93 = (bf16[32,80,256]{2,1,0:T(8,128)(2,1)}, bf16[80,512]{1,0:T(8,128)(2,1)S(1)}) custom-call(s32[5]{0:T(128)S(1)} %stack.38.place, s32[2,16]{1,0:T(2,128)S(1)} %bitcast.21, s32[16]{0:T(128)S(1)} %copy-done.6, bf16[16,64,256]{2,1,0:T(8,128)(2,1)S(1)} %copy-done.1, bf16[4,64,512]{2,1,0:T(8,128)(2,1)S(1)} %bitcast.19, bf16[64,512]{1,0:T(8,128)(2,1)S(1)} %copy-done.3), custom_call_target="tpu_custom_call" | custom-call | tf_op jit(solution)/shard_map/pallas_call | solution.py:479
  6.7 8.5 %all-to-all-start = ((bf16[32,80,256]{2,1,0:T(8,128)(2,1)}), bf16[32,80,256]{2,1,0:T(8,128)(2,1)S(1)}, u32[]{:S(2)}, u32[]{:S(2)}) async-start(bf16[32,80,256]{2,1,0:T(8,128)(2,1)} %get-tuple-element.46), calls=%async_computation | async-start | bytes 2621440 | tf_op jit(solution)/shard_map/all_to_all | solution.py:465
  15.2 5.5 %collective-permute-start.2 = (bf16[80,512]{1,0:T(8,128)(2,1)S(1)}, bf16[80,512]{1,0:T(8,128)(2,1)S(1)}, u32[]{:S(2)}, u32[]{:S(2)}) collective-permute-start(bf16[80,512]{1,0:T(8,128)(2,1)S(1)} %get-tuple-element.47), channel_id=1, source_target_pairs={{0,6},{2,0},{4,2},{6,4},{1,7},{3,1},{5,3},{7,5},{8,14},{10,8},{12,... | collective-permute-start | bytes 245768 | tf_op jit(solution)/shard_map/ppermute | solution.py:441
  22.1 2.4 %collective-permute-start = (bf16[80,512]{1,0:T(8,128)(2,1)S(1)}, bf16[80,512]{1,0:T(8,128)(2,1)S(1)}, u32[]{:S(2)}, u32[]{:S(2)}) collective-permute-start(bf16[80,512]{1,0:T(8,128)(2,1)S(1)} %get-tuple-element.47), channel_id=1, source_target_pairs={{0,2},{2,4},{4,6},{6,0},{1,3},{3,5},{5,7},{7,1},{8,10},{10,12},{12... | collective-permute-start | bytes 245768 | tf_op jit(solution)/shard_map/ppermute | solution.py:441
  24.5 12.7 %collective-permute-done.2.shard3 = bf16[80,512]{1,0:T(8,128)(2,1)S(1)} collective-permute-done((bf16[80,512]{1,0:T(8,128)(2,1)S(1)}, bf16[80,512]{1,0:T(8,128)(2,1)S(1)}, u32[]{:S(2)}, u32[]{:S(2)}) %collective-permute-start.2) | collective-permute-done | bytes 81952 | tf_op jit(solution)/shard_map/ppermute | solution.py:441
  37.2 4.4 %collective-permute-done.1.shard2 = bf16[80,512]{1,0:T(8,128)(2,1)S(1)} collective-permute-done((bf16[80,512]{1,0:T(8,128)(2,1)S(1)}, bf16[80,512]{1,0:T(8,128)(2,1)S(1)}, u32[]{:S(2)}, u32[]{:S(2)}) %collective-permute-start.1) | collective-permute-done | bytes 81952 | tf_op jit(solution)/shard_map/ppermute | solution.py:441
  42.9 4.0 %all-to-all-start.1 = ((bf16[16,64,256]{2,1,0:T(8,128)(2,1)}), bf16[16,64,256]{2,1,0:T(8,128)(2,1)S(1)}, u32[]{:S(2)}, u32[]{:S(2)}) async-start(bf16[16,64,256]{2,1,0:T(8,128)(2,1)} %get-tuple-element.49), calls=%async_computation.1 | async-start | bytes 1048576 | tf_op jit(solution)/shard_map/all_to_all | solution.py:465
  48.0 2.0 %collective-permute-start.4 = (bf16[4,80,512]{2,1,0:T(8,128)(2,1)S(1)}, bf16[4,80,512]{2,1,0:T(8,128)(2,1)S(1)}, u32[]{:S(2)}, u32[]{:S(2)}) collective-permute-start(bf16[4,80,512]{2,1,0:T(8,128)(2,1)S(1)} %pad_maximum_fusion.own0), channel_id=1, source_target_pairs={{0,32},{1,129},{16,48},{17,145},{32,0},{33,161},{48,16},{49,177},{... | collective-permute-start | bytes 983048 | tf_op jit(solution)/shard_map/ppermute | solution.py:455
  50.0 1.7 %collective-permute-start.3 = (bf16[4,80,512]{2,1,0:T(8,128)(2,1)S(1)}, bf16[4,80,512]{2,1,0:T(8,128)(2,1)S(1)}, u32[]{:S(2)}, u32[]{:S(2)}) collective-permute-start(bf16[4,80,512]{2,1,0:T(8,128)(2,1)S(1)} %pad_maximum_fusion.own0), channel_id=1, source_target_pairs={{0,16},{1,65},{16,32},{17,81},{32,48},{33,97},{48,0},{49,113},{64,... | collective-permute-start | bytes 983048 | tf_op jit(solution)/shard_map/ppermute | solution.py:455
  51.7 2.4 %collective-permute-done.5.own3 = bf16[4,80,512]{2,1,0:T(8,128)(2,1)S(1)} collective-permute-done((bf16[4,80,512]{2,1,0:T(8,128)(2,1)S(1)}, bf16[4,80,512]{2,1,0:T(8,128)(2,1)S(1)}, u32[]{:S(2)}, u32[]{:S(2)}) %collective-permute-start.5) | collective-permute-done | bytes 327712 | tf_op jit(solution)/shard_map/ppermute | solution.py:455
  54.1 3.4 %collective-permute-start.9 = (bf16[4,80,512]{2,1,0:T(8,128)(2,1)S(1)}, bf16[4,80,512]{2,1,0:T(8,128)(2,1)S(1)}, u32[]{:S(2)}, u32[]{:S(2)}) collective-permute-start(bf16[4,80,512]{2,1,0:T(8,128)(2,1)S(1)} %collective-permute-done.5.own3), channel_id=1, source_target_pairs={{0,1},{1,0},{2,3},{3,2},{4,5},{5,4},{6,7},{7,6},{8,9},{9,8},{10,11... | collective-permute-start | bytes 983048 | tf_op jit(solution)/shard_map/ppermute | solution.py:445
  63.0 2.0 %all-to-all-done.1 = bf16[16,64,256]{2,1,0:T(8,128)(2,1)S(1)} async-done(((bf16[16,64,256]{2,1,0:T(8,128)(2,1)}), bf16[16,64,256]{2,1,0:T(8,128)(2,1)S(1)}, u32[]{:S(2)}, u32[]{:S(2)}) %all-to-all-start.1) | async-done | bytes 524320 | tf_op jit(solution)/shard_map/all_to_all | solution.py:465
  66.0 8.1 %shard_map.95 = (bf16[4,2,64,256]{3,2,1,0:T(8,128)(2,1)S(1)}, bf16[4,2,64,256]{3,2,1,0:T(8,128)(2,1)S(1)}, bf16[8,256,512]{2,1,0:T(8,128)(2,1)S(1)}, bf16[512,51...) custom-call(s32[5]{0:T(128)S(1)} %stack.38.place, ...), custom_call_target="tpu_custom_call" | custom-call | flops 10000000000 | bytes 16777216 | tf_op jit(solution)/shard_map/pallas_call | solution.py:385
  74.8 8.7 %shard_map.96 = (bf16[8,2,64,256]{3,2,1,0:T(8,128)(2,1)S(1)}, bf16[16,4,80,128]{3,2,1,0:T(8,128)(2,1)S(1)}, bf16[16,4,80,128]{3,2,1,0:T(8,128)(2,1)}) custom-call(s32[5]{0:T(128)S(1)} %stack.38.place, s32[2,16]{1,0:T(2,128)S(1)} %get-tuple-element.48.meta, bf16[2,512,256]{2,1,0:T(8,128)(2,1)S(1)} %constant_dynamic-slice_fusion.gy_ref, ...), custom_call_target="tpu_custom_call" | custom-call | flops 12000000000 | bytes 16777216 | tf_op jit(solution)/shard_map/pallas_call | solution.py:413
  84.3 4.6 %all-to-all-start.2 = ((bf16[16,64,256]{2,1,0:T(8,128)(2,1)}), bf16[16,64,256]{2,1,0:T(8,128)(2,1)S(1)}, u32[]{:S(2)}, u32[]{:S(2)}) async-start(bf16[16,64,256]{2,1,0:T(8,128)(2,1)} %bitcast.14), calls=%async_computation.2 | async-start | bytes 1048576 | tf_op jit(solution)/shard_map/all_to_all | solution.py:465
  89.8 1.8 %collective-permute-start.11 = (bf16[4,4,80,128]{3,2,1,0:T(8,128)(2,1)S(1)}, bf16[4,4,80,128]{3,2,1,0:T(8,128)(2,1)S(1)}, u32[]{:S(2)}, u32[]{:S(2)}) collective-permute-start(bf16[4,4,80,128]{3,2,1,0:T(8,128)(2,1)S(1)} %get-tuple-element.65), channel_id=1, source_target_pairs={{0,16},{1,65},{16,32},{17,81},{32,48},{33,97},{48,0},{49,113},{64,... | collective-permute-start | bytes 983048 | tf_op jit(solution)/shard_map/ppermute | solution.py:455
  91.7 2.7 %collective-permute-start.12 = (bf16[4,4,80,128]{3,2,1,0:T(8,128)(2,1)S(1)}, bf16[4,4,80,128]{3,2,1,0:T(8,128)(2,1)S(1)}, u32[]{:S(2)}, u32[]{:S(2)}) collective-permute-start(bf16[4,4,80,128]{3,2,1,0:T(8,128)(2,1)S(1)} %get-tuple-element.66), channel_id=1, source_target_pairs={{0,32},{1,129},{16,48},{17,145},{32,0},{33,161},{48,16},{49,177},{... | collective-permute-start | bytes 983048 | tf_op jit(solution)/shard_map/ppermute | solution.py:455
  94.8 2.5 %collective-permute-done.11.came1 = bf16[4,4,80,128]{3,2,1,0:T(8,128)(2,1)S(1)} collective-permute-done((bf16[4,4,80,128]{3,2,1,0:T(8,128)(2,1)S(1)}, bf16[4,4,80,128]{3,2,1,0:T(8,128)(2,1)S(1)}, u32[]{:S(2)}, u32[]{:S(2)}) %collective-permute-start.11) | collective-permute-done | bytes 327712 | tf_op jit(solution)/shard_map/ppermute | solution.py:455
  97.4 3.0 %collective-permute-done.12.came2 = bf16[4,4,80,128]{3,2,1,0:T(8,128)(2,1)S(1)} collective-permute-done((bf16[4,4,80,128]{3,2,1,0:T(8,128)(2,1)S(1)}, bf16[4,4,80,128]{3,2,1,0:T(8,128)(2,1)S(1)}, u32[]{:S(2)}, u32[]{:S(2)}) %collective-permute-start.12) | collective-permute-done | bytes 327712 | tf_op jit(solution)/shard_map/ppermute | solution.py:455
  100.3 3.4 %collective-permute-done.13.came3 = bf16[4,4,80,128]{3,2,1,0:T(8,128)(2,1)S(1)} collective-permute-done((bf16[4,4,80,128]{3,2,1,0:T(8,128)(2,1)S(1)}, bf16[4,4,80,128]{3,2,1,0:T(8,128)(2,1)S(1)}, u32[]{:S(2)}, u32[]{:S(2)}) %collective-permute-start.13) | collective-permute-done | bytes 327712 | tf_op jit(solution)/shard_map/ppermute | solution.py:455
  105.4 2.7 %collective-permute-start.15 = (bf16[4,80,128]{2,1,0:T(8,128)(2,1)S(1)}, bf16[4,80,128]{2,1,0:T(8,128)(2,1)S(1)}, u32[]{:S(2)}, u32[]{:S(2)}) collective-permute-start(bf16[4,80,128]{2,1,0:T(8,128)(2,1)S(1)} %get-tuple-element.70), channel_id=1, source_target_pairs={{0,128},{1,33},{16,144},{17,49},{32,160},{33,1},{48,176},{49,17},{... | collective-permute-start | bytes 245768 | tf_op jit(solution)/shard_map/ppermute | solution.py:455
  113.2 1.7 shard_map.100
  114.9 8.8 %all-to-all-start.3 = ((bf16[32,64,256]{2,1,0:T(8,128)(2,1)}), bf16[32,64,256]{2,1,0:T(8,128)(2,1)S(1)}, u32[]{:S(2)}, u32[]{:S(2)}) async-start(bf16[32,64,256]{2,1,0:T(8,128)(2,1)} %shard_map.100), calls=%async_computation.3 | async-start | bytes 2097152 | tf_op jit(solution)/shard_map/all_to_all | solution.py:465
  123.8 6.0 %collective-permute-start.19 = (bf16[80,128]{1,0:T(8,128)(2,1)S(1)}, bf16[80,128]{1,0:T(8,128)(2,1)S(1)}, u32[]{:S(2)}, u32[]{:S(2)}) collective-permute-start(bf16[80,128]{1,0:T(8,128)(2,1)S(1)} %get-tuple-element.76), channel_id=1, source_target_pairs={{0,4},{2,6},{4,0},{6,2},{1,5},{3,7},{5,1},{7,3},{8,12},{10,14},{12... | collective-permute-start | bytes 61448 | tf_op jit(solution)/shard_map/ppermute | solution.py:441
  130.4 2.4 %collective-permute-start.18 = (bf16[80,128]{1,0:T(8,128)(2,1)S(1)}, bf16[80,128]{1,0:T(8,128)(2,1)S(1)}, u32[]{:S(2)}, u32[]{:S(2)}) collective-permute-start(bf16[80,128]{1,0:T(8,128)(2,1)S(1)} %get-tuple-element.72.after), channel_id=1, source_target_pairs={{0,2},{2,4},{4,6},{6,0},{1,3},{3,5},{5,7},{7,1},{8,10},{10,12},{12... | collective-permute-start | bytes 61448 | tf_op jit(solution)/shard_map/ppermute | solution.py:441
  132.8 6.3 %collective-permute-done.19.came2 = bf16[80,128]{1,0:T(8,128)(2,1)S(1)} collective-permute-done((bf16[80,128]{1,0:T(8,128)(2,1)S(1)}, bf16[80,128]{1,0:T(8,128)(2,1)S(1)}, u32[]{:S(2)}, u32[]{:S(2)}) %collective-permute-start.19) | collective-permute-done | bytes 20512 | tf_op jit(solution)/shard_map/ppermute | solution.py:441
  139.6 3.3 %collective-permute-done.24.came = bf16[80,128]{1,0:T(8,128)(2,1)S(1)} collective-permute-done((bf16[80,128]{1,0:T(8,128)(2,1)S(1)}, bf16[80,128]{1,0:T(8,128)(2,1)S(1)}, u32[]{:S(2)}, u32[]{:S(2)}) %collective-permute-start.24) | collective-permute-done | bytes 20512 | tf_op jit(solution)/shard_map/ppermute | solution.py:445
  143.7 7.2 %all-to-all-start.4 = ((bf16[16,80,128]{2,1,0:T(8,128)(2,1)}), bf16[16,80,128]{2,1,0:T(8,128)(2,1)S(1)}, u32[]{:S(2)}, u32[]{:S(2)}) async-start(bf16[16,80,128]{2,1,0:T(8,128)(2,1)} %shard_map.104), calls=%async_computation.4 | async-start | bytes 655360 | tf_op jit(solution)/shard_map/all_to_all | solution.py:465
  152.1 1.9 %collective-permute-start.22 = (bf16[2,2,64,256]{3,2,1,0:T(8,128)(2,1)S(1)}, bf16[2,2,64,256]{3,2,1,0:T(8,128)(2,1)S(1)}, u32[]{:S(2)}, u32[]{:S(2)}) collective-permute-start(bf16[2,2,64,256]{3,2,1,0:T(8,128)(2,1)S(1)} %get-tuple-element.81), channel_id=1, source_target_pairs={{0,4},{2,6},{4,0},{6,2},{1,5},{3,7},{5,1},{7,3},{8,12},{10,14},{12... | collective-permute-start | bytes 393224 | tf_op jit(solution)/shard_map/ppermute | solution.py:441
  154.1 2.4 %collective-permute-start.23 = (bf16[2,2,64,256]{3,2,1,0:T(8,128)(2,1)S(1)}, bf16[2,2,64,256]{3,2,1,0:T(8,128)(2,1)S(1)}, u32[]{:S(2)}, u32[]{:S(2)}) collective-permute-start(bf16[2,2,64,256]{3,2,1,0:T(8,128)(2,1)S(1)} %get-tuple-element.82), channel_id=1, source_target_pairs={{0,6},{2,0},{4,2},{6,4},{1,7},{3,1},{5,3},{7,5},{8,14},{10,8},{12,... | collective-permute-start | bytes 393224 | tf_op jit(solution)/shard_map/ppermute | solution.py:441
  156.5 5.7 %collective-permute-done.21.pair1 = bf16[2,2,64,256]{3,2,1,0:T(8,128)(2,1)S(1)} collective-permute-done((bf16[2,2,64,256]{3,2,1,0:T(8,128)(2,1)S(1)}, bf16[2,2,64,256]{3,2,1,0:T(8,128)(2,1)S(1)}, u32[]{:S(2)}, u32[]{:S(2)}) %collective-permute-start.21) | collective-permute-done | bytes 131104 | tf_op jit(solution)/shard_map/ppermute | solution.py:441
  162.2 3.0 %collective-permute-done.23.pair3 = bf16[2,2,64,256]{3,2,1,0:T(8,128)(2,1)S(1)} collective-permute-done((bf16[2,2,64,256]{3,2,1,0:T(8,128)(2,1)S(1)}, bf16[2,2,64,256]{3,2,1,0:T(8,128)(2,1)S(1)}, u32[]{:S(2)}, u32[]{:S(2)}) %collective-permute-start.23) | collective-permute-done | bytes 131104 | tf_op jit(solution)/shard_map/ppermute | solution.py:441
  (66 shorter events, 29.7 us)
Async XLA Ops:
  6.7 34.9 %all-to-all-start = ((bf16[32,80,256]{2,1,0:T(8,128)(2,1)}), bf16[32,80,256]{2,1,0:T(8,128)(2,1)S(1)}, u32[]{:S(2)}, u32[]{:S(2)}) async-start(bf16[32,80,256]{2,1,0:T(8,128)(2,1)} %get-tuple-element.46), calls=%async_computation | async-start | bytes 2621440 | tf_op jit(solution)/shard_map/all_to_all | solution.py:465
  15.2 22.0 %collective-permute-start.2 = (bf16[80,512]{1,0:T(8,128)(2,1)S(1)}, bf16[80,512]{1,0:T(8,128)(2,1)S(1)}, u32[]{:S(2)}, u32[]{:S(2)}) collective-permute-start(bf16[80,512]{1,0:T(8,128)(2,1)S(1)} %get-tuple-element.47), channel_id=1, source_target_pairs={{0,6},{2,0},{4,2},{6,4},{1,7},{3,1},{5,3},{7,5},{8,14},{10,8},{12,... | collective-permute-start | bytes 245768 | tf_op jit(solution)/shard_map/ppermute | solution.py:441
  20.7 20.9 %collective-permute-start.1 = (bf16[80,512]{1,0:T(8,128)(2,1)S(1)}, bf16[80,512]{1,0:T(8,128)(2,1)S(1)}, u32[]{:S(2)}, u32[]{:S(2)}) collective-permute-start(bf16[80,512]{1,0:T(8,128)(2,1)S(1)} %get-tuple-element.47), channel_id=1, source_target_pairs={{0,4},{2,6},{4,0},{6,2},{1,5},{3,7},{5,1},{7,3},{8,12},{10,14},{12... | collective-permute-start | bytes 245768 | tf_op jit(solution)/shard_map/ppermute | solution.py:441
  22.1 19.5 %collective-permute-start = (bf16[80,512]{1,0:T(8,128)(2,1)S(1)}, bf16[80,512]{1,0:T(8,128)(2,1)S(1)}, u32[]{:S(2)}, u32[]{:S(2)}) collective-permute-start(bf16[80,512]{1,0:T(8,128)(2,1)S(1)} %get-tuple-element.47), channel_id=1, source_target_pairs={{0,2},{2,4},{4,6},{6,0},{1,3},{3,5},{5,7},{7,1},{8,10},{10,12},{12... | collective-permute-start | bytes 245768 | tf_op jit(solution)/shard_map/ppermute | solution.py:441
  42.9 22.2 %all-to-all-start.1 = ((bf16[16,64,256]{2,1,0:T(8,128)(2,1)}), bf16[16,64,256]{2,1,0:T(8,128)(2,1)S(1)}, u32[]{:S(2)}, u32[]{:S(2)}) async-start(bf16[16,64,256]{2,1,0:T(8,128)(2,1)} %get-tuple-element.49), calls=%async_computation.1 | async-start | bytes 1048576 | tf_op jit(solution)/shard_map/all_to_all | solution.py:465
  46.9 7.2 %collective-permute-start.5 = (bf16[4,80,512]{2,1,0:T(8,128)(2,1)S(1)}, bf16[4,80,512]{2,1,0:T(8,128)(2,1)S(1)}, u32[]{:S(2)}, u32[]{:S(2)}) collective-permute-start(bf16[4,80,512]{2,1,0:T(8,128)(2,1)S(1)} %pad_maximum_fusion.own0), channel_id=1, source_target_pairs={{0,48},{1,193},{16,0},{17,209},{32,16},{33,225},{48,32},{49,241},{... | collective-permute-start | bytes 983048 | tf_op jit(solution)/shard_map/ppermute | solution.py:455
  48.0 10.5 %collective-permute-start.4 = (bf16[4,80,512]{2,1,0:T(8,128)(2,1)S(1)}, bf16[4,80,512]{2,1,0:T(8,128)(2,1)S(1)}, u32[]{:S(2)}, u32[]{:S(2)}) collective-permute-start(bf16[4,80,512]{2,1,0:T(8,128)(2,1)S(1)} %pad_maximum_fusion.own0), channel_id=1, source_target_pairs={{0,32},{1,129},{16,48},{17,145},{32,0},{33,161},{48,16},{49,177},{... | collective-permute-start | bytes 983048 | tf_op jit(solution)/shard_map/ppermute | solution.py:455
  50.0 9.7 %collective-permute-start.3 = (bf16[4,80,512]{2,1,0:T(8,128)(2,1)S(1)}, bf16[4,80,512]{2,1,0:T(8,128)(2,1)S(1)}, u32[]{:S(2)}, u32[]{:S(2)}) collective-permute-start(bf16[4,80,512]{2,1,0:T(8,128)(2,1)S(1)} %pad_maximum_fusion.own0), channel_id=1, source_target_pairs={{0,16},{1,65},{16,32},{17,81},{32,48},{33,97},{48,0},{49,113},{64,... | collective-permute-start | bytes 983048 | tf_op jit(solution)/shard_map/ppermute | solution.py:455
  51.7 10.6 %collective-permute-start.6 = (bf16[4,80,512]{2,1,0:T(8,128)(2,1)S(1)}, bf16[4,80,512]{2,1,0:T(8,128)(2,1)S(1)}, u32[]{:S(2)}, u32[]{:S(2)}) collective-permute-start(bf16[4,80,512]{2,1,0:T(8,128)(2,1)S(1)} %pad_maximum_fusion.own0), channel_id=1, source_target_pairs={{0,1},{1,0},{2,3},{3,2},{4,5},{5,4},{6,7},{7,6},{8,9},{9,8},{10,11... | collective-permute-start | bytes 983048 | tf_op jit(solution)/shard_map/ppermute | solution.py:445
  54.1 8.2 %collective-permute-start.9 = (bf16[4,80,512]{2,1,0:T(8,128)(2,1)S(1)}, bf16[4,80,512]{2,1,0:T(8,128)(2,1)S(1)}, u32[]{:S(2)}, u32[]{:S(2)}) collective-permute-start(bf16[4,80,512]{2,1,0:T(8,128)(2,1)S(1)} %collective-permute-done.5.own3), channel_id=1, source_target_pairs={{0,1},{1,0},{2,3},{3,2},{4,5},{5,4},{6,7},{7,6},{8,9},{9,8},{10,11... | collective-permute-start | bytes 983048 | tf_op jit(solution)/shard_map/ppermute | solution.py:445
  58.5 3.8 %collective-permute-start.8 = (bf16[4,80,512]{2,1,0:T(8,128)(2,1)S(1)}, bf16[4,80,512]{2,1,0:T(8,128)(2,1)S(1)}, u32[]{:S(2)}, u32[]{:S(2)}) collective-permute-start(bf16[4,80,512]{2,1,0:T(8,128)(2,1)S(1)} %collective-permute-done.4.own2), channel_id=1, source_target_pairs={{0,1},{1,0},{2,3},{3,2},{4,5},{5,4},{6,7},{7,6},{8,9},{9,8},{10,11... | collective-permute-start | bytes 983048 | tf_op jit(solution)/shard_map/ppermute | solution.py:445
  59.7 3.3 %collective-permute-start.7 = (bf16[4,80,512]{2,1,0:T(8,128)(2,1)S(1)}, bf16[4,80,512]{2,1,0:T(8,128)(2,1)}, u32[]{:S(2)}, u32[]{:S(2)}) collective-permute-start(bf16[4,80,512]{2,1,0:T(8,128)(2,1)S(1)} %collective-permute-done.3.own1), channel_id=1, source_target_pairs={{0,1},{1,0},{2,3},{3,2},{4,5},{5,4},{6,7},{7,6},{8,9},{9,8},{10,11... | collective-permute-start | bytes 983048 | tf_op jit(solution)/shard_map/ppermute | solution.py:445
  84.3 4.6 %collective-permute-start.10 = (bf16[16,4,80,128]{3,2,1,0:T(8,128)(2,1)}, bf16[16,4,80,128]{3,2,1,0:T(8,128)(2,1)S(1)}, u32[]{:S(2)}, u32[]{:S(2)}) collective-permute-start(bf16[16,4,80,128]{3,2,1,0:T(8,128)(2,1)} %get-tuple-element.63), channel_id=1, source_target_pairs={{0,1},{1,0},{2,3},{3,2},{4,5},{5,4},{6,7},{7,6},{8,9},{9,8},{10,11... | collective-permute-start | bytes 3932168 | tf_op jit(solution)/shard_map/ppermute | solution.py:445
  84.3 28.9 %all-to-all-start.2 = ((bf16[16,64,256]{2,1,0:T(8,128)(2,1)}), bf16[16,64,256]{2,1,0:T(8,128)(2,1)S(1)}, u32[]{:S(2)}, u32[]{:S(2)}) async-start(bf16[16,64,256]{2,1,0:T(8,128)(2,1)} %bitcast.14), calls=%async_computation.2 | async-start | bytes 1048576 | tf_op jit(solution)/shard_map/all_to_all | solution.py:465
  89.8 7.5 %collective-permute-start.11 = (bf16[4,4,80,128]{3,2,1,0:T(8,128)(2,1)S(1)}, bf16[4,4,80,128]{3,2,1,0:T(8,128)(2,1)S(1)}, u32[]{:S(2)}, u32[]{:S(2)}) collective-permute-start(bf16[4,4,80,128]{3,2,1,0:T(8,128)(2,1)S(1)} %get-tuple-element.65), channel_id=1, source_target_pairs={{0,16},{1,65},{16,32},{17,81},{32,48},{33,97},{48,0},{49,113},{64,... | collective-permute-start | bytes 983048 | tf_op jit(solution)/shard_map/ppermute | solution.py:455
  91.7 8.7 %collective-permute-start.12 = (bf16[4,4,80,128]{3,2,1,0:T(8,128)(2,1)S(1)}, bf16[4,4,80,128]{3,2,1,0:T(8,128)(2,1)S(1)}, u32[]{:S(2)}, u32[]{:S(2)}) collective-permute-start(bf16[4,4,80,128]{3,2,1,0:T(8,128)(2,1)S(1)} %get-tuple-element.66), channel_id=1, source_target_pairs={{0,32},{1,129},{16,48},{17,145},{32,0},{33,161},{48,16},{49,177},{... | collective-permute-start | bytes 983048 | tf_op jit(solution)/shard_map/ppermute | solution.py:455
  94.4 9.4 %collective-permute-start.13 = (bf16[4,4,80,128]{3,2,1,0:T(8,128)(2,1)S(1)}, bf16[4,4,80,128]{3,2,1,0:T(8,128)(2,1)S(1)}, u32[]{:S(2)}, u32[]{:S(2)}) collective-permute-start(bf16[4,4,80,128]{3,2,1,0:T(8,128)(2,1)S(1)} %get-tuple-element.67), channel_id=1, source_target_pairs={{0,48},{1,193},{16,0},{17,209},{32,16},{33,225},{48,32},{49,241},{... | collective-permute-start | bytes 983048 | tf_op jit(solution)/shard_map/ppermute | solution.py:455
  104.5 5.7 %collective-permute-start.14 = (bf16[4,80,128]{2,1,0:T(8,128)(2,1)S(1)}, bf16[4,80,128]{2,1,0:T(8,128)(2,1)S(1)}, u32[]{:S(2)}, u32[]{:S(2)}) collective-permute-start(bf16[4,80,128]{2,1,0:T(8,128)(2,1)S(1)} %get-tuple-element.69), channel_id=1, source_target_pairs={{0,64},{1,17},{16,80},{17,33},{32,96},{33,49},{48,112},{49,1},{64,... | collective-permute-start | bytes 245768 | tf_op jit(solution)/shard_map/ppermute | solution.py:455
  105.4 6.0 %collective-permute-start.15 = (bf16[4,80,128]{2,1,0:T(8,128)(2,1)S(1)}, bf16[4,80,128]{2,1,0:T(8,128)(2,1)S(1)}, u32[]{:S(2)}, u32[]{:S(2)}) collective-permute-start(bf16[4,80,128]{2,1,0:T(8,128)(2,1)S(1)} %get-tuple-element.70), channel_id=1, source_target_pairs={{0,128},{1,33},{16,144},{17,49},{32,160},{33,1},{48,176},{49,17},{... | collective-permute-start | bytes 245768 | tf_op jit(solution)/shard_map/ppermute | solution.py:455
  108.2 4.4 %collective-permute-start.16 = (bf16[4,80,128]{2,1,0:T(8,128)(2,1)S(1)}, bf16[4,80,128]{2,1,0:T(8,128)(2,1)S(1)}, u32[]{:S(2)}, u32[]{:S(2)}) collective-permute-start(bf16[4,80,128]{2,1,0:T(8,128)(2,1)S(1)} %get-tuple-element.71), channel_id=1, source_target_pairs={{0,192},{1,49},{16,208},{17,1},{32,224},{33,17},{48,240},{49,33},{... | collective-permute-start | bytes 245768 | tf_op jit(solution)/shard_map/ppermute | solution.py:455
  113.2 10.5 %copy-start.10 = (bf16[4,2,64,256]{3,2,1,0:T(8,128)(2,1)S(1)}, bf16[4,2,64,256]{3,2,1,0:T(8,128)(2,1)}, u32[]{:S(2)}) copy-start(bf16[4,2,64,256]{3,2,1,0:T(8,128)(2,1)} %copy-done.9) | copy-start | bytes 786436
  114.9 28.1 %all-to-all-start.3 = ((bf16[32,64,256]{2,1,0:T(8,128)(2,1)}), bf16[32,64,256]{2,1,0:T(8,128)(2,1)S(1)}, u32[]{:S(2)}, u32[]{:S(2)}) async-start(bf16[32,64,256]{2,1,0:T(8,128)(2,1)} %shard_map.100), calls=%async_computation.3 | async-start | bytes 2097152 | tf_op jit(solution)/shard_map/all_to_all | solution.py:465
  123.7 41.4 %copy-start.5 = (s32[16,2]{0,1:T(2,128)S(1)}, s32[16,2]{0,1:T(2,128)}, u32[]{:S(2)}) copy-start(s32[16,2]{0,1:T(2,128)} %param.9) | copy-start | bytes 388
  123.7 27.3 %collective-permute-start.17 = (bf16[4,2,64,256]{3,2,1,0:T(8,128)(2,1)S(1)}, bf16[4,2,64,256]{3,2,1,0:T(8,128)(2,1)S(1)}, u32[]{:S(2)}, u32[]{:S(2)}) collective-permute-start(bf16[4,2,64,256]{3,2,1,0:T(8,128)(2,1)S(1)} %copy-done.10), channel_id=1, source_target_pairs={{0,1},{1,0},{2,3},{3,2},{4,5},{5,4},{6,7},{7,6},{8,9},{9,8},{10,11... | collective-permute-start | bytes 786440 | tf_op jit(solution)/shard_map/ppermute | solution.py:445
  123.8 15.3 %collective-permute-start.19 = (bf16[80,128]{1,0:T(8,128)(2,1)S(1)}, bf16[80,128]{1,0:T(8,128)(2,1)S(1)}, u32[]{:S(2)}, u32[]{:S(2)}) collective-permute-start(bf16[80,128]{1,0:T(8,128)(2,1)S(1)} %get-tuple-element.76), channel_id=1, source_target_pairs={{0,4},{2,6},{4,0},{6,2},{1,5},{3,7},{5,1},{7,3},{8,12},{10,14},{12... | collective-permute-start | bytes 61448 | tf_op jit(solution)/shard_map/ppermute | solution.py:441
  129.8 9.3 %collective-permute-start.20 = (bf16[80,128]{1,0:T(8,128)(2,1)S(1)}, bf16[80,128]{1,0:T(8,128)(2,1)S(1)}, u32[]{:S(2)}, u32[]{:S(2)}) collective-permute-start(bf16[80,128]{1,0:T(8,128)(2,1)S(1)} %get-tuple-element.77), channel_id=1, source_target_pairs={{0,6},{2,0},{4,2},{6,4},{1,7},{3,1},{5,3},{7,5},{8,14},{10,8},{12,... | collective-permute-start | bytes 61448 | tf_op jit(solution)/shard_map/ppermute | solution.py:441
  130.4 8.7 %collective-permute-start.18 = (bf16[80,128]{1,0:T(8,128)(2,1)S(1)}, bf16[80,128]{1,0:T(8,128)(2,1)S(1)}, u32[]{:S(2)}, u32[]{:S(2)}) collective-permute-start(bf16[80,128]{1,0:T(8,128)(2,1)S(1)} %get-tuple-element.72.after), channel_id=1, source_target_pairs={{0,2},{2,4},{4,6},{6,0},{1,3},{3,5},{5,7},{7,1},{8,10},{10,12},{12... | collective-permute-start | bytes 61448 | tf_op jit(solution)/shard_map/ppermute | solution.py:441
  139.1 3.9 %collective-permute-start.24 = (bf16[80,128]{1,0:T(8,128)(2,1)S(1)}, bf16[80,128]{1,0:T(8,128)(2,1)S(1)}, u32[]{:S(2)}, u32[]{:S(2)}) collective-permute-start(bf16[80,128]{1,0:T(8,128)(2,1)S(1)} %get-tuple-element.78.after), channel_id=1, source_target_pairs={{0,8},{8,0},{1,9},{9,1},{2,10},{10,2},{3,11},{11,3},{4,12},{12,4},... | collective-permute-start | bytes 61448 | tf_op jit(solution)/shard_map/ppermute | solution.py:445
  143.7 23.0 %all-to-all-start.4 = ((bf16[16,80,128]{2,1,0:T(8,128)(2,1)}), bf16[16,80,128]{2,1,0:T(8,128)(2,1)S(1)}, u32[]{:S(2)}, u32[]{:S(2)}) async-start(bf16[16,80,128]{2,1,0:T(8,128)(2,1)} %shard_map.104), calls=%async_computation.4 | async-start | bytes 655360 | tf_op jit(solution)/shard_map/all_to_all | solution.py:465
  151.0 11.1 %collective-permute-start.21 = (bf16[2,2,64,256]{3,2,1,0:T(8,128)(2,1)S(1)}, bf16[2,2,64,256]{3,2,1,0:T(8,128)(2,1)S(1)}, u32[]{:S(2)}, u32[]{:S(2)}) collective-permute-start(bf16[2,2,64,256]{3,2,1,0:T(8,128)(2,1)S(1)} %get-tuple-element.80), channel_id=1, source_target_pairs={{0,2},{2,4},{4,6},{6,0},{1,3},{3,5},{5,7},{7,1},{8,10},{10,12},{12... | collective-permute-start | bytes 393224 | tf_op jit(solution)/shard_map/ppermute | solution.py:441
  152.1 10.0 %collective-permute-start.22 = (bf16[2,2,64,256]{3,2,1,0:T(8,128)(2,1)S(1)}, bf16[2,2,64,256]{3,2,1,0:T(8,128)(2,1)S(1)}, u32[]{:S(2)}, u32[]{:S(2)}) collective-permute-start(bf16[2,2,64,256]{3,2,1,0:T(8,128)(2,1)S(1)} %get-tuple-element.81), channel_id=1, source_target_pairs={{0,4},{2,6},{4,0},{6,2},{1,5},{3,7},{5,1},{7,3},{8,12},{10,14},{12... | collective-permute-start | bytes 393224 | tf_op jit(solution)/shard_map/ppermute | solution.py:441
  154.1 11.0 %collective-permute-start.23 = (bf16[2,2,64,256]{3,2,1,0:T(8,128)(2,1)S(1)}, bf16[2,2,64,256]{3,2,1,0:T(8,128)(2,1)S(1)}, u32[]{:S(2)}, u32[]{:S(2)}) collective-permute-start(bf16[2,2,64,256]{3,2,1,0:T(8,128)(2,1)S(1)} %get-tuple-element.82), channel_id=1, source_target_pairs={{0,6},{2,0},{4,2},{6,4},{1,7},{3,1},{5,3},{7,5},{8,14},{10,8},{12,... | collective-permute-start | bytes 393224 | tf_op jit(solution)/shard_map/ppermute | solution.py:441
  (9 other events, 7.4 us)

commit v4 on v3

--- a/solution.py
+++ b/solution.py
@@ -33,32 +33,42 @@
     return pl.CostEstimate(flops=flops, bytes_accessed=moved, transcendentals=0)
 
 
-def spread_kernel(place, route, lengths, rows, proj, wout, sent, piece):
+def spread_kernel(place, route, lengths, rows, proj, wout, sent, piece, rows_s, sems):
     along = place[3]
-    piece[:DH, :] = proj[along]
-    piece[DH:, :] = wout[pl.ds(pl.multiple_of(along * (DH // 4), DH // 4), DH // 4), :]
+    wrows = pl.ds(pl.multiple_of(along * (DH // 4), DH // 4), DH // 4)
+    copies = (
+        pltpu.make_async_copy(proj.at[along], piece.at[pl.ds(0, DH)], sems.at[0]),
+        pltpu.make_async_copy(wout.at[wrows], piece.at[pl.ds(DH, DH // 4)], sems.at[1]),
+        pltpu.make_async_copy(rows, rows_s, sems.at[2]),
+    )
+    for copy in copies:
+        copy.start()
     sent[...] = jnp.zeros_like(sent)
+    for copy in copies:
+        copy.wait()
     for h in range(HIST):
         group = route[0, h]
-        sent[group, :DH, :] = rows[h]
+        sent[group, :DH, :] = rows_s[h, :, :TILE]
+        sent[group, DH : 2 * DH, :] = rows_s[h, :, TILE:]
         slot = (route[1, h] + 1).astype(F32)
         count = lengths[h].astype(F32)
-        sent[group, DH:, : SLOT // 2] = jnp.full((META, SLOT // 2), slot, F32).astype(BF16)
-        sent[group, DH:, SLOT // 2 :] = jnp.full((META, SLOT // 2), count, F32).astype(BF16)
+        note = jnp.concatenate([jnp.full((8, TILE), slot, F32), jnp.full((8, TILE), count, F32)], axis=0)
+        sent[group, 2 * DH :, :] = note.astype(BF16)
 
 
 def settle_kernel(arrived, shard1, shard2, shard3, rows, meta):
     codes = []
     for group in range(arrived.shape[0]):
-        note = arrived[group, DH:, :].astype(F32)[:8]
-        code = jnp.max(note[:, : SLOT // 2] * 512.0 + note[:, SLOT // 2 :])
+        note = arrived[group, 2 * DH :, :].astype(F32)
+        code = jnp.max(note[:8] * 512.0 + note[8:])
         codes.append(code.astype(jnp.int32))
     for group, code in enumerate(codes):
 
         @pl.when(code >= 512)
         def _():
             slot = lax.shift_right_logical(code, 9) - 1
-            rows[slot] = arrived[group, :DH, :]
+            rows[slot, :, :TILE] = arrived[group, :DH, :]
+            rows[slot, :, TILE:] = arrived[group, DH : 2 * DH, :]
             meta[0, slot] = group
             meta[1, slot] = code & 511
 
@@ -402,7 +412,7 @@
         in_specs=[SMEM, SMEM] + [VMEM] * 9,
         out_specs=(VMEM,) * 13,
         scratch_shapes=[pltpu.VMEM((H, 2, DH, SLOT), BF16), pltpu.VMEM((D, tokens), F32)],
-        compiler_params=params(28),
+        compiler_params=params(10),
         cost_estimate=cost(10**10, 2**24),
     )(place, meta, xa, *pieces)
 
@@ -423,7 +433,7 @@
             pltpu.VMEM((D, tokens), F32),
             pltpu.VMEM((D, D), BF16),
         ],
-        compiler_params=params(32),
+        compiler_params=params(14),
     )(place, meta, grad_y, *saved)
 
 
@@ -479,12 +489,13 @@
     sent, piece = pl.pallas_call(
         spread_kernel,
         out_shape=(
-            jax.ShapeDtypeStruct((groups, DH + META, SLOT), BF16),
+            jax.ShapeDtypeStruct((groups, 2 * DH + META, TILE), BF16),
             jax.ShapeDtypeStruct((PIECE, D), BF16),
         ),
-        in_specs=[SMEM, SMEM, SMEM, VMEM, VMEM, VMEM],
+        in_specs=[SMEM, SMEM, SMEM, ANY, ANY, ANY],
         out_specs=(VMEM, VMEM),
-        compiler_params=params(16),
+        scratch_shapes=[pltpu.VMEM((HIST, DH, SLOT), BF16), pltpu.SemaphoreType.DMA((3,))],
+        compiler_params=params(60),
     )(place, route, lengths, features, w_in.transpose(0, 2, 1), w_out)
     arrived = swap(sent, DP)
     shards = [piece] + [shift(piece, "zhi", k) for k in range(1, 4)]
@@ -496,7 +507,7 @@
         ),
         in_specs=[VMEM, ANY, ANY, ANY],
         out_specs=(VMEM, SMEM),
-        compiler_params=params(16),
+        compiler_params=params(6),
     )(arrived, *shards[1:])
     pieces = gather_weights(shards)
     xa = swap(rows, COL).reshape(H, 2, DH, SLOT)
@@ -511,7 +522,7 @@
             out_shape=outs,
             in_specs=[SMEM] + [VMEM] * (len(args) - 1),
             out_specs=(VMEM,) * len(outs),
-            compiler_params=params(16),
+            compiler_params=params(6),
         )(*args)
 
     part = jax.ShapeDtypeStruct((4, 4, PIECE, 128), BF16)
@@ -531,7 +542,7 @@
         out_shape=(kept, part),
         in_specs=[VMEM] * 4,
         out_specs=(VMEM, VMEM),
-        compiler_params=params(16),
+        compiler_params=params(6),
     )(sums[0], *came)
 
     def col_pairs(same, cross, after):
@@ -541,7 +552,7 @@
             out_shape=(pair,) * 4,
             in_specs=[VMEM, VMEM, ANY],
             out_specs=(VMEM,) * 4,
-            compiler_params=params(16),
+            compiler_params=params(6),
         )(same, trade(cross, "core"), after)
         return [pairs[0]] + [shift(pairs[k], "zhi", k) for k in range(1, 4)]
 
@@ -550,7 +561,7 @@
         out_shape=jax.ShapeDtypeStruct((groups, DH, SLOT), BF16),
         in_specs=[SMEM, VMEM, ANY],
         out_specs=VMEM,
-        compiler_params=params(16),
+        compiler_params=params(6),
     )(meta, home, gate2)
     arrived = swap(back, DP)
     moved = col_pairs(msame, mcross, rounded)
@@ -560,7 +571,7 @@
         out_shape=(block, block),
         in_specs=[SMEM, SMEM] + [VMEM] * 5,
         out_specs=(VMEM, VMEM),
-        compiler_params=params(16),
+        compiler_params=params(6),
     )(place, route, arrived, *moved)
 
     whole = pl.pallas_call(
@@ -568,7 +579,7 @@
         out_shape=jax.ShapeDtypeStruct((16, PIECE, 128), BF16),
         in_specs=[VMEM, VMEM, ANY],
         out_specs=VMEM,
-        compiler_params=params(16),
+        compiler_params=params(6),
     )(total, trade(rounded, "zlo"), arrived)
     whole = swap(whole, ("y", "x"))
     grad_in, grad_out = pl.pallas_call(
@@ -576,7 +587,7 @@
         out_shape=(jax.ShapeDtypeStruct((4, DH, D), F32), jax.ShapeDtypeStruct((DH, D), F32)),
         in_specs=[VMEM],
         out_specs=(VMEM, VMEM),
-        compiler_params=params(16),
+        compiler_params=params(6),
     )(whole)
     return (mixed, grad_features, grad_in.transpose(0, 2, 1), grad_out)
 

time: 168 us -> 165 us (0.982)
  local copies, waits for them, and re-layouts: 8.52 us -> 4.96 us
    unnamed x22 -> x16, local copies, waits for them, and re-layouts: 7.36 us -> 3.2 us
where the time goes in v4:
time: 165 us; the launch traced here: 164 us
  starting transfers between devices  77.5 us (47%)
  waiting for transfers between devices  52.6 us (32%)
  Pallas kernels  28.3 us (17%)
  local copies, waits for them, and re-layouts  4.96 us (3%)
    all_to_all x5, starting transfers between devices, swap(): return lax.all_to_all(x, axes, split_axis=0, concat_axis=0, tiled=True)  33.3 us
    ppermute x9, waiting for transfers between devices, shift(): return lax.ppermute(x, axis, [(i, (i + k) % 4) for i in range(4)])  30.7 us
    ppermute x9, starting transfers between devices, shift(): return lax.ppermute(x, axis, [(i, (i + k) % 4) for i in range(4)])  23.7 us
    ppermute x9, waiting for transfers between devices, turn(): return lax.ppermute(part, ('y', 'x', 'core'), pairs)  16.5 us
    ppermute x9, starting transfers between devices, turn(): return lax.ppermute(part, ('y', 'x', 'core'), pairs)  14.9 us
    pallas_call x1, Pallas kernels, run_backward(): pl.pallas_call(backward_kernel, out_shape=(jax.ShapeDtypeStruct((H, 2, DH...  8.7 us
    pallas_call x1, Pallas kernels, run_forward(): pl.pallas_call(forward_kernel, out_shape=(shape((4, 2, DH, SLOT), BF16),...  8.17 us
    ppermute x7, starting transfers between devices, trade(): return lax.ppermute(x, axis, [(0, 1), (1, 0)])  5.51 us
  transfers between devices with their start and end apart: 30, of which 16 were waited for; matrix products, arithmetic and copies ran while one was open for 1% of the time, Pallas kernels for 3%

profile of v4, /device:TPU:34, one launch (start us, length us, event | category | flops | bytes accessed | tf_op | source)
XLA Modules:
  0.0 164.2 jit_solution(2639159402931021634)
XLA Ops:
  1.3 3.0 %shard_map.93 = (bf16[32,144,128]{2,1,0:T(8,128)(2,1)}, bf16[80,512]{1,0:T(8,128)(2,1)}) custom-call(s32[5]{0:T(128)} %stack.38.place, s32[2,16]{1,0:T(2,128)} %bitcast.19, s32[16]{0:T(128)} %lengths.1, bf16[16,64,256]{2,1,0:T(8,128)(2,1)} %rows.1, bf16[4,64,512]{2,1,0:T(8,128)(2,1)} %bitcast.21, bf16[64,512]{1,0:T(8,128)(2,1)} %wout.1), custom_call_target="tpu_custom_call" | custom-call | tf_op jit(solution)/shard_map/pallas_call | solution.py:489
  4.4 8.7 %all-to-all-start = ((bf16[32,144,128]{2,1,0:T(8,128)(2,1)}), bf16[32,144,128]{2,1,0:T(8,128)(2,1)S(1)}, u32[]{:S(2)}, u32[]{:S(2)}) async-start(bf16[32,144,128]{2,1,0:T(8,128)(2,1)} %get-tuple-element.46), calls=%async_computation | async-start | bytes 2359296 | tf_op jit(solution)/shard_map/all_to_all | solution.py:475
  13.0 5.5 %collective-permute-start.2 = (bf16[80,512]{1,0:T(8,128)(2,1)S(1)}, bf16[80,512]{1,0:T(8,128)(2,1)S(1)}, u32[]{:S(2)}, u32[]{:S(2)}) collective-permute-start(bf16[80,512]{1,0:T(8,128)(2,1)S(1)} %copy-done.7), channel_id=1, source_target_pairs={{0,6},{2,0},{4,2},{6,4},{1,7},{3,1},{5,3},{7,5},{8,14},{10,8},{12,... | collective-permute-start | bytes 245768 | tf_op jit(solution)/shard_map/ppermute | solution.py:451
  20.0 2.4 %collective-permute-start = (bf16[80,512]{1,0:T(8,128)(2,1)S(1)}, bf16[80,512]{1,0:T(8,128)(2,1)S(1)}, u32[]{:S(2)}, u32[]{:S(2)}) collective-permute-start(bf16[80,512]{1,0:T(8,128)(2,1)S(1)} %copy-done.7), channel_id=1, source_target_pairs={{0,2},{2,4},{4,6},{6,0},{1,3},{3,5},{5,7},{7,1},{8,10},{10,12},{12... | collective-permute-start | bytes 245768 | tf_op jit(solution)/shard_map/ppermute | solution.py:451
  22.3 11.3 %collective-permute-done.2.shard3 = bf16[80,512]{1,0:T(8,128)(2,1)S(1)} collective-permute-done((bf16[80,512]{1,0:T(8,128)(2,1)S(1)}, bf16[80,512]{1,0:T(8,128)(2,1)S(1)}, u32[]{:S(2)}, u32[]{:S(2)}) %collective-permute-start.2) | collective-permute-done | bytes 81952 | tf_op jit(solution)/shard_map/ppermute | solution.py:451
  33.6 4.4 %collective-permute-done.1.shard2 = bf16[80,512]{1,0:T(8,128)(2,1)S(1)} collective-permute-done((bf16[80,512]{1,0:T(8,128)(2,1)S(1)}, bf16[80,512]{1,0:T(8,128)(2,1)S(1)}, u32[]{:S(2)}, u32[]{:S(2)}) %collective-permute-start.1) | collective-permute-done | bytes 81952 | tf_op jit(solution)/shard_map/ppermute | solution.py:451
  39.3 4.0 %all-to-all-start.1 = ((bf16[16,64,256]{2,1,0:T(8,128)(2,1)}), bf16[16,64,256]{2,1,0:T(8,128)(2,1)S(1)}, u32[]{:S(2)}, u32[]{:S(2)}) async-start(bf16[16,64,256]{2,1,0:T(8,128)(2,1)} %get-tuple-element.49), calls=%async_computation.1 | async-start | bytes 1048576 | tf_op jit(solution)/shard_map/all_to_all | solution.py:475
  44.4 2.0 %collective-permute-start.4 = (bf16[4,80,512]{2,1,0:T(8,128)(2,1)S(1)}, bf16[4,80,512]{2,1,0:T(8,128)(2,1)S(1)}, u32[]{:S(2)}, u32[]{:S(2)}) collective-permute-start(bf16[4,80,512]{2,1,0:T(8,128)(2,1)S(1)} %pad_maximum_fusion.own0), channel_id=1, source_target_pairs={{0,32},{1,129},{16,48},{17,145},{32,0},{33,161},{48,16},{49,177},{... | collective-permute-start | bytes 983048 | tf_op jit(solution)/shard_map/ppermute | solution.py:465
  46.4 1.7 %collective-permute-start.3 = (bf16[4,80,512]{2,1,0:T(8,128)(2,1)S(1)}, bf16[4,80,512]{2,1,0:T(8,128)(2,1)S(1)}, u32[]{:S(2)}, u32[]{:S(2)}) collective-permute-start(bf16[4,80,512]{2,1,0:T(8,128)(2,1)S(1)} %pad_maximum_fusion.own0), channel_id=1, source_target_pairs={{0,16},{1,65},{16,32},{17,81},{32,48},{33,97},{48,0},{49,113},{64,... | collective-permute-start | bytes 983048 | tf_op jit(solution)/shard_map/ppermute | solution.py:465
  48.1 2.4 %collective-permute-done.5.own3 = bf16[4,80,512]{2,1,0:T(8,128)(2,1)S(1)} collective-permute-done((bf16[4,80,512]{2,1,0:T(8,128)(2,1)S(1)}, bf16[4,80,512]{2,1,0:T(8,128)(2,1)S(1)}, u32[]{:S(2)}, u32[]{:S(2)}) %collective-permute-start.5) | collective-permute-done | bytes 327712 | tf_op jit(solution)/shard_map/ppermute | solution.py:465
  50.5 3.4 %collective-permute-start.9 = (bf16[4,80,512]{2,1,0:T(8,128)(2,1)S(1)}, bf16[4,80,512]{2,1,0:T(8,128)(2,1)S(1)}, u32[]{:S(2)}, u32[]{:S(2)}) collective-permute-start(bf16[4,80,512]{2,1,0:T(8,128)(2,1)S(1)} %collective-permute-done.5.own3), channel_id=1, source_target_pairs={{0,1},{1,0},{2,3},{3,2},{4,5},{5,4},{6,7},{7,6},{8,9},{9,8},{10,11... | collective-permute-start | bytes 983048 | tf_op jit(solution)/shard_map/ppermute | solution.py:455
  59.4 2.0 %all-to-all-done.1 = bf16[16,64,256]{2,1,0:T(8,128)(2,1)S(1)} async-done(((bf16[16,64,256]{2,1,0:T(8,128)(2,1)}), bf16[16,64,256]{2,1,0:T(8,128)(2,1)S(1)}, u32[]{:S(2)}, u32[]{:S(2)}) %all-to-all-start.1) | async-done | bytes 524320 | tf_op jit(solution)/shard_map/all_to_all | solution.py:475
  62.5 8.2 %shard_map.95 = (bf16[4,2,64,256]{3,2,1,0:T(8,128)(2,1)S(1)}, bf16[4,2,64,256]{3,2,1,0:T(8,128)(2,1)S(1)}, bf16[8,256,512]{2,1,0:T(8,128)(2,1)S(1)}, bf16[512,51...) custom-call(s32[5]{0:T(128)S(1)} %copy-done.1, ...), custom_call_target="tpu_custom_call" | custom-call | flops 10000000000 | bytes 16777216 | tf_op jit(solution)/shard_map/pallas_call | solution.py:395
  71.3 8.7 %shard_map.96 = (bf16[8,2,64,256]{3,2,1,0:T(8,128)(2,1)S(1)}, bf16[16,4,80,128]{3,2,1,0:T(8,128)(2,1)S(1)}, bf16[16,4,80,128]{3,2,1,0:T(8,128)(2,1)}) custom-call(s32[5]{0:T(128)S(1)} %copy-done.1, s32[2,16]{1,0:T(2,128)S(1)} %get-tuple-element.48.meta, bf16[2,512,256]{2,1,0:T(8,128)(2,1)S(1)} %constant_dynamic-slice_fusion.gy_ref, ...), custom_call_target="tpu_custom_call" | custom-call | flops 12000000000 | bytes 16777216 | tf_op jit(solution)/shard_map/pallas_call | solution.py:423
  80.8 4.6 %all-to-all-start.2 = ((bf16[16,64,256]{2,1,0:T(8,128)(2,1)}), bf16[16,64,256]{2,1,0:T(8,128)(2,1)S(1)}, u32[]{:S(2)}, u32[]{:S(2)}) async-start(bf16[16,64,256]{2,1,0:T(8,128)(2,1)} %bitcast.14), calls=%async_computation.2 | async-start | bytes 1048576 | tf_op jit(solution)/shard_map/all_to_all | solution.py:475
  86.4 1.8 %collective-permute-start.11 = (bf16[4,4,80,128]{3,2,1,0:T(8,128)(2,1)S(1)}, bf16[4,4,80,128]{3,2,1,0:T(8,128)(2,1)S(1)}, u32[]{:S(2)}, u32[]{:S(2)}) collective-permute-start(bf16[4,4,80,128]{3,2,1,0:T(8,128)(2,1)S(1)} %get-tuple-element.65), channel_id=1, source_target_pairs={{0,16},{1,65},{16,32},{17,81},{32,48},{33,97},{48,0},{49,113},{64,... | collective-permute-start | bytes 983048 | tf_op jit(solution)/shard_map/ppermute | solution.py:465
  88.2 2.7 %collective-permute-start.12 = (bf16[4,4,80,128]{3,2,1,0:T(8,128)(2,1)S(1)}, bf16[4,4,80,128]{3,2,1,0:T(8,128)(2,1)S(1)}, u32[]{:S(2)}, u32[]{:S(2)}) collective-permute-start(bf16[4,4,80,128]{3,2,1,0:T(8,128)(2,1)S(1)} %get-tuple-element.66), channel_id=1, source_target_pairs={{0,32},{1,129},{16,48},{17,145},{32,0},{33,161},{48,16},{49,177},{... | collective-permute-start | bytes 983048 | tf_op jit(solution)/shard_map/ppermute | solution.py:465
  91.4 2.5 %collective-permute-done.11.came1 = bf16[4,4,80,128]{3,2,1,0:T(8,128)(2,1)S(1)} collective-permute-done((bf16[4,4,80,128]{3,2,1,0:T(8,128)(2,1)S(1)}, bf16[4,4,80,128]{3,2,1,0:T(8,128)(2,1)S(1)}, u32[]{:S(2)}, u32[]{:S(2)}) %collective-permute-start.11) | collective-permute-done | bytes 327712 | tf_op jit(solution)/shard_map/ppermute | solution.py:465
  93.9 3.0 %collective-permute-done.12.came2 = bf16[4,4,80,128]{3,2,1,0:T(8,128)(2,1)S(1)} collective-permute-done((bf16[4,4,80,128]{3,2,1,0:T(8,128)(2,1)S(1)}, bf16[4,4,80,128]{3,2,1,0:T(8,128)(2,1)S(1)}, u32[]{:S(2)}, u32[]{:S(2)}) %collective-permute-start.12) | collective-permute-done | bytes 327712 | tf_op jit(solution)/shard_map/ppermute | solution.py:465
  96.8 3.4 %collective-permute-done.13.came3 = bf16[4,4,80,128]{3,2,1,0:T(8,128)(2,1)S(1)} collective-permute-done((bf16[4,4,80,128]{3,2,1,0:T(8,128)(2,1)S(1)}, bf16[4,4,80,128]{3,2,1,0:T(8,128)(2,1)S(1)}, u32[]{:S(2)}, u32[]{:S(2)}) %collective-permute-start.13) | collective-permute-done | bytes 327712 | tf_op jit(solution)/shard_map/ppermute | solution.py:465
  102.0 2.7 %collective-permute-start.15 = (bf16[4,80,128]{2,1,0:T(8,128)(2,1)S(1)}, bf16[4,80,128]{2,1,0:T(8,128)(2,1)S(1)}, u32[]{:S(2)}, u32[]{:S(2)}) collective-permute-start(bf16[4,80,128]{2,1,0:T(8,128)(2,1)S(1)} %get-tuple-element.70), channel_id=1, source_target_pairs={{0,128},{1,33},{16,144},{17,49},{32,160},{33,1},{48,176},{49,17},{... | collective-permute-start | bytes 245768 | tf_op jit(solution)/shard_map/ppermute | solution.py:465
  109.8 1.6 %shard_map.100 = bf16[32,64,256]{2,1,0:T(8,128)(2,1)} custom-call(s32[2,16]{1,0:T(2,128)S(1)} %get-tuple-element.48.meta, bf16[16,64,256]{2,1,0:T(8,128)(2,1)S(1)} %all-to-all-done.2.rows, bf16[80,128]{1,0:T(8,128)(2,1)S(1)} %get-tuple-element.72.after), custom_call_target="tpu_custom_call" | custom-call | tf_op jit(solution)/shard_map/pallas_call | solution.py:559
  111.4 8.8 %all-to-all-start.3 = ((bf16[32,64,256]{2,1,0:T(8,128)(2,1)}), bf16[32,64,256]{2,1,0:T(8,128)(2,1)S(1)}, u32[]{:S(2)}, u32[]{:S(2)}) async-start(bf16[32,64,256]{2,1,0:T(8,128)(2,1)} %shard_map.100), calls=%async_computation.3 | async-start | bytes 2097152 | tf_op jit(solution)/shard_map/all_to_all | solution.py:475
  120.3 6.0 %collective-permute-start.19 = (bf16[80,128]{1,0:T(8,128)(2,1)S(1)}, bf16[80,128]{1,0:T(8,128)(2,1)S(1)}, u32[]{:S(2)}, u32[]{:S(2)}) collective-permute-start(bf16[80,128]{1,0:T(8,128)(2,1)S(1)} %get-tuple-element.76), channel_id=1, source_target_pairs={{0,4},{2,6},{4,0},{6,2},{1,5},{3,7},{5,1},{7,3},{8,12},{10,14},{12... | collective-permute-start | bytes 61448 | tf_op jit(solution)/shard_map/ppermute | solution.py:451
  126.9 2.4 %collective-permute-start.18 = (bf16[80,128]{1,0:T(8,128)(2,1)S(1)}, bf16[80,128]{1,0:T(8,128)(2,1)S(1)}, u32[]{:S(2)}, u32[]{:S(2)}) collective-permute-start(bf16[80,128]{1,0:T(8,128)(2,1)S(1)} %get-tuple-element.72.after), channel_id=1, source_target_pairs={{0,2},{2,4},{4,6},{6,0},{1,3},{3,5},{5,7},{7,1},{8,10},{10,12},{12... | collective-permute-start | bytes 61448 | tf_op jit(solution)/shard_map/ppermute | solution.py:451
  129.3 6.4 %collective-permute-done.19.came2 = bf16[80,128]{1,0:T(8,128)(2,1)S(1)} collective-permute-done((bf16[80,128]{1,0:T(8,128)(2,1)S(1)}, bf16[80,128]{1,0:T(8,128)(2,1)S(1)}, u32[]{:S(2)}, u32[]{:S(2)}) %collective-permute-start.19) | collective-permute-done | bytes 20512 | tf_op jit(solution)/shard_map/ppermute | solution.py:451
  136.2 3.4 %collective-permute-done.24.came = bf16[80,128]{1,0:T(8,128)(2,1)S(1)} collective-permute-done((bf16[80,128]{1,0:T(8,128)(2,1)S(1)}, bf16[80,128]{1,0:T(8,128)(2,1)S(1)}, u32[]{:S(2)}, u32[]{:S(2)}) %collective-permute-start.24) | collective-permute-done | bytes 20512 | tf_op jit(solution)/shard_map/ppermute | solution.py:455
  140.3 7.2 %all-to-all-start.4 = ((bf16[16,80,128]{2,1,0:T(8,128)(2,1)}), bf16[16,80,128]{2,1,0:T(8,128)(2,1)S(1)}, u32[]{:S(2)}, u32[]{:S(2)}) async-start(bf16[16,80,128]{2,1,0:T(8,128)(2,1)} %shard_map.104), calls=%async_computation.4 | async-start | bytes 655360 | tf_op jit(solution)/shard_map/all_to_all | solution.py:475
  148.6 2.0 %collective-permute-start.22 = (bf16[2,2,64,256]{3,2,1,0:T(8,128)(2,1)S(1)}, bf16[2,2,64,256]{3,2,1,0:T(8,128)(2,1)S(1)}, u32[]{:S(2)}, u32[]{:S(2)}) collective-permute-start(bf16[2,2,64,256]{3,2,1,0:T(8,128)(2,1)S(1)} %get-tuple-element.81), channel_id=1, source_target_pairs={{0,4},{2,6},{4,0},{6,2},{1,5},{3,7},{5,1},{7,3},{8,12},{10,14},{12... | collective-permute-start | bytes 393224 | tf_op jit(solution)/shard_map/ppermute | solution.py:451
  150.6 2.4 %collective-permute-start.23 = (bf16[2,2,64,256]{3,2,1,0:T(8,128)(2,1)S(1)}, bf16[2,2,64,256]{3,2,1,0:T(8,128)(2,1)S(1)}, u32[]{:S(2)}, u32[]{:S(2)}) collective-permute-start(bf16[2,2,64,256]{3,2,1,0:T(8,128)(2,1)S(1)} %get-tuple-element.82), channel_id=1, source_target_pairs={{0,6},{2,0},{4,2},{6,4},{1,7},{3,1},{5,3},{7,5},{8,14},{10,8},{12,... | collective-permute-start | bytes 393224 | tf_op jit(solution)/shard_map/ppermute | solution.py:451
  153.0 5.8 %collective-permute-done.21.pair1 = bf16[2,2,64,256]{3,2,1,0:T(8,128)(2,1)S(1)} collective-permute-done((bf16[2,2,64,256]{3,2,1,0:T(8,128)(2,1)S(1)}, bf16[2,2,64,256]{3,2,1,0:T(8,128)(2,1)S(1)}, u32[]{:S(2)}, u32[]{:S(2)}) %collective-permute-start.21) | collective-permute-done | bytes 131104 | tf_op jit(solution)/shard_map/ppermute | solution.py:451
  158.8 2.9 %collective-permute-done.23.pair3 = bf16[2,2,64,256]{3,2,1,0:T(8,128)(2,1)S(1)} collective-permute-done((bf16[2,2,64,256]{3,2,1,0:T(8,128)(2,1)S(1)}, bf16[2,2,64,256]{3,2,1,0:T(8,128)(2,1)S(1)}, u32[]{:S(2)}, u32[]{:S(2)}) %collective-permute-start.23) | collective-permute-done | bytes 131104 | tf_op jit(solution)/shard_map/ppermute | solution.py:451
  (60 shorter events, 26.1 us)
Async XLA Ops:
  4.4 33.6 %all-to-all-start = ((bf16[32,144,128]{2,1,0:T(8,128)(2,1)}), bf16[32,144,128]{2,1,0:T(8,128)(2,1)S(1)}, u32[]{:S(2)}, u32[]{:S(2)}) async-start(bf16[32,144,128]{2,1,0:T(8,128)(2,1)} %get-tuple-element.46), calls=%async_computation | async-start | bytes 2359296 | tf_op jit(solution)/shard_map/all_to_all | solution.py:475
  13.0 20.6 %collective-permute-start.2 = (bf16[80,512]{1,0:T(8,128)(2,1)S(1)}, bf16[80,512]{1,0:T(8,128)(2,1)S(1)}, u32[]{:S(2)}, u32[]{:S(2)}) collective-permute-start(bf16[80,512]{1,0:T(8,128)(2,1)S(1)} %copy-done.7), channel_id=1, source_target_pairs={{0,6},{2,0},{4,2},{6,4},{1,7},{3,1},{5,3},{7,5},{8,14},{10,8},{12,... | collective-permute-start | bytes 245768 | tf_op jit(solution)/shard_map/ppermute | solution.py:451
  18.5 19.5 %collective-permute-start.1 = (bf16[80,512]{1,0:T(8,128)(2,1)S(1)}, bf16[80,512]{1,0:T(8,128)(2,1)S(1)}, u32[]{:S(2)}, u32[]{:S(2)}) collective-permute-start(bf16[80,512]{1,0:T(8,128)(2,1)S(1)} %copy-done.7), channel_id=1, source_target_pairs={{0,4},{2,6},{4,0},{6,2},{1,5},{3,7},{5,1},{7,3},{8,12},{10,14},{12... | collective-permute-start | bytes 245768 | tf_op jit(solution)/shard_map/ppermute | solution.py:451
  20.0 18.0 %collective-permute-start = (bf16[80,512]{1,0:T(8,128)(2,1)S(1)}, bf16[80,512]{1,0:T(8,128)(2,1)S(1)}, u32[]{:S(2)}, u32[]{:S(2)}) collective-permute-start(bf16[80,512]{1,0:T(8,128)(2,1)S(1)} %copy-done.7), channel_id=1, source_target_pairs={{0,2},{2,4},{4,6},{6,0},{1,3},{3,5},{5,7},{7,1},{8,10},{10,12},{12... | collective-permute-start | bytes 245768 | tf_op jit(solution)/shard_map/ppermute | solution.py:451
  39.3 22.2 %copy-start.1 = (s32[5]{0:T(128)S(1)}, s32[5]{0:T(128)}, u32[]{:S(2)}) copy-start(s32[5]{0:T(128)} %stack.38.place) | copy-start | bytes 64
  39.3 22.2 %all-to-all-start.1 = ((bf16[16,64,256]{2,1,0:T(8,128)(2,1)}), bf16[16,64,256]{2,1,0:T(8,128)(2,1)S(1)}, u32[]{:S(2)}, u32[]{:S(2)}) async-start(bf16[16,64,256]{2,1,0:T(8,128)(2,1)} %get-tuple-element.49), calls=%async_computation.1 | async-start | bytes 1048576 | tf_op jit(solution)/shard_map/all_to_all | solution.py:475
  43.3 7.2 %collective-permute-start.5 = (bf16[4,80,512]{2,1,0:T(8,128)(2,1)S(1)}, bf16[4,80,512]{2,1,0:T(8,128)(2,1)S(1)}, u32[]{:S(2)}, u32[]{:S(2)}) collective-permute-start(bf16[4,80,512]{2,1,0:T(8,128)(2,1)S(1)} %pad_maximum_fusion.own0), channel_id=1, source_target_pairs={{0,48},{1,193},{16,0},{17,209},{32,16},{33,225},{48,32},{49,241},{... | collective-permute-start | bytes 983048 | tf_op jit(solution)/shard_map/ppermute | solution.py:465
  44.4 10.5 %collective-permute-start.4 = (bf16[4,80,512]{2,1,0:T(8,128)(2,1)S(1)}, bf16[4,80,512]{2,1,0:T(8,128)(2,1)S(1)}, u32[]{:S(2)}, u32[]{:S(2)}) collective-permute-start(bf16[4,80,512]{2,1,0:T(8,128)(2,1)S(1)} %pad_maximum_fusion.own0), channel_id=1, source_target_pairs={{0,32},{1,129},{16,48},{17,145},{32,0},{33,161},{48,16},{49,177},{... | collective-permute-start | bytes 983048 | tf_op jit(solution)/shard_map/ppermute | solution.py:465
  46.4 9.7 %collective-permute-start.3 = (bf16[4,80,512]{2,1,0:T(8,128)(2,1)S(1)}, bf16[4,80,512]{2,1,0:T(8,128)(2,1)S(1)}, u32[]{:S(2)}, u32[]{:S(2)}) collective-permute-start(bf16[4,80,512]{2,1,0:T(8,128)(2,1)S(1)} %pad_maximum_fusion.own0), channel_id=1, source_target_pairs={{0,16},{1,65},{16,32},{17,81},{32,48},{33,97},{48,0},{49,113},{64,... | collective-permute-start | bytes 983048 | tf_op jit(solution)/shard_map/ppermute | solution.py:465
  48.1 10.6 %collective-permute-start.6 = (bf16[4,80,512]{2,1,0:T(8,128)(2,1)S(1)}, bf16[4,80,512]{2,1,0:T(8,128)(2,1)S(1)}, u32[]{:S(2)}, u32[]{:S(2)}) collective-permute-start(bf16[4,80,512]{2,1,0:T(8,128)(2,1)S(1)} %pad_maximum_fusion.own0), channel_id=1, source_target_pairs={{0,1},{1,0},{2,3},{3,2},{4,5},{5,4},{6,7},{7,6},{8,9},{9,8},{10,11... | collective-permute-start | bytes 983048 | tf_op jit(solution)/shard_map/ppermute | solution.py:455
  50.5 8.2 %collective-permute-start.9 = (bf16[4,80,512]{2,1,0:T(8,128)(2,1)S(1)}, bf16[4,80,512]{2,1,0:T(8,128)(2,1)S(1)}, u32[]{:S(2)}, u32[]{:S(2)}) collective-permute-start(bf16[4,80,512]{2,1,0:T(8,128)(2,1)S(1)} %collective-permute-done.5.own3), channel_id=1, source_target_pairs={{0,1},{1,0},{2,3},{3,2},{4,5},{5,4},{6,7},{7,6},{8,9},{9,8},{10,11... | collective-permute-start | bytes 983048 | tf_op jit(solution)/shard_map/ppermute | solution.py:455
  54.9 4.5 %collective-permute-start.8 = (bf16[4,80,512]{2,1,0:T(8,128)(2,1)S(1)}, bf16[4,80,512]{2,1,0:T(8,128)(2,1)}, u32[]{:S(2)}, u32[]{:S(2)}) collective-permute-start(bf16[4,80,512]{2,1,0:T(8,128)(2,1)S(1)} %collective-permute-done.4.own2), channel_id=1, source_target_pairs={{0,1},{1,0},{2,3},{3,2},{4,5},{5,4},{6,7},{7,6},{8,9},{9,8},{10,11... | collective-permute-start | bytes 983048 | tf_op jit(solution)/shard_map/ppermute | solution.py:455
  56.1 3.3 %collective-permute-start.7 = (bf16[4,80,512]{2,1,0:T(8,128)(2,1)S(1)}, bf16[4,80,512]{2,1,0:T(8,128)(2,1)}, u32[]{:S(2)}, u32[]{:S(2)}) collective-permute-start(bf16[4,80,512]{2,1,0:T(8,128)(2,1)S(1)} %collective-permute-done.3.own1), channel_id=1, source_target_pairs={{0,1},{1,0},{2,3},{3,2},{4,5},{5,4},{6,7},{7,6},{8,9},{9,8},{10,11... | collective-permute-start | bytes 983048 | tf_op jit(solution)/shard_map/ppermute | solution.py:455
  80.8 4.6 %collective-permute-start.10 = (bf16[16,4,80,128]{3,2,1,0:T(8,128)(2,1)}, bf16[16,4,80,128]{3,2,1,0:T(8,128)(2,1)S(1)}, u32[]{:S(2)}, u32[]{:S(2)}) collective-permute-start(bf16[16,4,80,128]{3,2,1,0:T(8,128)(2,1)} %get-tuple-element.63), channel_id=1, source_target_pairs={{0,1},{1,0},{2,3},{3,2},{4,5},{5,4},{6,7},{7,6},{8,9},{9,8},{10,11... | collective-permute-start | bytes 3932168 | tf_op jit(solution)/shard_map/ppermute | solution.py:455
  80.8 28.9 %all-to-all-start.2 = ((bf16[16,64,256]{2,1,0:T(8,128)(2,1)}), bf16[16,64,256]{2,1,0:T(8,128)(2,1)S(1)}, u32[]{:S(2)}, u32[]{:S(2)}) async-start(bf16[16,64,256]{2,1,0:T(8,128)(2,1)} %bitcast.14), calls=%async_computation.2 | async-start | bytes 1048576 | tf_op jit(solution)/shard_map/all_to_all | solution.py:475
  86.4 7.5 %collective-permute-start.11 = (bf16[4,4,80,128]{3,2,1,0:T(8,128)(2,1)S(1)}, bf16[4,4,80,128]{3,2,1,0:T(8,128)(2,1)S(1)}, u32[]{:S(2)}, u32[]{:S(2)}) collective-permute-start(bf16[4,4,80,128]{3,2,1,0:T(8,128)(2,1)S(1)} %get-tuple-element.65), channel_id=1, source_target_pairs={{0,16},{1,65},{16,32},{17,81},{32,48},{33,97},{48,0},{49,113},{64,... | collective-permute-start | bytes 983048 | tf_op jit(solution)/shard_map/ppermute | solution.py:465
  88.2 8.7 %collective-permute-start.12 = (bf16[4,4,80,128]{3,2,1,0:T(8,128)(2,1)S(1)}, bf16[4,4,80,128]{3,2,1,0:T(8,128)(2,1)S(1)}, u32[]{:S(2)}, u32[]{:S(2)}) collective-permute-start(bf16[4,4,80,128]{3,2,1,0:T(8,128)(2,1)S(1)} %get-tuple-element.66), channel_id=1, source_target_pairs={{0,32},{1,129},{16,48},{17,145},{32,0},{33,161},{48,16},{49,177},{... | collective-permute-start | bytes 983048 | tf_op jit(solution)/shard_map/ppermute | solution.py:465
  90.9 9.3 %collective-permute-start.13 = (bf16[4,4,80,128]{3,2,1,0:T(8,128)(2,1)S(1)}, bf16[4,4,80,128]{3,2,1,0:T(8,128)(2,1)S(1)}, u32[]{:S(2)}, u32[]{:S(2)}) collective-permute-start(bf16[4,4,80,128]{3,2,1,0:T(8,128)(2,1)S(1)} %get-tuple-element.67), channel_id=1, source_target_pairs={{0,48},{1,193},{16,0},{17,209},{32,16},{33,225},{48,32},{49,241},{... | collective-permute-start | bytes 983048 | tf_op jit(solution)/shard_map/ppermute | solution.py:465
  101.0 5.7 %collective-permute-start.14 = (bf16[4,80,128]{2,1,0:T(8,128)(2,1)S(1)}, bf16[4,80,128]{2,1,0:T(8,128)(2,1)S(1)}, u32[]{:S(2)}, u32[]{:S(2)}) collective-permute-start(bf16[4,80,128]{2,1,0:T(8,128)(2,1)S(1)} %get-tuple-element.69), channel_id=1, source_target_pairs={{0,64},{1,17},{16,80},{17,33},{32,96},{33,49},{48,112},{49,1},{64,... | collective-permute-start | bytes 245768 | tf_op jit(solution)/shard_map/ppermute | solution.py:465
  102.0 6.0 %collective-permute-start.15 = (bf16[4,80,128]{2,1,0:T(8,128)(2,1)S(1)}, bf16[4,80,128]{2,1,0:T(8,128)(2,1)S(1)}, u32[]{:S(2)}, u32[]{:S(2)}) collective-permute-start(bf16[4,80,128]{2,1,0:T(8,128)(2,1)S(1)} %get-tuple-element.70), channel_id=1, source_target_pairs={{0,128},{1,33},{16,144},{17,49},{32,160},{33,1},{48,176},{49,17},{... | collective-permute-start | bytes 245768 | tf_op jit(solution)/shard_map/ppermute | solution.py:465
  104.7 4.4 %collective-permute-start.16 = (bf16[4,80,128]{2,1,0:T(8,128)(2,1)S(1)}, bf16[4,80,128]{2,1,0:T(8,128)(2,1)S(1)}, u32[]{:S(2)}, u32[]{:S(2)}) collective-permute-start(bf16[4,80,128]{2,1,0:T(8,128)(2,1)S(1)} %get-tuple-element.71), channel_id=1, source_target_pairs={{0,192},{1,49},{16,208},{17,1},{32,224},{33,17},{48,240},{49,33},{... | collective-permute-start | bytes 245768 | tf_op jit(solution)/shard_map/ppermute | solution.py:465
  111.4 28.1 %all-to-all-start.3 = ((bf16[32,64,256]{2,1,0:T(8,128)(2,1)}), bf16[32,64,256]{2,1,0:T(8,128)(2,1)S(1)}, u32[]{:S(2)}, u32[]{:S(2)}) async-start(bf16[32,64,256]{2,1,0:T(8,128)(2,1)} %shard_map.100), calls=%async_computation.3 | async-start | bytes 2097152 | tf_op jit(solution)/shard_map/all_to_all | solution.py:475
  120.2 41.5 %copy-start.2 = (s32[16,2]{0,1:T(2,128)S(1)}, s32[16,2]{0,1:T(2,128)}, u32[]{:S(2)}) copy-start(s32[16,2]{0,1:T(2,128)} %param.9) | copy-start | bytes 388
  120.2 27.3 %collective-permute-start.17 = (bf16[4,2,64,256]{3,2,1,0:T(8,128)(2,1)S(1)}, bf16[4,2,64,256]{3,2,1,0:T(8,128)(2,1)S(1)}, u32[]{:S(2)}, u32[]{:S(2)}) collective-permute-start(bf16[4,2,64,256]{3,2,1,0:T(8,128)(2,1)S(1)} %copy-done.6), channel_id=1, source_target_pairs={{0,1},{1,0},{2,3},{3,2},{4,5},{5,4},{6,7},{7,6},{8,9},{9,8},{10,11... | collective-permute-start | bytes 786440 | tf_op jit(solution)/shard_map/ppermute | solution.py:455
  120.3 15.3 %collective-permute-start.19 = (bf16[80,128]{1,0:T(8,128)(2,1)S(1)}, bf16[80,128]{1,0:T(8,128)(2,1)S(1)}, u32[]{:S(2)}, u32[]{:S(2)}) collective-permute-start(bf16[80,128]{1,0:T(8,128)(2,1)S(1)} %get-tuple-element.76), channel_id=1, source_target_pairs={{0,4},{2,6},{4,0},{6,2},{1,5},{3,7},{5,1},{7,3},{8,12},{10,14},{12... | collective-permute-start | bytes 61448 | tf_op jit(solution)/shard_map/ppermute | solution.py:451
  126.3 9.3 %collective-permute-start.20 = (bf16[80,128]{1,0:T(8,128)(2,1)S(1)}, bf16[80,128]{1,0:T(8,128)(2,1)S(1)}, u32[]{:S(2)}, u32[]{:S(2)}) collective-permute-start(bf16[80,128]{1,0:T(8,128)(2,1)S(1)} %get-tuple-element.77), channel_id=1, source_target_pairs={{0,6},{2,0},{4,2},{6,4},{1,7},{3,1},{5,3},{7,5},{8,14},{10,8},{12,... | collective-permute-start | bytes 61448 | tf_op jit(solution)/shard_map/ppermute | solution.py:451
  126.9 8.7 %collective-permute-start.18 = (bf16[80,128]{1,0:T(8,128)(2,1)S(1)}, bf16[80,128]{1,0:T(8,128)(2,1)S(1)}, u32[]{:S(2)}, u32[]{:S(2)}) collective-permute-start(bf16[80,128]{1,0:T(8,128)(2,1)S(1)} %get-tuple-element.72.after), channel_id=1, source_target_pairs={{0,2},{2,4},{4,6},{6,0},{1,3},{3,5},{5,7},{7,1},{8,10},{10,12},{12... | collective-permute-start | bytes 61448 | tf_op jit(solution)/shard_map/ppermute | solution.py:451
  135.7 3.9 %collective-permute-start.24 = (bf16[80,128]{1,0:T(8,128)(2,1)S(1)}, bf16[80,128]{1,0:T(8,128)(2,1)S(1)}, u32[]{:S(2)}, u32[]{:S(2)}) collective-permute-start(bf16[80,128]{1,0:T(8,128)(2,1)S(1)} %get-tuple-element.78.after), channel_id=1, source_target_pairs={{0,8},{8,0},{1,9},{9,1},{2,10},{10,2},{3,11},{11,3},{4,12},{12,4},... | collective-permute-start | bytes 61448 | tf_op jit(solution)/shard_map/ppermute | solution.py:455
  140.3 23.0 %all-to-all-start.4 = ((bf16[16,80,128]{2,1,0:T(8,128)(2,1)}), bf16[16,80,128]{2,1,0:T(8,128)(2,1)S(1)}, u32[]{:S(2)}, u32[]{:S(2)}) async-start(bf16[16,80,128]{2,1,0:T(8,128)(2,1)} %shard_map.104), calls=%async_computation.4 | async-start | bytes 655360 | tf_op jit(solution)/shard_map/all_to_all | solution.py:475
  147.6 11.2 %collective-permute-start.21 = (bf16[2,2,64,256]{3,2,1,0:T(8,128)(2,1)S(1)}, bf16[2,2,64,256]{3,2,1,0:T(8,128)(2,1)S(1)}, u32[]{:S(2)}, u32[]{:S(2)}) collective-permute-start(bf16[2,2,64,256]{3,2,1,0:T(8,128)(2,1)S(1)} %get-tuple-element.80), channel_id=1, source_target_pairs={{0,2},{2,4},{4,6},{6,0},{1,3},{3,5},{5,7},{7,1},{8,10},{10,12},{12... | collective-permute-start | bytes 393224 | tf_op jit(solution)/shard_map/ppermute | solution.py:451
  148.6 10.1 %collective-permute-start.22 = (bf16[2,2,64,256]{3,2,1,0:T(8,128)(2,1)S(1)}, bf16[2,2,64,256]{3,2,1,0:T(8,128)(2,1)S(1)}, u32[]{:S(2)}, u32[]{:S(2)}) collective-permute-start(bf16[2,2,64,256]{3,2,1,0:T(8,128)(2,1)S(1)} %get-tuple-element.81), channel_id=1, source_target_pairs={{0,4},{2,6},{4,0},{6,2},{1,5},{3,7},{5,1},{7,3},{8,12},{10,14},{12... | collective-permute-start | bytes 393224 | tf_op jit(solution)/shard_map/ppermute | solution.py:451
  150.6 11.1 %collective-permute-start.23 = (bf16[2,2,64,256]{3,2,1,0:T(8,128)(2,1)S(1)}, bf16[2,2,64,256]{3,2,1,0:T(8,128)(2,1)S(1)}, u32[]{:S(2)}, u32[]{:S(2)}) collective-permute-start(bf16[2,2,64,256]{3,2,1,0:T(8,128)(2,1)S(1)} %get-tuple-element.82), channel_id=1, source_target_pairs={{0,6},{2,0},{4,2},{6,4},{1,7},{3,1},{5,3},{7,5},{8,14},{10,8},{12,... | collective-permute-start | bytes 393224 | tf_op jit(solution)/shard_map/ppermute | solution.py:451
  (6 other events, 22.4 us)

commit v5 on v4

--- a/solution.py
+++ b/solution.py
@@ -33,8 +33,8 @@
     return pl.CostEstimate(flops=flops, bytes_accessed=moved, transcendentals=0)
 
 
-def spread_kernel(place, route, lengths, rows, proj, wout, sent, piece, rows_s, sems):
-    along = place[3]
+def spread_kernel(route, lengths, rows, proj, wout, sent, piece, rows_s, sems):
+    along = jnp.where(lax.axis_index("core") == 0, lax.axis_index("x"), lax.axis_index("y"))
     wrows = pl.ds(pl.multiple_of(along * (DH // 4), DH // 4), DH // 4)
     copies = (
         pltpu.make_async_copy(proj.at[along], piece.at[pl.ds(0, DH)], sems.at[0]),
@@ -126,9 +126,12 @@
         sent[meta[0, k]] = rows[k]
 
 
-def collect_kernel(place, route, arrived, pair0, pair1, pair2, pair3, rows, mixed):
+def collect_kernel(route, arrived, rows):
     for h in range(HIST):
         rows[h] = arrived[route[0, h]]
+
+
+def mixed_kernel(place, pair0, pair1, pair2, pair3, mixed):
     core = place[1]
     for k, pair in enumerate((pair0, pair1, pair2, pair3)):
         for side in range(2):
@@ -412,7 +415,7 @@
         in_specs=[SMEM, SMEM] + [VMEM] * 9,
         out_specs=(VMEM,) * 13,
         scratch_shapes=[pltpu.VMEM((H, 2, DH, SLOT), BF16), pltpu.VMEM((D, tokens), F32)],
-        compiler_params=params(10),
+        compiler_params=params(14),
         cost_estimate=cost(10**10, 2**24),
     )(place, meta, xa, *pieces)
 
@@ -492,11 +495,11 @@
             jax.ShapeDtypeStruct((groups, 2 * DH + META, TILE), BF16),
             jax.ShapeDtypeStruct((PIECE, D), BF16),
         ),
-        in_specs=[SMEM, SMEM, SMEM, ANY, ANY, ANY],
+        in_specs=[SMEM, SMEM, ANY, ANY, ANY],
         out_specs=(VMEM, VMEM),
         scratch_shapes=[pltpu.VMEM((HIST, DH, SLOT), BF16), pltpu.SemaphoreType.DMA((3,))],
         compiler_params=params(60),
-    )(place, route, lengths, features, w_in.transpose(0, 2, 1), w_out)
+    )(route, lengths, features, w_in.transpose(0, 2, 1), w_out)
     arrived = swap(sent, DP)
     shards = [piece] + [shift(piece, "zhi", k) for k in range(1, 4)]
     rows, meta = pl.pallas_call(
@@ -507,7 +510,7 @@
         ),
         in_specs=[VMEM, ANY, ANY, ANY],
         out_specs=(VMEM, SMEM),
-        compiler_params=params(6),
+        compiler_params=params(14),
     )(arrived, *shards[1:])
     pieces = gather_weights(shards)
     xa = swap(rows, COL).reshape(H, 2, DH, SLOT)
@@ -522,7 +525,7 @@
             out_shape=outs,
             in_specs=[SMEM] + [VMEM] * (len(args) - 1),
             out_specs=(VMEM,) * len(outs),
-            compiler_params=params(6),
+            compiler_params=params(14),
         )(*args)
 
     part = jax.ShapeDtypeStruct((4, 4, PIECE, 128), BF16)
@@ -542,7 +545,7 @@
         out_shape=(kept, part),
         in_specs=[VMEM] * 4,
         out_specs=(VMEM, VMEM),
-        compiler_params=params(6),
+        compiler_params=params(14),
     )(sums[0], *came)
 
     def col_pairs(same, cross, after):
@@ -552,7 +555,7 @@
             out_shape=(pair,) * 4,
             in_specs=[VMEM, VMEM, ANY],
             out_specs=(VMEM,) * 4,
-            compiler_params=params(6),
+            compiler_params=params(14),
         )(same, trade(cross, "core"), after)
         return [pairs[0]] + [shift(pairs[k], "zhi", k) for k in range(1, 4)]
 
@@ -561,25 +564,32 @@
         out_shape=jax.ShapeDtypeStruct((groups, DH, SLOT), BF16),
         in_specs=[SMEM, VMEM, ANY],
         out_specs=VMEM,
-        compiler_params=params(6),
+        compiler_params=params(14),
     )(meta, home, gate2)
     arrived = swap(back, DP)
     moved = col_pairs(msame, mcross, rounded)
     block = jax.ShapeDtypeStruct((HIST, DH, SLOT), BF16)
-    grad_features, mixed = pl.pallas_call(
+    grad_features = pl.pallas_call(
         collect_kernel,
-        out_shape=(block, block),
-        in_specs=[SMEM, SMEM] + [VMEM] * 5,
-        out_specs=(VMEM, VMEM),
-        compiler_params=params(6),
-    )(place, route, arrived, *moved)
+        out_shape=block,
+        in_specs=[SMEM, VMEM],
+        out_specs=VMEM,
+        compiler_params=params(14),
+    )(route, arrived)
+    mixed = pl.pallas_call(
+        mixed_kernel,
+        out_shape=block,
+        in_specs=[SMEM] + [VMEM] * 4,
+        out_specs=VMEM,
+        compiler_params=params(14),
+    )(place, *moved)
 
     whole = pl.pallas_call(
         repeat_kernel,
         out_shape=jax.ShapeDtypeStruct((16, PIECE, 128), BF16),
         in_specs=[VMEM, VMEM, ANY],
         out_specs=VMEM,
-        compiler_params=params(6),
+        compiler_params=params(14),
     )(total, trade(rounded, "zlo"), arrived)
     whole = swap(whole, ("y", "x"))
     grad_in, grad_out = pl.pallas_call(
@@ -587,7 +597,7 @@
         out_shape=(jax.ShapeDtypeStruct((4, DH, D), F32), jax.ShapeDtypeStruct((DH, D), F32)),
         in_specs=[VMEM],
         out_specs=(VMEM, VMEM),
-        compiler_params=params(6),
+        compiler_params=params(14),
     )(whole)
     return (mixed, grad_features, grad_in.transpose(0, 2, 1), grad_out)
 

time: 165 us -> 164 us (level)
  waiting for transfers between devices: 52.6 us -> 50.7 us
    ppermute x9, starting transfers between devices: 23.7 us -> 25.5 us  [shift(): return lax.ppermute(x, axis, [(i, (i + k) % 4) for i in range(4)])]
    ppermute x9, waiting for transfers between devices: 30.7 us -> 29.1 us  [shift(): return lax.ppermute(x, axis, [(i, (i + k) % 4) for i in range(4)])]
  transfers between devices with their start and end apart: 30 -> 30, of which waited for: 16 -> 15; matrix products, arithmetic and copies ran while one was open for 1% -> 1% of each run, Pallas kernels for 3% -> 4%
where the time goes in v5:
time: 164 us; the launch traced here: 163 us
  starting transfers between devices  78.1 us (48%)
  waiting for transfers between devices  50.7 us (31%)
  Pallas kernels  29.4 us (18%)
  local copies, waits for them, and re-layouts  3.67 us (2%)
    all_to_all x5, starting transfers between devices, swap(): return lax.all_to_all(x, axes, split_axis=0, concat_axis=0, tiled=True)  33.8 us
    ppermute x9, waiting for transfers between devices, shift(): return lax.ppermute(x, axis, [(i, (i + k) % 4) for i in range(4)])  29.1 us
    ppermute x9, starting transfers between devices, shift(): return lax.ppermute(x, axis, [(i, (i + k) % 4) for i in range(4)])  25.5 us
    ppermute x9, waiting for transfers between devices, turn(): return lax.ppermute(part, ('y', 'x', 'core'), pairs)  16.6 us
    ppermute x9, starting transfers between devices, turn(): return lax.ppermute(part, ('y', 'x', 'core'), pairs)  14.7 us
    pallas_call x1, Pallas kernels, run_backward(): pl.pallas_call(backward_kernel, out_shape=(jax.ShapeDtypeStruct((H, 2, DH...  8.7 us
    pallas_call x1, Pallas kernels, run_forward(): pl.pallas_call(forward_kernel, out_shape=(shape((4, 2, DH, SLOT), BF16),...  8.17 us
    ppermute x7, starting transfers between devices, trade(): return lax.ppermute(x, axis, [(0, 1), (1, 0)])  4.21 us
  transfers between devices with their start and end apart: 30, of which 15 were waited for; matrix products, arithmetic and copies ran while one was open for 1% of the time, Pallas kernels for 4%

profile of v5, /device:TPU:34, one launch (start us, length us, event | category | flops | bytes accessed | tf_op | source)
XLA Modules:
  0.0 162.8 jit_solution(12150450358381326239)
XLA Ops:
  0.6 3.0 %shard_map.93 = (bf16[32,144,128]{2,1,0:T(8,128)(2,1)}, bf16[80,512]{1,0:T(8,128)(2,1)}) custom-call(s32[2,16]{1,0:T(2,128)} %bitcast.19, s32[16]{0:T(128)} %lengths.1, bf16[16,64,256]{2,1,0:T(8,128)(2,1)} %rows.1, bf16[4,64,512]{2,1,0:T(8,128)(2,1)} %bitcast.21, bf16[64,512]{1,0:T(8,128)(2,1)} %wout.1), custom_call_target="tpu_custom_call" | custom-call | tf_op jit(solution)/shard_map/pallas_call | solution.py:492
  3.7 8.7 %all-to-all-start = ((bf16[32,144,128]{2,1,0:T(8,128)(2,1)}), bf16[32,144,128]{2,1,0:T(8,128)(2,1)S(1)}, u32[]{:S(2)}, u32[]{:S(2)}) async-start(bf16[32,144,128]{2,1,0:T(8,128)(2,1)} %get-tuple-element.44), calls=%async_computation | async-start | bytes 2359296 | tf_op jit(solution)/shard_map/all_to_all | solution.py:478
  12.3 3.3 %collective-permute-start = (bf16[80,512]{1,0:T(8,128)(2,1)S(1)}, bf16[80,512]{1,0:T(8,128)(2,1)S(1)}, u32[]{:S(2)}, u32[]{:S(2)}) collective-permute-start(bf16[80,512]{1,0:T(8,128)(2,1)S(1)} %copy-done.6), channel_id=1, source_target_pairs={{0,2},{2,4},{4,6},{6,0},{1,3},{3,5},{5,7},{7,1},{8,10},{10,12},{12... | collective-permute-start | bytes 245768 | tf_op jit(solution)/shard_map/ppermute | solution.py:454
  15.7 4.5 %collective-permute-start.1 = (bf16[80,512]{1,0:T(8,128)(2,1)S(1)}, bf16[80,512]{1,0:T(8,128)(2,1)S(1)}, u32[]{:S(2)}, u32[]{:S(2)}) collective-permute-start(bf16[80,512]{1,0:T(8,128)(2,1)S(1)} %copy-done.6), channel_id=1, source_target_pairs={{0,4},{2,6},{4,0},{6,2},{1,5},{3,7},{5,1},{7,3},{8,12},{10,14},{12... | collective-permute-start | bytes 245768 | tf_op jit(solution)/shard_map/ppermute | solution.py:454
  20.2 2.7 %collective-permute-start.2 = (bf16[80,512]{1,0:T(8,128)(2,1)S(1)}, bf16[80,512]{1,0:T(8,128)(2,1)S(1)}, u32[]{:S(2)}, u32[]{:S(2)}) collective-permute-start(bf16[80,512]{1,0:T(8,128)(2,1)S(1)} %copy-done.6), channel_id=1, source_target_pairs={{0,6},{2,0},{4,2},{6,4},{1,7},{3,1},{5,3},{7,5},{8,14},{10,8},{12,... | collective-permute-start | bytes 245768 | tf_op jit(solution)/shard_map/ppermute | solution.py:454
  22.9 13.9 %collective-permute-done.1.shard2 = bf16[80,512]{1,0:T(8,128)(2,1)S(1)} collective-permute-done((bf16[80,512]{1,0:T(8,128)(2,1)S(1)}, bf16[80,512]{1,0:T(8,128)(2,1)S(1)}, u32[]{:S(2)}, u32[]{:S(2)}) %collective-permute-start.1) | collective-permute-done | bytes 81952 | tf_op jit(solution)/shard_map/ppermute | solution.py:454
  38.1 4.5 %all-to-all-start.1 = ((bf16[16,64,256]{2,1,0:T(8,128)(2,1)}), bf16[16,64,256]{2,1,0:T(8,128)(2,1)S(1)}, u32[]{:S(2)}, u32[]{:S(2)}) async-start(bf16[16,64,256]{2,1,0:T(8,128)(2,1)} %get-tuple-element.47), calls=%async_computation.1 | async-start | bytes 1048576 | tf_op jit(solution)/shard_map/all_to_all | solution.py:478
  45.3 2.1 %collective-permute-start.5 = (bf16[4,80,512]{2,1,0:T(8,128)(2,1)S(1)}, bf16[4,80,512]{2,1,0:T(8,128)(2,1)S(1)}, u32[]{:S(2)}, u32[]{:S(2)}) collective-permute-start(bf16[4,80,512]{2,1,0:T(8,128)(2,1)S(1)} %pad_maximum_fusion.own0), channel_id=1, source_target_pairs={{0,48},{1,193},{16,0},{17,209},{32,16},{33,225},{48,32},{49,241},{... | collective-permute-start | bytes 983048 | tf_op jit(solution)/shard_map/ppermute | solution.py:468
  48.0 1.8 %collective-permute-done.3.own1 = bf16[4,80,512]{2,1,0:T(8,128)(2,1)S(1)} collective-permute-done((bf16[4,80,512]{2,1,0:T(8,128)(2,1)S(1)}, bf16[4,80,512]{2,1,0:T(8,128)(2,1)S(1)}, u32[]{:S(2)}, u32[]{:S(2)}) %collective-permute-start.3) | collective-permute-done | bytes 327712 | tf_op jit(solution)/shard_map/ppermute | solution.py:468
  50.6 2.2 %collective-permute-done.4.own2 = bf16[4,80,512]{2,1,0:T(8,128)(2,1)S(1)} collective-permute-done((bf16[4,80,512]{2,1,0:T(8,128)(2,1)S(1)}, bf16[4,80,512]{2,1,0:T(8,128)(2,1)S(1)}, u32[]{:S(2)}, u32[]{:S(2)}) %collective-permute-start.4) | collective-permute-done | bytes 327712 | tf_op jit(solution)/shard_map/ppermute | solution.py:468
  52.9 2.3 %collective-permute-start.8 = (bf16[4,80,512]{2,1,0:T(8,128)(2,1)S(1)}, bf16[4,80,512]{2,1,0:T(8,128)(2,1)}, u32[]{:S(2)}, u32[]{:S(2)}) collective-permute-start(bf16[4,80,512]{2,1,0:T(8,128)(2,1)S(1)} %collective-permute-done.4.own2), channel_id=1, source_target_pairs={{0,1},{1,0},{2,3},{3,2},{4,5},{5,4},{6,7},{7,6},{8,9},{9,8},{10,11... | collective-permute-start | bytes 983048 | tf_op jit(solution)/shard_map/ppermute | solution.py:458
  60.4 8.2 %shard_map.95 = (bf16[4,2,64,256]{3,2,1,0:T(8,128)(2,1)S(1)}, bf16[4,2,64,256]{3,2,1,0:T(8,128)(2,1)S(1)}, bf16[8,256,512]{2,1,0:T(8,128)(2,1)S(1)}, bf16[512,51...) custom-call(s32[5]{0:T(128)S(1)} %stack.38.place, ...), custom_call_target="tpu_custom_call" | custom-call | flops 10000000000 | bytes 16777216 | tf_op jit(solution)/shard_map/pallas_call | solution.py:398
  68.6 8.7 %shard_map.96 = (bf16[8,2,64,256]{3,2,1,0:T(8,128)(2,1)S(1)}, bf16[16,4,80,128]{3,2,1,0:T(8,128)(2,1)S(1)}, bf16[16,4,80,128]{3,2,1,0:T(8,128)(2,1)}) custom-call(s32[5]{0:T(128)S(1)} %stack.38.place, s32[2,16]{1,0:T(2,128)S(1)} %get-tuple-element.46.meta, bf16[2,512,256]{2,1,0:T(8,128)(2,1)S(1)} %constant_dynamic-slice_fusion.gy_ref, ...), custom_call_target="tpu_custom_call" | custom-call | flops 12000000000 | bytes 16777216 | tf_op jit(solution)/shard_map/pallas_call | solution.py:426
  78.1 6.1 %all-to-all-start.2 = ((bf16[16,64,256]{2,1,0:T(8,128)(2,1)}), bf16[16,64,256]{2,1,0:T(8,128)(2,1)S(1)}, u32[]{:S(2)}, u32[]{:S(2)}) async-start(bf16[16,64,256]{2,1,0:T(8,128)(2,1)} %bitcast.15), calls=%async_computation.2 | async-start | bytes 1048576 | tf_op jit(solution)/shard_map/all_to_all | solution.py:478
  87.4 1.9 %collective-permute-start.14 = (bf16[4,4,80,128]{3,2,1,0:T(8,128)(2,1)S(1)}, bf16[4,4,80,128]{3,2,1,0:T(8,128)(2,1)S(1)}, u32[]{:S(2)}, u32[]{:S(2)}) collective-permute-start(bf16[4,4,80,128]{3,2,1,0:T(8,128)(2,1)S(1)} %get-tuple-element.66), channel_id=1, source_target_pairs={{0,48},{1,193},{16,0},{17,209},{32,16},{33,225},{48,32},{49,241},{... | collective-permute-start | bytes 983048 | tf_op jit(solution)/shard_map/ppermute | solution.py:468
  89.3 3.0 %collective-permute-done.12.came1 = bf16[4,4,80,128]{3,2,1,0:T(8,128)(2,1)S(1)} collective-permute-done((bf16[4,4,80,128]{3,2,1,0:T(8,128)(2,1)S(1)}, bf16[4,4,80,128]{3,2,1,0:T(8,128)(2,1)S(1)}, u32[]{:S(2)}, u32[]{:S(2)}) %collective-permute-start.12) | collective-permute-done | bytes 327712 | tf_op jit(solution)/shard_map/ppermute | solution.py:468
  92.2 2.6 %collective-permute-done.13.came2 = bf16[4,4,80,128]{3,2,1,0:T(8,128)(2,1)S(1)} collective-permute-done((bf16[4,4,80,128]{3,2,1,0:T(8,128)(2,1)S(1)}, bf16[4,4,80,128]{3,2,1,0:T(8,128)(2,1)S(1)}, u32[]{:S(2)}, u32[]{:S(2)}) %collective-permute-start.13) | collective-permute-done | bytes 327712 | tf_op jit(solution)/shard_map/ppermute | solution.py:468
  94.8 3.2 %collective-permute-done.14.came3 = bf16[4,4,80,128]{3,2,1,0:T(8,128)(2,1)S(1)} collective-permute-done((bf16[4,4,80,128]{3,2,1,0:T(8,128)(2,1)S(1)}, bf16[4,4,80,128]{3,2,1,0:T(8,128)(2,1)S(1)}, u32[]{:S(2)}, u32[]{:S(2)}) %collective-permute-start.14) | collective-permute-done | bytes 327712 | tf_op jit(solution)/shard_map/ppermute | solution.py:468
  100.3 2.7 %collective-permute-start.16 = (bf16[4,80,128]{2,1,0:T(8,128)(2,1)S(1)}, bf16[4,80,128]{2,1,0:T(8,128)(2,1)S(1)}, u32[]{:S(2)}, u32[]{:S(2)}) collective-permute-start(bf16[4,80,128]{2,1,0:T(8,128)(2,1)S(1)} %get-tuple-element.69), channel_id=1, source_target_pairs={{0,128},{1,33},{16,144},{17,49},{32,160},{33,1},{48,176},{49,17},{... | collective-permute-start | bytes 245768 | tf_op jit(solution)/shard_map/ppermute | solution.py:468
  104.4 1.9 %collective-permute-done.16.came2 = bf16[4,80,128]{2,1,0:T(8,128)(2,1)S(1)} collective-permute-done((bf16[4,80,128]{2,1,0:T(8,128)(2,1)S(1)}, bf16[4,80,128]{2,1,0:T(8,128)(2,1)S(1)}, u32[]{:S(2)}, u32[]{:S(2)}) %collective-permute-start.16) | collective-permute-done | bytes 81952 | tf_op jit(solution)/shard_map/ppermute | solution.py:468
  108.1 1.6 %shard_map.103 = bf16[32,64,256]{2,1,0:T(8,128)(2,1)} custom-call(s32[2,16]{1,0:T(2,128)S(1)} %get-tuple-element.46.meta, bf16[16,64,256]{2,1,0:T(8,128)(2,1)S(1)} %all-to-all-done.2.rows, bf16[80,128]{1,0:T(8,128)(2,1)S(1)} %get-tuple-element.72.after), custom_call_target="tpu_custom_call" | custom-call | tf_op jit(solution)/shard_map/pallas_call | solution.py:562
  109.7 7.3 %all-to-all-start.3 = ((bf16[32,64,256]{2,1,0:T(8,128)(2,1)}), bf16[32,64,256]{2,1,0:T(8,128)(2,1)S(1)}, u32[]{:S(2)}, u32[]{:S(2)}) async-start(bf16[32,64,256]{2,1,0:T(8,128)(2,1)} %shard_map.103), calls=%async_computation.3 | async-start | bytes 2097152 | tf_op jit(solution)/shard_map/all_to_all | solution.py:478
  117.1 3.0 %collective-permute-start.18 = (bf16[80,128]{1,0:T(8,128)(2,1)S(1)}, bf16[80,128]{1,0:T(8,128)(2,1)S(1)}, u32[]{:S(2)}, u32[]{:S(2)}) collective-permute-start(bf16[80,128]{1,0:T(8,128)(2,1)S(1)} %get-tuple-element.72.after), channel_id=1, source_target_pairs={{0,2},{2,4},{4,6},{6,0},{1,3},{3,5},{5,7},{7,1},{8,10},{10,12},{12... | collective-permute-start | bytes 61448 | tf_op jit(solution)/shard_map/ppermute | solution.py:454
  120.1 3.6 %collective-permute-start.19 = (bf16[80,128]{1,0:T(8,128)(2,1)S(1)}, bf16[80,128]{1,0:T(8,128)(2,1)S(1)}, u32[]{:S(2)}, u32[]{:S(2)}) collective-permute-start(bf16[80,128]{1,0:T(8,128)(2,1)S(1)} %get-tuple-element.73), channel_id=1, source_target_pairs={{0,4},{2,6},{4,0},{6,2},{1,5},{3,7},{5,1},{7,3},{8,12},{10,14},{12... | collective-permute-start | bytes 61448 | tf_op jit(solution)/shard_map/ppermute | solution.py:454
  123.7 3.6 %collective-permute-start.20 = (bf16[80,128]{1,0:T(8,128)(2,1)S(1)}, bf16[80,128]{1,0:T(8,128)(2,1)S(1)}, u32[]{:S(2)}, u32[]{:S(2)}) collective-permute-start(bf16[80,128]{1,0:T(8,128)(2,1)S(1)} %get-tuple-element.74), channel_id=1, source_target_pairs={{0,6},{2,0},{4,2},{6,4},{1,7},{3,1},{5,3},{7,5},{8,14},{10,8},{12,... | collective-permute-start | bytes 61448 | tf_op jit(solution)/shard_map/ppermute | solution.py:454
  127.2 6.4 %collective-permute-done.19.came2 = bf16[80,128]{1,0:T(8,128)(2,1)S(1)} collective-permute-done((bf16[80,128]{1,0:T(8,128)(2,1)S(1)}, bf16[80,128]{1,0:T(8,128)(2,1)S(1)}, u32[]{:S(2)}, u32[]{:S(2)}) %collective-permute-start.19) | collective-permute-done | bytes 20512 | tf_op jit(solution)/shard_map/ppermute | solution.py:454
  134.1 3.4 %collective-permute-done.24.came = bf16[80,128]{1,0:T(8,128)(2,1)S(1)} collective-permute-done((bf16[80,128]{1,0:T(8,128)(2,1)S(1)}, bf16[80,128]{1,0:T(8,128)(2,1)S(1)}, u32[]{:S(2)}, u32[]{:S(2)}) %collective-permute-start.24) | collective-permute-done | bytes 20512 | tf_op jit(solution)/shard_map/ppermute | solution.py:458
  138.3 7.2 %all-to-all-start.4 = ((bf16[16,80,128]{2,1,0:T(8,128)(2,1)}), bf16[16,80,128]{2,1,0:T(8,128)(2,1)S(1)}, u32[]{:S(2)}, u32[]{:S(2)}) async-start(bf16[16,80,128]{2,1,0:T(8,128)(2,1)} %shard_map.105), calls=%async_computation.4 | async-start | bytes 655360 | tf_op jit(solution)/shard_map/all_to_all | solution.py:478
  146.4 1.7 %collective-permute-start.22 = (bf16[2,2,64,256]{3,2,1,0:T(8,128)(2,1)S(1)}, bf16[2,2,64,256]{3,2,1,0:T(8,128)(2,1)S(1)}, u32[]{:S(2)}, u32[]{:S(2)}) collective-permute-start(bf16[2,2,64,256]{3,2,1,0:T(8,128)(2,1)S(1)} %get-tuple-element.78), channel_id=1, source_target_pairs={{0,4},{2,6},{4,0},{6,2},{1,5},{3,7},{5,1},{7,3},{8,12},{10,14},{12... | collective-permute-start | bytes 393224 | tf_op jit(solution)/shard_map/ppermute | solution.py:454
  148.1 2.3 %collective-permute-start.23 = (bf16[2,2,64,256]{3,2,1,0:T(8,128)(2,1)S(1)}, bf16[2,2,64,256]{3,2,1,0:T(8,128)(2,1)S(1)}, u32[]{:S(2)}, u32[]{:S(2)}) collective-permute-start(bf16[2,2,64,256]{3,2,1,0:T(8,128)(2,1)S(1)} %get-tuple-element.79), channel_id=1, source_target_pairs={{0,6},{2,0},{4,2},{6,4},{1,7},{3,1},{5,3},{7,5},{8,14},{10,8},{12,... | collective-permute-start | bytes 393224 | tf_op jit(solution)/shard_map/ppermute | solution.py:454
  150.4 6.3 %collective-permute-done.21.pair1 = bf16[2,2,64,256]{3,2,1,0:T(8,128)(2,1)S(1)} collective-permute-done((bf16[2,2,64,256]{3,2,1,0:T(8,128)(2,1)S(1)}, bf16[2,2,64,256]{3,2,1,0:T(8,128)(2,1)S(1)}, u32[]{:S(2)}, u32[]{:S(2)}) %collective-permute-start.21) | collective-permute-done | bytes 131104 | tf_op jit(solution)/shard_map/ppermute | solution.py:454
  157.1 2.0 %collective-permute-done.23.pair3 = bf16[2,2,64,256]{3,2,1,0:T(8,128)(2,1)S(1)} collective-permute-done((bf16[2,2,64,256]{3,2,1,0:T(8,128)(2,1)S(1)}, bf16[2,2,64,256]{3,2,1,0:T(8,128)(2,1)S(1)}, u32[]{:S(2)}, u32[]{:S(2)}) %collective-permute-start.23) | collective-permute-done | bytes 131104 | tf_op jit(solution)/shard_map/ppermute | solution.py:454
  (59 shorter events, 26.4 us)
Async XLA Ops:
  3.7 33.1 %all-to-all-start = ((bf16[32,144,128]{2,1,0:T(8,128)(2,1)}), bf16[32,144,128]{2,1,0:T(8,128)(2,1)S(1)}, u32[]{:S(2)}, u32[]{:S(2)}) async-start(bf16[32,144,128]{2,1,0:T(8,128)(2,1)} %get-tuple-element.44), calls=%async_computation | async-start | bytes 2359296 | tf_op jit(solution)/shard_map/all_to_all | solution.py:478
  12.3 10.5 %collective-permute-start = (bf16[80,512]{1,0:T(8,128)(2,1)S(1)}, bf16[80,512]{1,0:T(8,128)(2,1)S(1)}, u32[]{:S(2)}, u32[]{:S(2)}) collective-permute-start(bf16[80,512]{1,0:T(8,128)(2,1)S(1)} %copy-done.6), channel_id=1, source_target_pairs={{0,2},{2,4},{4,6},{6,0},{1,3},{3,5},{5,7},{7,1},{8,10},{10,12},{12... | collective-permute-start | bytes 245768 | tf_op jit(solution)/shard_map/ppermute | solution.py:454
  15.7 21.1 %collective-permute-start.1 = (bf16[80,512]{1,0:T(8,128)(2,1)S(1)}, bf16[80,512]{1,0:T(8,128)(2,1)S(1)}, u32[]{:S(2)}, u32[]{:S(2)}) collective-permute-start(bf16[80,512]{1,0:T(8,128)(2,1)S(1)} %copy-done.6), channel_id=1, source_target_pairs={{0,4},{2,6},{4,0},{6,2},{1,5},{3,7},{5,1},{7,3},{8,12},{10,14},{12... | collective-permute-start | bytes 245768 | tf_op jit(solution)/shard_map/ppermute | solution.py:454
  20.2 16.6 %collective-permute-start.2 = (bf16[80,512]{1,0:T(8,128)(2,1)S(1)}, bf16[80,512]{1,0:T(8,128)(2,1)S(1)}, u32[]{:S(2)}, u32[]{:S(2)}) collective-permute-start(bf16[80,512]{1,0:T(8,128)(2,1)S(1)} %copy-done.6), channel_id=1, source_target_pairs={{0,6},{2,0},{4,2},{6,4},{1,7},{3,1},{5,3},{7,5},{8,14},{10,8},{12,... | collective-permute-start | bytes 245768 | tf_op jit(solution)/shard_map/ppermute | solution.py:454
  38.1 21.4 %all-to-all-start.1 = ((bf16[16,64,256]{2,1,0:T(8,128)(2,1)}), bf16[16,64,256]{2,1,0:T(8,128)(2,1)S(1)}, u32[]{:S(2)}, u32[]{:S(2)}) async-start(bf16[16,64,256]{2,1,0:T(8,128)(2,1)} %get-tuple-element.47), calls=%async_computation.1 | async-start | bytes 1048576 | tf_op jit(solution)/shard_map/all_to_all | solution.py:478
  42.6 7.2 %collective-permute-start.3 = (bf16[4,80,512]{2,1,0:T(8,128)(2,1)S(1)}, bf16[4,80,512]{2,1,0:T(8,128)(2,1)S(1)}, u32[]{:S(2)}, u32[]{:S(2)}) collective-permute-start(bf16[4,80,512]{2,1,0:T(8,128)(2,1)S(1)} %pad_maximum_fusion.own0), channel_id=1, source_target_pairs={{0,16},{1,65},{16,32},{17,81},{32,48},{33,97},{48,0},{49,113},{64,... | collective-permute-start | bytes 983048 | tf_op jit(solution)/shard_map/ppermute | solution.py:468
  44.2 8.7 %collective-permute-start.4 = (bf16[4,80,512]{2,1,0:T(8,128)(2,1)S(1)}, bf16[4,80,512]{2,1,0:T(8,128)(2,1)S(1)}, u32[]{:S(2)}, u32[]{:S(2)}) collective-permute-start(bf16[4,80,512]{2,1,0:T(8,128)(2,1)S(1)} %pad_maximum_fusion.own0), channel_id=1, source_target_pairs={{0,32},{1,129},{16,48},{17,145},{32,0},{33,161},{48,16},{49,177},{... | collective-permute-start | bytes 983048 | tf_op jit(solution)/shard_map/ppermute | solution.py:468
  45.3 10.6 %collective-permute-start.5 = (bf16[4,80,512]{2,1,0:T(8,128)(2,1)S(1)}, bf16[4,80,512]{2,1,0:T(8,128)(2,1)S(1)}, u32[]{:S(2)}, u32[]{:S(2)}) collective-permute-start(bf16[4,80,512]{2,1,0:T(8,128)(2,1)S(1)} %pad_maximum_fusion.own0), channel_id=1, source_target_pairs={{0,48},{1,193},{16,0},{17,209},{32,16},{33,225},{48,32},{49,241},{... | collective-permute-start | bytes 983048 | tf_op jit(solution)/shard_map/ppermute | solution.py:468
  47.4 9.7 %collective-permute-start.6 = (bf16[4,80,512]{2,1,0:T(8,128)(2,1)S(1)}, bf16[4,80,512]{2,1,0:T(8,128)(2,1)S(1)}, u32[]{:S(2)}, u32[]{:S(2)}) collective-permute-start(bf16[4,80,512]{2,1,0:T(8,128)(2,1)S(1)} %pad_maximum_fusion.own0), channel_id=1, source_target_pairs={{0,1},{1,0},{2,3},{3,2},{4,5},{5,4},{6,7},{7,6},{8,9},{9,8},{10,11... | collective-permute-start | bytes 983048 | tf_op jit(solution)/shard_map/ppermute | solution.py:458
  49.8 7.3 %collective-permute-start.7 = (bf16[4,80,512]{2,1,0:T(8,128)(2,1)S(1)}, bf16[4,80,512]{2,1,0:T(8,128)(2,1)S(1)}, u32[]{:S(2)}, u32[]{:S(2)}) collective-permute-start(bf16[4,80,512]{2,1,0:T(8,128)(2,1)S(1)} %collective-permute-done.3.own1), channel_id=1, source_target_pairs={{0,1},{1,0},{2,3},{3,2},{4,5},{5,4},{6,7},{7,6},{8,9},{9,8},{10,11... | collective-permute-start | bytes 983048 | tf_op jit(solution)/shard_map/ppermute | solution.py:458
  52.9 5.0 %collective-permute-start.8 = (bf16[4,80,512]{2,1,0:T(8,128)(2,1)S(1)}, bf16[4,80,512]{2,1,0:T(8,128)(2,1)}, u32[]{:S(2)}, u32[]{:S(2)}) collective-permute-start(bf16[4,80,512]{2,1,0:T(8,128)(2,1)S(1)} %collective-permute-done.4.own2), channel_id=1, source_target_pairs={{0,1},{1,0},{2,3},{3,2},{4,5},{5,4},{6,7},{7,6},{8,9},{9,8},{10,11... | collective-permute-start | bytes 983048 | tf_op jit(solution)/shard_map/ppermute | solution.py:458
  55.9 1.9 %collective-permute-start.9 = (bf16[4,80,512]{2,1,0:T(8,128)(2,1)S(1)}, bf16[4,80,512]{2,1,0:T(8,128)(2,1)}, u32[]{:S(2)}, u32[]{:S(2)}) collective-permute-start(bf16[4,80,512]{2,1,0:T(8,128)(2,1)S(1)} %collective-permute-done.5.own3), channel_id=1, source_target_pairs={{0,1},{1,0},{2,3},{3,2},{4,5},{5,4},{6,7},{7,6},{8,9},{9,8},{10,11... | collective-permute-start | bytes 983048 | tf_op jit(solution)/shard_map/ppermute | solution.py:458
  78.1 6.1 %collective-permute-start.11 = (bf16[16,4,80,128]{3,2,1,0:T(8,128)(2,1)}, bf16[16,4,80,128]{3,2,1,0:T(8,128)(2,1)S(1)}, u32[]{:S(2)}, u32[]{:S(2)}) collective-permute-start(bf16[16,4,80,128]{3,2,1,0:T(8,128)(2,1)} %get-tuple-element.62), channel_id=1, source_target_pairs={{0,1},{1,0},{2,3},{3,2},{4,5},{5,4},{6,7},{7,6},{8,9},{9,8},{10,11... | collective-permute-start | bytes 3932168 | tf_op jit(solution)/shard_map/ppermute | solution.py:458
  78.1 29.9 %all-to-all-start.2 = ((bf16[16,64,256]{2,1,0:T(8,128)(2,1)}), bf16[16,64,256]{2,1,0:T(8,128)(2,1)S(1)}, u32[]{:S(2)}, u32[]{:S(2)}) async-start(bf16[16,64,256]{2,1,0:T(8,128)(2,1)} %bitcast.15), calls=%async_computation.2 | async-start | bytes 1048576 | tf_op jit(solution)/shard_map/all_to_all | solution.py:478
  85.1 7.2 %collective-permute-start.12 = (bf16[4,4,80,128]{3,2,1,0:T(8,128)(2,1)S(1)}, bf16[4,4,80,128]{3,2,1,0:T(8,128)(2,1)S(1)}, u32[]{:S(2)}, u32[]{:S(2)}) collective-permute-start(bf16[4,4,80,128]{3,2,1,0:T(8,128)(2,1)S(1)} %get-tuple-element.64), channel_id=1, source_target_pairs={{0,16},{1,65},{16,32},{17,81},{32,48},{33,97},{48,0},{49,113},{64,... | collective-permute-start | bytes 983048 | tf_op jit(solution)/shard_map/ppermute | solution.py:468
  86.1 8.7 %collective-permute-start.13 = (bf16[4,4,80,128]{3,2,1,0:T(8,128)(2,1)S(1)}, bf16[4,4,80,128]{3,2,1,0:T(8,128)(2,1)S(1)}, u32[]{:S(2)}, u32[]{:S(2)}) collective-permute-start(bf16[4,4,80,128]{3,2,1,0:T(8,128)(2,1)S(1)} %get-tuple-element.65), channel_id=1, source_target_pairs={{0,32},{1,129},{16,48},{17,145},{32,0},{33,161},{48,16},{49,177},{... | collective-permute-start | bytes 983048 | tf_op jit(solution)/shard_map/ppermute | solution.py:468
  87.4 10.6 %collective-permute-start.14 = (bf16[4,4,80,128]{3,2,1,0:T(8,128)(2,1)S(1)}, bf16[4,4,80,128]{3,2,1,0:T(8,128)(2,1)S(1)}, u32[]{:S(2)}, u32[]{:S(2)}) collective-permute-start(bf16[4,4,80,128]{3,2,1,0:T(8,128)(2,1)S(1)} %get-tuple-element.66), channel_id=1, source_target_pairs={{0,48},{1,193},{16,0},{17,209},{32,16},{33,225},{48,32},{49,241},{... | collective-permute-start | bytes 983048 | tf_op jit(solution)/shard_map/ppermute | solution.py:468
  98.7 5.7 %collective-permute-start.15 = (bf16[4,80,128]{2,1,0:T(8,128)(2,1)S(1)}, bf16[4,80,128]{2,1,0:T(8,128)(2,1)S(1)}, u32[]{:S(2)}, u32[]{:S(2)}) collective-permute-start(bf16[4,80,128]{2,1,0:T(8,128)(2,1)S(1)} %get-tuple-element.68), channel_id=1, source_target_pairs={{0,64},{1,17},{16,80},{17,33},{32,96},{33,49},{48,112},{49,1},{64,... | collective-permute-start | bytes 245768 | tf_op jit(solution)/shard_map/ppermute | solution.py:468
  100.3 6.0 %collective-permute-start.16 = (bf16[4,80,128]{2,1,0:T(8,128)(2,1)S(1)}, bf16[4,80,128]{2,1,0:T(8,128)(2,1)S(1)}, u32[]{:S(2)}, u32[]{:S(2)}) collective-permute-start(bf16[4,80,128]{2,1,0:T(8,128)(2,1)S(1)} %get-tuple-element.69), channel_id=1, source_target_pairs={{0,128},{1,33},{16,144},{17,49},{32,160},{33,1},{48,176},{49,17},{... | collective-permute-start | bytes 245768 | tf_op jit(solution)/shard_map/ppermute | solution.py:468
  103.0 4.4 %collective-permute-start.17 = (bf16[4,80,128]{2,1,0:T(8,128)(2,1)S(1)}, bf16[4,80,128]{2,1,0:T(8,128)(2,1)S(1)}, u32[]{:S(2)}, u32[]{:S(2)}) collective-permute-start(bf16[4,80,128]{2,1,0:T(8,128)(2,1)S(1)} %get-tuple-element.70), channel_id=1, source_target_pairs={{0,192},{1,49},{16,208},{17,1},{32,224},{33,17},{48,240},{49,33},{... | collective-permute-start | bytes 245768 | tf_op jit(solution)/shard_map/ppermute | solution.py:468
  108.1 8.9 %copy-start.5 = (bf16[4,2,64,256]{3,2,1,0:T(8,128)(2,1)S(1)}, bf16[4,2,64,256]{3,2,1,0:T(8,128)(2,1)}, u32[]{:S(2)}) copy-start(bf16[4,2,64,256]{3,2,1,0:T(8,128)(2,1)} %copy-done.4) | copy-start | bytes 786436
  109.7 27.8 %all-to-all-start.3 = ((bf16[32,64,256]{2,1,0:T(8,128)(2,1)}), bf16[32,64,256]{2,1,0:T(8,128)(2,1)S(1)}, u32[]{:S(2)}, u32[]{:S(2)}) async-start(bf16[32,64,256]{2,1,0:T(8,128)(2,1)} %shard_map.103), calls=%async_computation.3 | async-start | bytes 2097152 | tf_op jit(solution)/shard_map/all_to_all | solution.py:478
  117.0 28.5 %collective-permute-start.10 = (bf16[4,2,64,256]{3,2,1,0:T(8,128)(2,1)S(1)}, bf16[4,2,64,256]{3,2,1,0:T(8,128)(2,1)S(1)}, u32[]{:S(2)}, u32[]{:S(2)}) collective-permute-start(bf16[4,2,64,256]{3,2,1,0:T(8,128)(2,1)S(1)} %copy-done.5), channel_id=1, source_target_pairs={{0,1},{1,0},{2,3},{3,2},{4,5},{5,4},{6,7},{7,6},{8,9},{9,8},{10,11... | collective-permute-start | bytes 786440 | tf_op jit(solution)/shard_map/ppermute | solution.py:458
  117.1 10.1 %collective-permute-start.18 = (bf16[80,128]{1,0:T(8,128)(2,1)S(1)}, bf16[80,128]{1,0:T(8,128)(2,1)S(1)}, u32[]{:S(2)}, u32[]{:S(2)}) collective-permute-start(bf16[80,128]{1,0:T(8,128)(2,1)S(1)} %get-tuple-element.72.after), channel_id=1, source_target_pairs={{0,2},{2,4},{4,6},{6,0},{1,3},{3,5},{5,7},{7,1},{8,10},{10,12},{12... | collective-permute-start | bytes 61448 | tf_op jit(solution)/shard_map/ppermute | solution.py:454
  120.1 13.5 %collective-permute-start.19 = (bf16[80,128]{1,0:T(8,128)(2,1)S(1)}, bf16[80,128]{1,0:T(8,128)(2,1)S(1)}, u32[]{:S(2)}, u32[]{:S(2)}) collective-permute-start(bf16[80,128]{1,0:T(8,128)(2,1)S(1)} %get-tuple-element.73), channel_id=1, source_target_pairs={{0,4},{2,6},{4,0},{6,2},{1,5},{3,7},{5,1},{7,3},{8,12},{10,14},{12... | collective-permute-start | bytes 61448 | tf_op jit(solution)/shard_map/ppermute | solution.py:454
  123.7 10.0 %collective-permute-start.20 = (bf16[80,128]{1,0:T(8,128)(2,1)S(1)}, bf16[80,128]{1,0:T(8,128)(2,1)S(1)}, u32[]{:S(2)}, u32[]{:S(2)}) collective-permute-start(bf16[80,128]{1,0:T(8,128)(2,1)S(1)} %get-tuple-element.74), channel_id=1, source_target_pairs={{0,6},{2,0},{4,2},{6,4},{1,7},{3,1},{5,3},{7,5},{8,14},{10,8},{12,... | collective-permute-start | bytes 61448 | tf_op jit(solution)/shard_map/ppermute | solution.py:454
  133.6 3.9 %collective-permute-start.24 = (bf16[80,128]{1,0:T(8,128)(2,1)S(1)}, bf16[80,128]{1,0:T(8,128)(2,1)S(1)}, u32[]{:S(2)}, u32[]{:S(2)}) collective-permute-start(bf16[80,128]{1,0:T(8,128)(2,1)S(1)} %get-tuple-element.75.after), channel_id=1, source_target_pairs={{0,8},{8,0},{1,9},{9,1},{2,10},{10,2},{3,11},{11,3},{4,12},{12,4},... | collective-permute-start | bytes 61448 | tf_op jit(solution)/shard_map/ppermute | solution.py:458
  137.5 23.0 %copy-start.1 = (s32[16,2]{0,1:T(2,128)S(1)}, s32[16,2]{0,1:T(2,128)}, u32[]{:S(2)}) copy-start(s32[16,2]{0,1:T(2,128)} %param.9) | copy-start | bytes 388
  138.3 23.6 %all-to-all-start.4 = ((bf16[16,80,128]{2,1,0:T(8,128)(2,1)}), bf16[16,80,128]{2,1,0:T(8,128)(2,1)S(1)}, u32[]{:S(2)}, u32[]{:S(2)}) async-start(bf16[16,80,128]{2,1,0:T(8,128)(2,1)} %shard_map.105), calls=%async_computation.4 | async-start | bytes 655360 | tf_op jit(solution)/shard_map/all_to_all | solution.py:478
  145.6 11.1 %collective-permute-start.21 = (bf16[2,2,64,256]{3,2,1,0:T(8,128)(2,1)S(1)}, bf16[2,2,64,256]{3,2,1,0:T(8,128)(2,1)S(1)}, u32[]{:S(2)}, u32[]{:S(2)}) collective-permute-start(bf16[2,2,64,256]{3,2,1,0:T(8,128)(2,1)S(1)} %get-tuple-element.77), channel_id=1, source_target_pairs={{0,2},{2,4},{4,6},{6,0},{1,3},{3,5},{5,7},{7,1},{8,10},{10,12},{12... | collective-permute-start | bytes 393224 | tf_op jit(solution)/shard_map/ppermute | solution.py:454
  146.4 10.7 %collective-permute-start.22 = (bf16[2,2,64,256]{3,2,1,0:T(8,128)(2,1)S(1)}, bf16[2,2,64,256]{3,2,1,0:T(8,128)(2,1)S(1)}, u32[]{:S(2)}, u32[]{:S(2)}) collective-permute-start(bf16[2,2,64,256]{3,2,1,0:T(8,128)(2,1)S(1)} %get-tuple-element.78), channel_id=1, source_target_pairs={{0,4},{2,6},{4,0},{6,2},{1,5},{3,7},{5,1},{7,3},{8,12},{10,14},{12... | collective-permute-start | bytes 393224 | tf_op jit(solution)/shard_map/ppermute | solution.py:454
  148.1 11.0 %collective-permute-start.23 = (bf16[2,2,64,256]{3,2,1,0:T(8,128)(2,1)S(1)}, bf16[2,2,64,256]{3,2,1,0:T(8,128)(2,1)S(1)}, u32[]{:S(2)}, u32[]{:S(2)}) collective-permute-start(bf16[2,2,64,256]{3,2,1,0:T(8,128)(2,1)S(1)} %get-tuple-element.79), channel_id=1, source_target_pairs={{0,6},{2,0},{4,2},{6,4},{1,7},{3,1},{5,3},{7,5},{8,14},{10,8},{12,... | collective-permute-start | bytes 393224 | tf_op jit(solution)/shard_map/ppermute | solution.py:454
  (5 other events, 19.9 us)

commit v6 on v5

--- a/solution.py
+++ b/solution.py
@@ -126,12 +126,13 @@
         sent[meta[0, k]] = rows[k]
 
 
-def collect_kernel(route, arrived, rows):
+def collect_kernel(route, arrived, rows, done):
+    done[...] = jnp.zeros_like(done)
     for h in range(HIST):
         rows[h] = arrived[route[0, h]]
 
 
-def mixed_kernel(place, pair0, pair1, pair2, pair3, mixed):
+def mixed_kernel(place, pair0, pair1, pair2, pair3, after1, after2, mixed):
     core = place[1]
     for k, pair in enumerate((pair0, pair1, pair2, pair3)):
         for side in range(2):
@@ -440,7 +441,8 @@
     )(place, meta, grad_y, *saved)
 
 
-def finish_kernel(arrived, grad_in, grad_out):
+def finish_kernel(arrived, grad_in, grad_out, done):
+    done[...] = jnp.zeros_like(done)
     factor = float(HIST * 32 * SLOT) ** -0.5
     for part in range(4):
         lanes = slice(part * 128, (part + 1) * 128)
@@ -569,21 +571,14 @@
     arrived = swap(back, DP)
     moved = col_pairs(msame, mcross, rounded)
     block = jax.ShapeDtypeStruct((HIST, DH, SLOT), BF16)
-    grad_features = pl.pallas_call(
+    token = jax.ShapeDtypeStruct((8, 128), F32)
+    grad_features, done1 = pl.pallas_call(
         collect_kernel,
-        out_shape=block,
+        out_shape=(block, token),
         in_specs=[SMEM, VMEM],
-        out_specs=VMEM,
+        out_specs=(VMEM, VMEM),
         compiler_params=params(14),
     )(route, arrived)
-    mixed = pl.pallas_call(
-        mixed_kernel,
-        out_shape=block,
-        in_specs=[SMEM] + [VMEM] * 4,
-        out_specs=VMEM,
-        compiler_params=params(14),
-    )(place, *moved)
-
     whole = pl.pallas_call(
         repeat_kernel,
         out_shape=jax.ShapeDtypeStruct((16, PIECE, 128), BF16),
@@ -592,13 +587,20 @@
         compiler_params=params(14),
     )(total, trade(rounded, "zlo"), arrived)
     whole = swap(whole, ("y", "x"))
-    grad_in, grad_out = pl.pallas_call(
+    grad_in, grad_out, done2 = pl.pallas_call(
         finish_kernel,
-        out_shape=(jax.ShapeDtypeStruct((4, DH, D), F32), jax.ShapeDtypeStruct((DH, D), F32)),
+        out_shape=(jax.ShapeDtypeStruct((4, DH, D), F32), jax.ShapeDtypeStruct((DH, D), F32), token),
         in_specs=[VMEM],
-        out_specs=(VMEM, VMEM),
+        out_specs=(VMEM, VMEM, VMEM),
         compiler_params=params(14),
     )(whole)
+    mixed = pl.pallas_call(
+        mixed_kernel,
+        out_shape=block,
+        in_specs=[SMEM] + [VMEM] * 4 + [ANY] * 2,
+        out_specs=VMEM,
+        compiler_params=params(14),
+    )(place, *moved, done1, done2)
     return (mixed, grad_features, grad_in.transpose(0, 2, 1), grad_out)
 
 

time: 164 us -> 161 us (0.982)
  waiting for transfers between devices: 50.7 us -> 48.4 us
    ppermute x9, waiting for transfers between devices: 29.1 us -> 25.4 us  [shift(): return lax.ppermute(x, axis, [(i, (i + k) % 4) for i in range(4)])]
  transfers between devices with their start and end apart: 30 -> 30, of which waited for: 15 -> 16; matrix products, arithmetic and copies ran while one was open for 1% -> 1% of each run, Pallas kernels for 4% -> 3%
where the time goes in v6:
time: 161 us
  starting transfers between devices  78.2 us (49%)
  waiting for transfers between devices  48.4 us (30%)
  Pallas kernels  29.4 us (18%)
  local copies, waits for them, and re-layouts  3.67 us (2%)
    all_to_all x5, starting transfers between devices, swap(): return lax.all_to_all(x, axes, split_axis=0, concat_axis=0, tiled=True)  33.8 us
    ppermute x9, starting transfers between devices, shift(): return lax.ppermute(x, axis, [(i, (i + k) % 4) for i in range(4)])  25.5 us
    ppermute x9, waiting for transfers between devices, shift(): return lax.ppermute(x, axis, [(i, (i + k) % 4) for i in range(4)])  25.4 us
    ppermute x9, waiting for transfers between devices, turn(): return lax.ppermute(part, ('y', 'x', 'core'), pairs)  16.6 us
    ppermute x9, starting transfers between devices, turn(): return lax.ppermute(part, ('y', 'x', 'core'), pairs)  14.7 us
    pallas_call x1, Pallas kernels, run_backward(): pl.pallas_call(backward_kernel, out_shape=(jax.ShapeDtypeStruct((H, 2, DH...  8.7 us
    pallas_call x1, Pallas kernels, run_forward(): pl.pallas_call(forward_kernel, out_shape=(shape((4, 2, DH, SLOT), BF16),...  8.16 us
    ppermute x7, starting transfers between devices, trade(): return lax.ppermute(x, axis, [(0, 1), (1, 0)])  4.21 us
  transfers between devices with their start and end apart: 30, of which 16 were waited for; matrix products, arithmetic and copies ran while one was open for 1% of the time, Pallas kernels for 3%

profile of v6, /device:TPU:34, one launch (start us, length us, event | category | flops | bytes accessed | tf_op | source)
XLA Modules:
  0.0 160.5 jit_solution(15190234549535488055)
XLA Ops:
  0.6 3.0 %shard_map.93 = (bf16[32,144,128]{2,1,0:T(8,128)(2,1)}, bf16[80,512]{1,0:T(8,128)(2,1)}) custom-call(s32[2,16]{1,0:T(2,128)} %bitcast.19, s32[16]{0:T(128)} %lengths.1, bf16[16,64,256]{2,1,0:T(8,128)(2,1)} %rows.1, bf16[4,64,512]{2,1,0:T(8,128)(2,1)} %bitcast.21, bf16[64,512]{1,0:T(8,128)(2,1)} %wout.1), custom_call_target="tpu_custom_call" | custom-call | tf_op jit(solution)/shard_map/pallas_call | solution.py:494
  3.7 8.7 %all-to-all-start = ((bf16[32,144,128]{2,1,0:T(8,128)(2,1)}), bf16[32,144,128]{2,1,0:T(8,128)(2,1)S(1)}, u32[]{:S(2)}, u32[]{:S(2)}) async-start(bf16[32,144,128]{2,1,0:T(8,128)(2,1)} %get-tuple-element.47), calls=%async_computation | async-start | bytes 2359296 | tf_op jit(solution)/shard_map/all_to_all | solution.py:480
  12.3 3.3 %collective-permute-start = (bf16[80,512]{1,0:T(8,128)(2,1)S(1)}, bf16[80,512]{1,0:T(8,128)(2,1)S(1)}, u32[]{:S(2)}, u32[]{:S(2)}) collective-permute-start(bf16[80,512]{1,0:T(8,128)(2,1)S(1)} %copy-done.6), channel_id=1, source_target_pairs={{0,2},{2,4},{4,6},{6,0},{1,3},{3,5},{5,7},{7,1},{8,10},{10,12},{12... | collective-permute-start | bytes 245768 | tf_op jit(solution)/shard_map/ppermute | solution.py:456
  15.7 4.5 %collective-permute-start.1 = (bf16[80,512]{1,0:T(8,128)(2,1)S(1)}, bf16[80,512]{1,0:T(8,128)(2,1)S(1)}, u32[]{:S(2)}, u32[]{:S(2)}) collective-permute-start(bf16[80,512]{1,0:T(8,128)(2,1)S(1)} %copy-done.6), channel_id=1, source_target_pairs={{0,4},{2,6},{4,0},{6,2},{1,5},{3,7},{5,1},{7,3},{8,12},{10,14},{12... | collective-permute-start | bytes 245768 | tf_op jit(solution)/shard_map/ppermute | solution.py:456
  20.2 2.7 %collective-permute-start.2 = (bf16[80,512]{1,0:T(8,128)(2,1)S(1)}, bf16[80,512]{1,0:T(8,128)(2,1)S(1)}, u32[]{:S(2)}, u32[]{:S(2)}) collective-permute-start(bf16[80,512]{1,0:T(8,128)(2,1)S(1)} %copy-done.6), channel_id=1, source_target_pairs={{0,6},{2,0},{4,2},{6,4},{1,7},{3,1},{5,3},{7,5},{8,14},{10,8},{12,... | collective-permute-start | bytes 245768 | tf_op jit(solution)/shard_map/ppermute | solution.py:456
  22.8 13.9 %collective-permute-done.1.shard2 = bf16[80,512]{1,0:T(8,128)(2,1)S(1)} collective-permute-done((bf16[80,512]{1,0:T(8,128)(2,1)S(1)}, bf16[80,512]{1,0:T(8,128)(2,1)S(1)}, u32[]{:S(2)}, u32[]{:S(2)}) %collective-permute-start.1) | collective-permute-done | bytes 81952 | tf_op jit(solution)/shard_map/ppermute | solution.py:456
  38.1 4.5 %all-to-all-start.1 = ((bf16[16,64,256]{2,1,0:T(8,128)(2,1)}), bf16[16,64,256]{2,1,0:T(8,128)(2,1)S(1)}, u32[]{:S(2)}, u32[]{:S(2)}) async-start(bf16[16,64,256]{2,1,0:T(8,128)(2,1)} %get-tuple-element.50), calls=%async_computation.1 | async-start | bytes 1048576 | tf_op jit(solution)/shard_map/all_to_all | solution.py:480
  45.3 2.1 %collective-permute-start.5 = (bf16[4,80,512]{2,1,0:T(8,128)(2,1)S(1)}, bf16[4,80,512]{2,1,0:T(8,128)(2,1)S(1)}, u32[]{:S(2)}, u32[]{:S(2)}) collective-permute-start(bf16[4,80,512]{2,1,0:T(8,128)(2,1)S(1)} %pad_maximum_fusion.own0), channel_id=1, source_target_pairs={{0,48},{1,193},{16,0},{17,209},{32,16},{33,225},{48,32},{49,241},{... | collective-permute-start | bytes 983048 | tf_op jit(solution)/shard_map/ppermute | solution.py:470
  48.0 1.8 %collective-permute-done.3.own1 = bf16[4,80,512]{2,1,0:T(8,128)(2,1)S(1)} collective-permute-done((bf16[4,80,512]{2,1,0:T(8,128)(2,1)S(1)}, bf16[4,80,512]{2,1,0:T(8,128)(2,1)S(1)}, u32[]{:S(2)}, u32[]{:S(2)}) %collective-permute-start.3) | collective-permute-done | bytes 327712 | tf_op jit(solution)/shard_map/ppermute | solution.py:470
  50.6 2.2 %collective-permute-done.4.own2 = bf16[4,80,512]{2,1,0:T(8,128)(2,1)S(1)} collective-permute-done((bf16[4,80,512]{2,1,0:T(8,128)(2,1)S(1)}, bf16[4,80,512]{2,1,0:T(8,128)(2,1)S(1)}, u32[]{:S(2)}, u32[]{:S(2)}) %collective-permute-start.4) | collective-permute-done | bytes 327712 | tf_op jit(solution)/shard_map/ppermute | solution.py:470
  52.9 2.3 %collective-permute-start.8 = (bf16[4,80,512]{2,1,0:T(8,128)(2,1)S(1)}, bf16[4,80,512]{2,1,0:T(8,128)(2,1)}, u32[]{:S(2)}, u32[]{:S(2)}) collective-permute-start(bf16[4,80,512]{2,1,0:T(8,128)(2,1)S(1)} %collective-permute-done.4.own2), channel_id=1, source_target_pairs={{0,1},{1,0},{2,3},{3,2},{4,5},{5,4},{6,7},{7,6},{8,9},{9,8},{10,11... | collective-permute-start | bytes 983048 | tf_op jit(solution)/shard_map/ppermute | solution.py:460
  60.4 8.2 %shard_map.95 = (bf16[4,2,64,256]{3,2,1,0:T(8,128)(2,1)S(1)}, bf16[4,2,64,256]{3,2,1,0:T(8,128)(2,1)S(1)}, bf16[8,256,512]{2,1,0:T(8,128)(2,1)S(1)}, bf16[512,51...) custom-call(s32[5]{0:T(128)S(1)} %stack.38.place, ...), custom_call_target="tpu_custom_call" | custom-call | flops 10000000000 | bytes 16777216 | tf_op jit(solution)/shard_map/pallas_call | solution.py:399
  68.6 8.7 %shard_map.96 = (bf16[8,2,64,256]{3,2,1,0:T(8,128)(2,1)S(1)}, bf16[16,4,80,128]{3,2,1,0:T(8,128)(2,1)S(1)}, bf16[16,4,80,128]{3,2,1,0:T(8,128)(2,1)}) custom-call(s32[5]{0:T(128)S(1)} %stack.38.place, s32[2,16]{1,0:T(2,128)S(1)} %get-tuple-element.49.meta, bf16[2,512,256]{2,1,0:T(8,128)(2,1)S(1)} %constant_dynamic-slice_fusion.gy_ref, ...), custom_call_target="tpu_custom_call" | custom-call | flops 12000000000 | bytes 16777216 | tf_op jit(solution)/shard_map/pallas_call | solution.py:427
  78.1 6.1 %all-to-all-start.2 = ((bf16[16,64,256]{2,1,0:T(8,128)(2,1)}), bf16[16,64,256]{2,1,0:T(8,128)(2,1)S(1)}, u32[]{:S(2)}, u32[]{:S(2)}) async-start(bf16[16,64,256]{2,1,0:T(8,128)(2,1)} %bitcast.15), calls=%async_computation.2 | async-start | bytes 1048576 | tf_op jit(solution)/shard_map/all_to_all | solution.py:480
  87.4 1.9 %collective-permute-start.14 = (bf16[4,4,80,128]{3,2,1,0:T(8,128)(2,1)S(1)}, bf16[4,4,80,128]{3,2,1,0:T(8,128)(2,1)S(1)}, u32[]{:S(2)}, u32[]{:S(2)}) collective-permute-start(bf16[4,4,80,128]{3,2,1,0:T(8,128)(2,1)S(1)} %get-tuple-element.69), channel_id=1, source_target_pairs={{0,48},{1,193},{16,0},{17,209},{32,16},{33,225},{48,32},{49,241},{... | collective-permute-start | bytes 983048 | tf_op jit(solution)/shard_map/ppermute | solution.py:470
  89.3 3.0 %collective-permute-done.12.came1 = bf16[4,4,80,128]{3,2,1,0:T(8,128)(2,1)S(1)} collective-permute-done((bf16[4,4,80,128]{3,2,1,0:T(8,128)(2,1)S(1)}, bf16[4,4,80,128]{3,2,1,0:T(8,128)(2,1)S(1)}, u32[]{:S(2)}, u32[]{:S(2)}) %collective-permute-start.12) | collective-permute-done | bytes 327712 | tf_op jit(solution)/shard_map/ppermute | solution.py:470
  92.2 2.5 %collective-permute-done.13.came2 = bf16[4,4,80,128]{3,2,1,0:T(8,128)(2,1)S(1)} collective-permute-done((bf16[4,4,80,128]{3,2,1,0:T(8,128)(2,1)S(1)}, bf16[4,4,80,128]{3,2,1,0:T(8,128)(2,1)S(1)}, u32[]{:S(2)}, u32[]{:S(2)}) %collective-permute-start.13) | collective-permute-done | bytes 327712 | tf_op jit(solution)/shard_map/ppermute | solution.py:470
  94.8 3.2 %collective-permute-done.14.came3 = bf16[4,4,80,128]{3,2,1,0:T(8,128)(2,1)S(1)} collective-permute-done((bf16[4,4,80,128]{3,2,1,0:T(8,128)(2,1)S(1)}, bf16[4,4,80,128]{3,2,1,0:T(8,128)(2,1)S(1)}, u32[]{:S(2)}, u32[]{:S(2)}) %collective-permute-start.14) | collective-permute-done | bytes 327712 | tf_op jit(solution)/shard_map/ppermute | solution.py:470
  100.2 2.8 %collective-permute-start.16 = (bf16[4,80,128]{2,1,0:T(8,128)(2,1)S(1)}, bf16[4,80,128]{2,1,0:T(8,128)(2,1)S(1)}, u32[]{:S(2)}, u32[]{:S(2)}) collective-permute-start(bf16[4,80,128]{2,1,0:T(8,128)(2,1)S(1)} %get-tuple-element.72), channel_id=1, source_target_pairs={{0,128},{1,33},{16,144},{17,49},{32,160},{33,1},{48,176},{49,17},{... | collective-permute-start | bytes 245768 | tf_op jit(solution)/shard_map/ppermute | solution.py:470
  104.4 1.9 %collective-permute-done.16.came2 = bf16[4,80,128]{2,1,0:T(8,128)(2,1)S(1)} collective-permute-done((bf16[4,80,128]{2,1,0:T(8,128)(2,1)S(1)}, bf16[4,80,128]{2,1,0:T(8,128)(2,1)S(1)}, u32[]{:S(2)}, u32[]{:S(2)}) %collective-permute-start.16) | collective-permute-done | bytes 81952 | tf_op jit(solution)/shard_map/ppermute | solution.py:470
  108.1 1.7 %shard_map.102 = bf16[32,64,256]{2,1,0:T(8,128)(2,1)} custom-call(s32[2,16]{1,0:T(2,128)S(1)} %get-tuple-element.49.meta, bf16[16,64,256]{2,1,0:T(8,128)(2,1)S(1)} %all-to-all-done.2.rows, bf16[80,128]{1,0:T(8,128)(2,1)S(1)} %get-tuple-element.75.after), custom_call_target="tpu_custom_call" | custom-call | tf_op jit(solution)/shard_map/pallas_call | solution.py:564
  109.7 7.3 %all-to-all-start.3 = ((bf16[32,64,256]{2,1,0:T(8,128)(2,1)}), bf16[32,64,256]{2,1,0:T(8,128)(2,1)S(1)}, u32[]{:S(2)}, u32[]{:S(2)}) async-start(bf16[32,64,256]{2,1,0:T(8,128)(2,1)} %shard_map.102), calls=%async_computation.3 | async-start | bytes 2097152 | tf_op jit(solution)/shard_map/all_to_all | solution.py:480
  117.1 3.0 %collective-permute-start.18 = (bf16[80,128]{1,0:T(8,128)(2,1)S(1)}, bf16[80,128]{1,0:T(8,128)(2,1)S(1)}, u32[]{:S(2)}, u32[]{:S(2)}) collective-permute-start(bf16[80,128]{1,0:T(8,128)(2,1)S(1)} %get-tuple-element.75.after), channel_id=1, source_target_pairs={{0,2},{2,4},{4,6},{6,0},{1,3},{3,5},{5,7},{7,1},{8,10},{10,12},{12... | collective-permute-start | bytes 61448 | tf_op jit(solution)/shard_map/ppermute | solution.py:456
  120.1 3.6 %collective-permute-start.19 = (bf16[80,128]{1,0:T(8,128)(2,1)S(1)}, bf16[80,128]{1,0:T(8,128)(2,1)S(1)}, u32[]{:S(2)}, u32[]{:S(2)}) collective-permute-start(bf16[80,128]{1,0:T(8,128)(2,1)S(1)} %get-tuple-element.76), channel_id=1, source_target_pairs={{0,4},{2,6},{4,0},{6,2},{1,5},{3,7},{5,1},{7,3},{8,12},{10,14},{12... | collective-permute-start | bytes 61448 | tf_op jit(solution)/shard_map/ppermute | solution.py:456
  123.7 3.6 %collective-permute-start.20 = (bf16[80,128]{1,0:T(8,128)(2,1)S(1)}, bf16[80,128]{1,0:T(8,128)(2,1)S(1)}, u32[]{:S(2)}, u32[]{:S(2)}) collective-permute-start(bf16[80,128]{1,0:T(8,128)(2,1)S(1)} %get-tuple-element.77), channel_id=1, source_target_pairs={{0,6},{2,0},{4,2},{6,4},{1,7},{3,1},{5,3},{7,5},{8,14},{10,8},{12,... | collective-permute-start | bytes 61448 | tf_op jit(solution)/shard_map/ppermute | solution.py:456
  127.2 6.4 %collective-permute-done.19.came2 = bf16[80,128]{1,0:T(8,128)(2,1)S(1)} collective-permute-done((bf16[80,128]{1,0:T(8,128)(2,1)S(1)}, bf16[80,128]{1,0:T(8,128)(2,1)S(1)}, u32[]{:S(2)}, u32[]{:S(2)}) %collective-permute-start.19) | collective-permute-done | bytes 20512 | tf_op jit(solution)/shard_map/ppermute | solution.py:456
  134.1 3.4 %collective-permute-done.24.came = bf16[80,128]{1,0:T(8,128)(2,1)S(1)} collective-permute-done((bf16[80,128]{1,0:T(8,128)(2,1)S(1)}, bf16[80,128]{1,0:T(8,128)(2,1)S(1)}, u32[]{:S(2)}, u32[]{:S(2)}) %collective-permute-start.24) | collective-permute-done | bytes 20512 | tf_op jit(solution)/shard_map/ppermute | solution.py:460
  138.3 7.2 %all-to-all-start.4 = ((bf16[16,80,128]{2,1,0:T(8,128)(2,1)}), bf16[16,80,128]{2,1,0:T(8,128)(2,1)S(1)}, u32[]{:S(2)}, u32[]{:S(2)}) async-start(bf16[16,80,128]{2,1,0:T(8,128)(2,1)} %shard_map.104), calls=%async_computation.4 | async-start | bytes 655360 | tf_op jit(solution)/shard_map/all_to_all | solution.py:480
  146.4 1.7 %collective-permute-start.22 = (bf16[2,2,64,256]{3,2,1,0:T(8,128)(2,1)S(1)}, bf16[2,2,64,256]{3,2,1,0:T(8,128)(2,1)S(1)}, u32[]{:S(2)}, u32[]{:S(2)}) collective-permute-start(bf16[2,2,64,256]{3,2,1,0:T(8,128)(2,1)S(1)} %get-tuple-element.81), channel_id=1, source_target_pairs={{0,4},{2,6},{4,0},{6,2},{1,5},{3,7},{5,1},{7,3},{8,12},{10,14},{12... | collective-permute-start | bytes 393224 | tf_op jit(solution)/shard_map/ppermute | solution.py:456
  148.1 2.3 %collective-permute-start.23 = (bf16[2,2,64,256]{3,2,1,0:T(8,128)(2,1)S(1)}, bf16[2,2,64,256]{3,2,1,0:T(8,128)(2,1)S(1)}, u32[]{:S(2)}, u32[]{:S(2)}) collective-permute-start(bf16[2,2,64,256]{3,2,1,0:T(8,128)(2,1)S(1)} %get-tuple-element.82), channel_id=1, source_target_pairs={{0,6},{2,0},{4,2},{6,4},{1,7},{3,1},{5,3},{7,5},{8,14},{10,8},{12,... | collective-permute-start | bytes 393224 | tf_op jit(solution)/shard_map/ppermute | solution.py:456
  154.1 2.6 %collective-permute-done.21.pair1 = bf16[2,2,64,256]{3,2,1,0:T(8,128)(2,1)S(1)} collective-permute-done((bf16[2,2,64,256]{3,2,1,0:T(8,128)(2,1)S(1)}, bf16[2,2,64,256]{3,2,1,0:T(8,128)(2,1)S(1)}, u32[]{:S(2)}, u32[]{:S(2)}) %collective-permute-start.21) | collective-permute-done | bytes 131104 | tf_op jit(solution)/shard_map/ppermute | solution.py:456
  157.1 2.0 %collective-permute-done.23.pair3 = bf16[2,2,64,256]{3,2,1,0:T(8,128)(2,1)S(1)} collective-permute-done((bf16[2,2,64,256]{3,2,1,0:T(8,128)(2,1)S(1)}, bf16[2,2,64,256]{3,2,1,0:T(8,128)(2,1)S(1)}, u32[]{:S(2)}, u32[]{:S(2)}) %collective-permute-start.23) | collective-permute-done | bytes 131104 | tf_op jit(solution)/shard_map/ppermute | solution.py:456
  (59 shorter events, 27.8 us)
Async XLA Ops:
  3.7 33.1 %all-to-all-start = ((bf16[32,144,128]{2,1,0:T(8,128)(2,1)}), bf16[32,144,128]{2,1,0:T(8,128)(2,1)S(1)}, u32[]{:S(2)}, u32[]{:S(2)}) async-start(bf16[32,144,128]{2,1,0:T(8,128)(2,1)} %get-tuple-element.47), calls=%async_computation | async-start | bytes 2359296 | tf_op jit(solution)/shard_map/all_to_all | solution.py:480
  12.3 10.5 %collective-permute-start = (bf16[80,512]{1,0:T(8,128)(2,1)S(1)}, bf16[80,512]{1,0:T(8,128)(2,1)S(1)}, u32[]{:S(2)}, u32[]{:S(2)}) collective-permute-start(bf16[80,512]{1,0:T(8,128)(2,1)S(1)} %copy-done.6), channel_id=1, source_target_pairs={{0,2},{2,4},{4,6},{6,0},{1,3},{3,5},{5,7},{7,1},{8,10},{10,12},{12... | collective-permute-start | bytes 245768 | tf_op jit(solution)/shard_map/ppermute | solution.py:456
  15.7 21.1 %collective-permute-start.1 = (bf16[80,512]{1,0:T(8,128)(2,1)S(1)}, bf16[80,512]{1,0:T(8,128)(2,1)S(1)}, u32[]{:S(2)}, u32[]{:S(2)}) collective-permute-start(bf16[80,512]{1,0:T(8,128)(2,1)S(1)} %copy-done.6), channel_id=1, source_target_pairs={{0,4},{2,6},{4,0},{6,2},{1,5},{3,7},{5,1},{7,3},{8,12},{10,14},{12... | collective-permute-start | bytes 245768 | tf_op jit(solution)/shard_map/ppermute | solution.py:456
  20.2 16.6 %collective-permute-start.2 = (bf16[80,512]{1,0:T(8,128)(2,1)S(1)}, bf16[80,512]{1,0:T(8,128)(2,1)S(1)}, u32[]{:S(2)}, u32[]{:S(2)}) collective-permute-start(bf16[80,512]{1,0:T(8,128)(2,1)S(1)} %copy-done.6), channel_id=1, source_target_pairs={{0,6},{2,0},{4,2},{6,4},{1,7},{3,1},{5,3},{7,5},{8,14},{10,8},{12,... | collective-permute-start | bytes 245768 | tf_op jit(solution)/shard_map/ppermute | solution.py:456
  38.1 21.4 %all-to-all-start.1 = ((bf16[16,64,256]{2,1,0:T(8,128)(2,1)}), bf16[16,64,256]{2,1,0:T(8,128)(2,1)S(1)}, u32[]{:S(2)}, u32[]{:S(2)}) async-start(bf16[16,64,256]{2,1,0:T(8,128)(2,1)} %get-tuple-element.50), calls=%async_computation.1 | async-start | bytes 1048576 | tf_op jit(solution)/shard_map/all_to_all | solution.py:480
  42.6 7.2 %collective-permute-start.3 = (bf16[4,80,512]{2,1,0:T(8,128)(2,1)S(1)}, bf16[4,80,512]{2,1,0:T(8,128)(2,1)S(1)}, u32[]{:S(2)}, u32[]{:S(2)}) collective-permute-start(bf16[4,80,512]{2,1,0:T(8,128)(2,1)S(1)} %pad_maximum_fusion.own0), channel_id=1, source_target_pairs={{0,16},{1,65},{16,32},{17,81},{32,48},{33,97},{48,0},{49,113},{64,... | collective-permute-start | bytes 983048 | tf_op jit(solution)/shard_map/ppermute | solution.py:470
  44.2 8.7 %collective-permute-start.4 = (bf16[4,80,512]{2,1,0:T(8,128)(2,1)S(1)}, bf16[4,80,512]{2,1,0:T(8,128)(2,1)S(1)}, u32[]{:S(2)}, u32[]{:S(2)}) collective-permute-start(bf16[4,80,512]{2,1,0:T(8,128)(2,1)S(1)} %pad_maximum_fusion.own0), channel_id=1, source_target_pairs={{0,32},{1,129},{16,48},{17,145},{32,0},{33,161},{48,16},{49,177},{... | collective-permute-start | bytes 983048 | tf_op jit(solution)/shard_map/ppermute | solution.py:470
  45.3 10.6 %collective-permute-start.5 = (bf16[4,80,512]{2,1,0:T(8,128)(2,1)S(1)}, bf16[4,80,512]{2,1,0:T(8,128)(2,1)S(1)}, u32[]{:S(2)}, u32[]{:S(2)}) collective-permute-start(bf16[4,80,512]{2,1,0:T(8,128)(2,1)S(1)} %pad_maximum_fusion.own0), channel_id=1, source_target_pairs={{0,48},{1,193},{16,0},{17,209},{32,16},{33,225},{48,32},{49,241},{... | collective-permute-start | bytes 983048 | tf_op jit(solution)/shard_map/ppermute | solution.py:470
  47.4 9.7 %collective-permute-start.6 = (bf16[4,80,512]{2,1,0:T(8,128)(2,1)S(1)}, bf16[4,80,512]{2,1,0:T(8,128)(2,1)S(1)}, u32[]{:S(2)}, u32[]{:S(2)}) collective-permute-start(bf16[4,80,512]{2,1,0:T(8,128)(2,1)S(1)} %pad_maximum_fusion.own0), channel_id=1, source_target_pairs={{0,1},{1,0},{2,3},{3,2},{4,5},{5,4},{6,7},{7,6},{8,9},{9,8},{10,11... | collective-permute-start | bytes 983048 | tf_op jit(solution)/shard_map/ppermute | solution.py:460
  49.8 7.3 %collective-permute-start.7 = (bf16[4,80,512]{2,1,0:T(8,128)(2,1)S(1)}, bf16[4,80,512]{2,1,0:T(8,128)(2,1)S(1)}, u32[]{:S(2)}, u32[]{:S(2)}) collective-permute-start(bf16[4,80,512]{2,1,0:T(8,128)(2,1)S(1)} %collective-permute-done.3.own1), channel_id=1, source_target_pairs={{0,1},{1,0},{2,3},{3,2},{4,5},{5,4},{6,7},{7,6},{8,9},{9,8},{10,11... | collective-permute-start | bytes 983048 | tf_op jit(solution)/shard_map/ppermute | solution.py:460
  52.9 5.0 %collective-permute-start.8 = (bf16[4,80,512]{2,1,0:T(8,128)(2,1)S(1)}, bf16[4,80,512]{2,1,0:T(8,128)(2,1)}, u32[]{:S(2)}, u32[]{:S(2)}) collective-permute-start(bf16[4,80,512]{2,1,0:T(8,128)(2,1)S(1)} %collective-permute-done.4.own2), channel_id=1, source_target_pairs={{0,1},{1,0},{2,3},{3,2},{4,5},{5,4},{6,7},{7,6},{8,9},{9,8},{10,11... | collective-permute-start | bytes 983048 | tf_op jit(solution)/shard_map/ppermute | solution.py:460
  55.9 1.9 %collective-permute-start.9 = (bf16[4,80,512]{2,1,0:T(8,128)(2,1)S(1)}, bf16[4,80,512]{2,1,0:T(8,128)(2,1)}, u32[]{:S(2)}, u32[]{:S(2)}) collective-permute-start(bf16[4,80,512]{2,1,0:T(8,128)(2,1)S(1)} %collective-permute-done.5.own3), channel_id=1, source_target_pairs={{0,1},{1,0},{2,3},{3,2},{4,5},{5,4},{6,7},{7,6},{8,9},{9,8},{10,11... | collective-permute-start | bytes 983048 | tf_op jit(solution)/shard_map/ppermute | solution.py:460
  78.1 6.1 %collective-permute-start.11 = (bf16[16,4,80,128]{3,2,1,0:T(8,128)(2,1)}, bf16[16,4,80,128]{3,2,1,0:T(8,128)(2,1)S(1)}, u32[]{:S(2)}, u32[]{:S(2)}) collective-permute-start(bf16[16,4,80,128]{3,2,1,0:T(8,128)(2,1)} %get-tuple-element.65), channel_id=1, source_target_pairs={{0,1},{1,0},{2,3},{3,2},{4,5},{5,4},{6,7},{7,6},{8,9},{9,8},{10,11... | collective-permute-start | bytes 3932168 | tf_op jit(solution)/shard_map/ppermute | solution.py:460
  78.1 30.0 %all-to-all-start.2 = ((bf16[16,64,256]{2,1,0:T(8,128)(2,1)}), bf16[16,64,256]{2,1,0:T(8,128)(2,1)S(1)}, u32[]{:S(2)}, u32[]{:S(2)}) async-start(bf16[16,64,256]{2,1,0:T(8,128)(2,1)} %bitcast.15), calls=%async_computation.2 | async-start | bytes 1048576 | tf_op jit(solution)/shard_map/all_to_all | solution.py:480
  85.1 7.2 %collective-permute-start.12 = (bf16[4,4,80,128]{3,2,1,0:T(8,128)(2,1)S(1)}, bf16[4,4,80,128]{3,2,1,0:T(8,128)(2,1)S(1)}, u32[]{:S(2)}, u32[]{:S(2)}) collective-permute-start(bf16[4,4,80,128]{3,2,1,0:T(8,128)(2,1)S(1)} %get-tuple-element.67), channel_id=1, source_target_pairs={{0,16},{1,65},{16,32},{17,81},{32,48},{33,97},{48,0},{49,113},{64,... | collective-permute-start | bytes 983048 | tf_op jit(solution)/shard_map/ppermute | solution.py:470
  86.1 8.7 %collective-permute-start.13 = (bf16[4,4,80,128]{3,2,1,0:T(8,128)(2,1)S(1)}, bf16[4,4,80,128]{3,2,1,0:T(8,128)(2,1)S(1)}, u32[]{:S(2)}, u32[]{:S(2)}) collective-permute-start(bf16[4,4,80,128]{3,2,1,0:T(8,128)(2,1)S(1)} %get-tuple-element.68), channel_id=1, source_target_pairs={{0,32},{1,129},{16,48},{17,145},{32,0},{33,161},{48,16},{49,177},{... | collective-permute-start | bytes 983048 | tf_op jit(solution)/shard_map/ppermute | solution.py:470
  87.4 10.6 %collective-permute-start.14 = (bf16[4,4,80,128]{3,2,1,0:T(8,128)(2,1)S(1)}, bf16[4,4,80,128]{3,2,1,0:T(8,128)(2,1)S(1)}, u32[]{:S(2)}, u32[]{:S(2)}) collective-permute-start(bf16[4,4,80,128]{3,2,1,0:T(8,128)(2,1)S(1)} %get-tuple-element.69), channel_id=1, source_target_pairs={{0,48},{1,193},{16,0},{17,209},{32,16},{33,225},{48,32},{49,241},{... | collective-permute-start | bytes 983048 | tf_op jit(solution)/shard_map/ppermute | solution.py:470
  98.7 5.7 %collective-permute-start.15 = (bf16[4,80,128]{2,1,0:T(8,128)(2,1)S(1)}, bf16[4,80,128]{2,1,0:T(8,128)(2,1)S(1)}, u32[]{:S(2)}, u32[]{:S(2)}) collective-permute-start(bf16[4,80,128]{2,1,0:T(8,128)(2,1)S(1)} %get-tuple-element.71), channel_id=1, source_target_pairs={{0,64},{1,17},{16,80},{17,33},{32,96},{33,49},{48,112},{49,1},{64,... | collective-permute-start | bytes 245768 | tf_op jit(solution)/shard_map/ppermute | solution.py:470
  100.2 6.0 %collective-permute-start.16 = (bf16[4,80,128]{2,1,0:T(8,128)(2,1)S(1)}, bf16[4,80,128]{2,1,0:T(8,128)(2,1)S(1)}, u32[]{:S(2)}, u32[]{:S(2)}) collective-permute-start(bf16[4,80,128]{2,1,0:T(8,128)(2,1)S(1)} %get-tuple-element.72), channel_id=1, source_target_pairs={{0,128},{1,33},{16,144},{17,49},{32,160},{33,1},{48,176},{49,17},{... | collective-permute-start | bytes 245768 | tf_op jit(solution)/shard_map/ppermute | solution.py:470
  103.0 4.4 %collective-permute-start.17 = (bf16[4,80,128]{2,1,0:T(8,128)(2,1)S(1)}, bf16[4,80,128]{2,1,0:T(8,128)(2,1)S(1)}, u32[]{:S(2)}, u32[]{:S(2)}) collective-permute-start(bf16[4,80,128]{2,1,0:T(8,128)(2,1)S(1)} %get-tuple-element.73), channel_id=1, source_target_pairs={{0,192},{1,49},{16,208},{17,1},{32,224},{33,17},{48,240},{49,33},{... | collective-permute-start | bytes 245768 | tf_op jit(solution)/shard_map/ppermute | solution.py:470
  108.0 8.9 %copy-start.5 = (bf16[4,2,64,256]{3,2,1,0:T(8,128)(2,1)S(1)}, bf16[4,2,64,256]{3,2,1,0:T(8,128)(2,1)}, u32[]{:S(2)}) copy-start(bf16[4,2,64,256]{3,2,1,0:T(8,128)(2,1)} %copy-done.4) | copy-start | bytes 786436
  109.7 27.8 %all-to-all-start.3 = ((bf16[32,64,256]{2,1,0:T(8,128)(2,1)}), bf16[32,64,256]{2,1,0:T(8,128)(2,1)S(1)}, u32[]{:S(2)}, u32[]{:S(2)}) async-start(bf16[32,64,256]{2,1,0:T(8,128)(2,1)} %shard_map.102), calls=%async_computation.3 | async-start | bytes 2097152 | tf_op jit(solution)/shard_map/all_to_all | solution.py:480
  117.0 33.4 %copy-start.1 = (s32[16,2]{0,1:T(2,128)S(1)}, s32[16,2]{0,1:T(2,128)}, u32[]{:S(2)}) copy-start(s32[16,2]{0,1:T(2,128)} %param.9) | copy-start | bytes 388
  117.0 28.5 %collective-permute-start.10 = (bf16[4,2,64,256]{3,2,1,0:T(8,128)(2,1)S(1)}, bf16[4,2,64,256]{3,2,1,0:T(8,128)(2,1)S(1)}, u32[]{:S(2)}, u32[]{:S(2)}) collective-permute-start(bf16[4,2,64,256]{3,2,1,0:T(8,128)(2,1)S(1)} %copy-done.5), channel_id=1, source_target_pairs={{0,1},{1,0},{2,3},{3,2},{4,5},{5,4},{6,7},{7,6},{8,9},{9,8},{10,11... | collective-permute-start | bytes 786440 | tf_op jit(solution)/shard_map/ppermute | solution.py:460
  117.1 10.1 %collective-permute-start.18 = (bf16[80,128]{1,0:T(8,128)(2,1)S(1)}, bf16[80,128]{1,0:T(8,128)(2,1)S(1)}, u32[]{:S(2)}, u32[]{:S(2)}) collective-permute-start(bf16[80,128]{1,0:T(8,128)(2,1)S(1)} %get-tuple-element.75.after), channel_id=1, source_target_pairs={{0,2},{2,4},{4,6},{6,0},{1,3},{3,5},{5,7},{7,1},{8,10},{10,12},{12... | collective-permute-start | bytes 61448 | tf_op jit(solution)/shard_map/ppermute | solution.py:456
  120.1 13.5 %collective-permute-start.19 = (bf16[80,128]{1,0:T(8,128)(2,1)S(1)}, bf16[80,128]{1,0:T(8,128)(2,1)S(1)}, u32[]{:S(2)}, u32[]{:S(2)}) collective-permute-start(bf16[80,128]{1,0:T(8,128)(2,1)S(1)} %get-tuple-element.76), channel_id=1, source_target_pairs={{0,4},{2,6},{4,0},{6,2},{1,5},{3,7},{5,1},{7,3},{8,12},{10,14},{12... | collective-permute-start | bytes 61448 | tf_op jit(solution)/shard_map/ppermute | solution.py:456
  123.7 10.0 %collective-permute-start.20 = (bf16[80,128]{1,0:T(8,128)(2,1)S(1)}, bf16[80,128]{1,0:T(8,128)(2,1)S(1)}, u32[]{:S(2)}, u32[]{:S(2)}) collective-permute-start(bf16[80,128]{1,0:T(8,128)(2,1)S(1)} %get-tuple-element.77), channel_id=1, source_target_pairs={{0,6},{2,0},{4,2},{6,4},{1,7},{3,1},{5,3},{7,5},{8,14},{10,8},{12,... | collective-permute-start | bytes 61448 | tf_op jit(solution)/shard_map/ppermute | solution.py:456
  133.7 3.9 %collective-permute-start.24 = (bf16[80,128]{1,0:T(8,128)(2,1)S(1)}, bf16[80,128]{1,0:T(8,128)(2,1)S(1)}, u32[]{:S(2)}, u32[]{:S(2)}) collective-permute-start(bf16[80,128]{1,0:T(8,128)(2,1)S(1)} %get-tuple-element.78.after), channel_id=1, source_target_pairs={{0,8},{8,0},{1,9},{9,1},{2,10},{10,2},{3,11},{11,3},{4,12},{12,4},... | collective-permute-start | bytes 61448 | tf_op jit(solution)/shard_map/ppermute | solution.py:460
  138.3 14.9 %all-to-all-start.4 = ((bf16[16,80,128]{2,1,0:T(8,128)(2,1)}), bf16[16,80,128]{2,1,0:T(8,128)(2,1)S(1)}, u32[]{:S(2)}, u32[]{:S(2)}) async-start(bf16[16,80,128]{2,1,0:T(8,128)(2,1)} %shard_map.104), calls=%async_computation.4 | async-start | bytes 655360 | tf_op jit(solution)/shard_map/all_to_all | solution.py:480
  145.6 11.1 %collective-permute-start.21 = (bf16[2,2,64,256]{3,2,1,0:T(8,128)(2,1)S(1)}, bf16[2,2,64,256]{3,2,1,0:T(8,128)(2,1)S(1)}, u32[]{:S(2)}, u32[]{:S(2)}) collective-permute-start(bf16[2,2,64,256]{3,2,1,0:T(8,128)(2,1)S(1)} %get-tuple-element.80), channel_id=1, source_target_pairs={{0,2},{2,4},{4,6},{6,0},{1,3},{3,5},{5,7},{7,1},{8,10},{10,12},{12... | collective-permute-start | bytes 393224 | tf_op jit(solution)/shard_map/ppermute | solution.py:456
  146.4 10.7 %collective-permute-start.22 = (bf16[2,2,64,256]{3,2,1,0:T(8,128)(2,1)S(1)}, bf16[2,2,64,256]{3,2,1,0:T(8,128)(2,1)S(1)}, u32[]{:S(2)}, u32[]{:S(2)}) collective-permute-start(bf16[2,2,64,256]{3,2,1,0:T(8,128)(2,1)S(1)} %get-tuple-element.81), channel_id=1, source_target_pairs={{0,4},{2,6},{4,0},{6,2},{1,5},{3,7},{5,1},{7,3},{8,12},{10,14},{12... | collective-permute-start | bytes 393224 | tf_op jit(solution)/shard_map/ppermute | solution.py:456
  148.1 11.0 %collective-permute-start.23 = (bf16[2,2,64,256]{3,2,1,0:T(8,128)(2,1)S(1)}, bf16[2,2,64,256]{3,2,1,0:T(8,128)(2,1)S(1)}, u32[]{:S(2)}, u32[]{:S(2)}) collective-permute-start(bf16[2,2,64,256]{3,2,1,0:T(8,128)(2,1)S(1)} %get-tuple-element.82), channel_id=1, source_target_pairs={{0,6},{2,0},{4,2},{6,4},{1,7},{3,1},{5,3},{7,5},{8,14},{10,8},{12,... | collective-permute-start | bytes 393224 | tf_op jit(solution)/shard_map/ppermute | solution.py:456
  (5 other events, 19.9 us)
